TPU v7x, 32 devices: a whole 2x2x4 slice. The times are simulated.
32 devices in a mesh: dp: 16 (over z, y, core), mp: 2 (over x).
Axes of the slice: x: 2, y: 2, z: 4, core: 2. Of those that a mesh axis runs over, the one named last changes fastest.
Arguments:
- tokens: bfloat16 [23040, 768], P('dp'), may hold values from -6 to 6
- cotangent: bfloat16 [23040, 768], P('dp'), may hold values from -6 to 6
- lengths: int32 [80], P('dp'), may hold values from 72 to 288, as said below
- doc_ids: int32 [80, 8], P('dp'), may hold values from 0 to 127
- doc_rows: bfloat16 [80, 8, 128], P('dp'), may hold values from -6 to 6
- w_qkv: float32 [3, 768, 768], P(None, 'dp', 'mp'), may hold values from -0.21875 to 0.21875
- m_qkv: float32 [3, 768, 768], P(None, 'dp', 'mp'), may hold values from -0.00061035156 to 0.00061035156
- v_qkv: float32 [3, 768, 768], P(None, 'dp', 'mp'), may hold values from 6.958547e-11 to 1.1133675e-09
- w_attn: float32 [768, 768], P('dp', 'mp'), may hold values from -0.875 to 0.875
- m_attn: float32 [768, 768], P('dp', 'mp'), may hold values from -0.00061035156 to 0.00061035156
- v_attn: float32 [768, 768], P('dp', 'mp'), may hold values from 6.958547e-11 to 1.1133675e-09
- w_inner: float32 [768, 3072], P('dp', 'mp'), may hold values from -0.21875 to 0.21875
- m_inner: float32 [768, 3072], P('dp', 'mp'), may hold values from -0.00061035156 to 0.00061035156
- v_inner: float32 [768, 3072], P('dp', 'mp'), may hold values from 6.958547e-11 to 1.1133675e-09
- w_outer: float32 [768, 3072], P('dp', 'mp'), may hold values from -0.109375 to 0.109375
- m_outer: float32 [768, 3072], P('dp', 'mp'), may hold values from -0.00061035156 to 0.00061035156
- v_outer: float32 [768, 3072], P('dp', 'mp'), may hold values from 6.958547e-11 to 1.1133675e-09
- w_proj: float32 [768, 128], P('dp'), may hold values from -0.21875 to 0.21875
- m_proj: float32 [768, 128], P('dp'), may hold values from -3.0517578e-05 to 3.0517578e-05
- v_proj: float32 [768, 128], P('dp'), may hold values from 1.9329297e-13 to 2.8993947e-12
- vectors: float32 [12, 768], P(None, ('dp', 'mp')), may hold values from -1.2 to 2.5, as said below
- m_vectors: float32 [12, 768], P(None, ('dp', 'mp')), may hold values from -0.005859375 to 0.005859375
- v_vectors: float32 [12, 768], P(None, ('dp', 'mp')), may hold values from 6.958547e-09 to 1.1133675e-07
Outputs:
- out_tokens: bfloat16 [23040, 768], P('dp')
- input_grad: float32 [23040, 768], P('dp')
- grad_norm: float32 [], replicated
- qkv_first: float32 [3, 768, 768], P(None, 'dp', 'mp')
- qkv_second: float32 [3, 768, 768], P(None, 'dp', 'mp')
- qkv_new: float32 [3, 768, 768], P(None, 'dp', 'mp')
- attn_first: float32 [768, 768], P('dp', 'mp')
- attn_second: float32 [768, 768], P('dp', 'mp')
- attn_new: float32 [768, 768], P('dp', 'mp')
- inner_first: float32 [768, 3072], P('dp', 'mp')
- inner_second: float32 [768, 3072], P('dp', 'mp')
- inner_new: float32 [768, 3072], P('dp', 'mp')
- outer_first: float32 [768, 3072], P('dp', 'mp')
- outer_second: float32 [768, 3072], P('dp', 'mp')
- outer_new: float32 [768, 3072], P('dp', 'mp')
- proj_first: float32 [768, 128], P('dp')
- proj_second: float32 [768, 128], P('dp')
- proj_new: float32 [768, 128], P('dp')
- vector_first: float32 [12, 768], P(None, ('dp', 'mp'))
- vector_second: float32 [12, 768], P(None, ('dp', 'mp'))
- vector_new: float32 [12, 768], P(None, ('dp', 'mp'))
- table_grad: float32 [128, 128], P('dp')
Inputs may be any that keep to these rules, and one draw needn't show every extreme that they name: `lengths`: real tokens of each sequence; positions past it are padding keys; some sequence has all 288. `vectors`: norm gains positive, other rows of either sign.
All inputs are finite; a program needn't handle non-finite values.
Results may differ from a plain program's by a relative error of at most 0.012.
The roundings to bfloat16 on the way count: a program that leaves them out, or rounds other values in their place, can miss the bound.
Values may be sent and summed in bfloat16 or wider, within the bound.
A program may use at most 192 MiB of HBM per device.

v0:
```python
import jax
import jax.numpy as jnp
from jax import lax
from jax.sharding import PartitionSpec as P

HEAD_DIM = 64
STEP = 10
TAB_DEV = 8


highest_mode = lax.Precision.HIGHEST
retrieval_scale = 0.17677669529663687
ln_epsilon = 1e-12
beta_first = 0.9
beta_second = 0.999
learn_rate = 0.05
vector_rate = 0.5
decay_rate = 0.01
adam_epsilon = 1e-08
clip_norm = 1.0


def layer_norm(values, gain_row, shift_row):
    centre = jnp.mean(values, axis=-1, keepdims=True)
    centred = values - centre
    spread = jnp.mean(centred * centred, axis=-1, keepdims=True)
    return centred * lax.rsqrt(spread + ln_epsilon) * gain_row + shift_row


def gelu_exact(values):
    return jax.nn.gelu(values, approximate=False)


def adamw_update(weight, moment, second, gradient, decay_factor, step_rate):
    moment_new = beta_first * moment + (1.0 - beta_first) * gradient
    second_new = beta_second * second + (1.0 - beta_second) * gradient * gradient
    first_hat = moment_new / (1.0 - beta_first**STEP)
    second_hat = second_new / (1.0 - beta_second**STEP)
    weight_new = weight - step_rate * (
        first_hat / (jnp.sqrt(second_hat) + adam_epsilon) + decay_factor * weight
    )
    return (moment_new, second_new, weight_new)


def squared(values):
    return jnp.sum(values * values)


def local(
    tokens,
    cotangent,
    lengths,
    doc_ids,
    doc_rows,
    w_qkv,
    m_qkv,
    v_qkv,
    w_attn,
    m_attn,
    v_attn,
    w_inner,
    m_inner,
    v_inner,
    w_outer,
    m_outer,
    v_outer,
    w_proj,
    m_proj,
    v_proj,
    vectors,
    m_vectors,
    v_vectors,
):
    mp_rank = lax.axis_index("mp")
    mp_count = lax.axis_size("mp")
    seq_count = lengths.shape[0]
    row_count = tokens.shape[0]
    seq_len = row_count // seq_count
    model_width = tokens.shape[1]
    width_local = w_qkv.shape[2]
    ff_local = w_inner.shape[1]
    heads_local = width_local // HEAD_DIM
    score_scale = HEAD_DIM ** (-0.5)
    full_qkv, full_attn, full_inner, full_outer, full_proj = (
        lax.all_gather(w_qkv.astype(jnp.bfloat16), "dp", axis=1, tiled=True),
        lax.all_gather(w_attn.astype(jnp.bfloat16), "dp", axis=0, tiled=True),
        lax.all_gather(w_inner.astype(jnp.bfloat16), "dp", axis=0, tiled=True),
        lax.all_gather(w_outer.astype(jnp.bfloat16), "dp", axis=0, tiled=True),
        lax.all_gather(w_proj.astype(jnp.bfloat16), "dp", axis=0, tiled=True),
    )
    full_vectors = lax.all_gather(vectors, ("dp", "mp"), axis=1, tiled=True)
    head_start = mp_rank * width_local
    ff_start = mp_rank * ff_local
    ff_rows = full_vectors.shape[0] - 8
    bias_query = lax.dynamic_slice_in_dim(full_vectors[0], head_start, width_local)
    bias_value = lax.dynamic_slice_in_dim(full_vectors[1], head_start, width_local)
    bias_attn = full_vectors[2]
    gain_one = full_vectors[3]
    shift_one = full_vectors[4]
    bias_inner = lax.dynamic_slice_in_dim(
        full_vectors[5 : 5 + ff_rows].reshape(-1), ff_start, ff_local
    )
    bias_outer = full_vectors[5 + ff_rows]
    gain_two = full_vectors[6 + ff_rows]
    shift_two = full_vectors[7 + ff_rows]
    projected = jnp.einsum("td,jde->jte", tokens, full_qkv, preferred_element_type=jnp.float32)
    queries = (projected[0] + bias_query).astype(jnp.bfloat16)
    keys_low = projected[1].astype(jnp.bfloat16)
    values_low = (projected[2] + bias_value).astype(jnp.bfloat16)
    head_shape = (seq_count, seq_len, heads_local, HEAD_DIM)
    query_heads = queries.reshape(head_shape)
    key_heads = keys_low.reshape(head_shape)
    value_heads = values_low.reshape(head_shape)
    positions = jnp.arange(seq_len)
    key_valid = (positions[None, :] < lengths[:, None])[:, None, None, :]

    def attention_scores():
        raw_scores = (
            jnp.einsum(
                "gqhe,gkhe->ghqk", query_heads, key_heads, preferred_element_type=jnp.float32
            )
            * score_scale
        )
        return jnp.where(key_valid, raw_scores, -1000000000.0)

    scores = attention_scores()
    top_score = jnp.max(scores, axis=-1, keepdims=True)
    log_total = top_score + jnp.log(jnp.sum(jnp.exp(scores - top_score), axis=-1, keepdims=True))
    probs_low = jnp.exp(scores - log_total).astype(jnp.bfloat16)
    mixed_out = jnp.einsum(
        "ghqk,gkhe->gqhe", probs_low, value_heads, preferred_element_type=jnp.float32
    )
    mixed_low = mixed_out.reshape(row_count, width_local).astype(jnp.bfloat16)
    attn_part = jnp.einsum("te,de->td", mixed_low, full_attn, preferred_element_type=jnp.float32)
    attn_sum = lax.psum(attn_part, "mp")
    resid_one = tokens.astype(jnp.float32) + attn_sum + bias_attn
    normed, norm_one_back = jax.vjp(layer_norm, resid_one, gain_one, shift_one)
    normed_low = normed.astype(jnp.bfloat16)
    inner_pre = jnp.dot(normed_low, full_inner, preferred_element_type=jnp.float32) + bias_inner
    activated, gelu_back = jax.vjp(gelu_exact, inner_pre)
    active_low = activated.astype(jnp.bfloat16)
    outer_part = jnp.einsum("tf,df->td", active_low, full_outer, preferred_element_type=jnp.float32)
    outer_sum = lax.psum(outer_part, "mp")
    resid_two = normed + outer_sum + bias_outer
    output, norm_two_back = jax.vjp(layer_norm, resid_two, gain_two, shift_two)
    out_tokens = output.astype(jnp.bfloat16)
    cls_low = out_tokens.reshape(seq_count, seq_len, model_width)[:, 0]
    query_proj = jnp.dot(cls_low, full_proj, preferred_element_type=jnp.float32).astype(
        jnp.bfloat16
    )
    query_float = query_proj.astype(jnp.float32)
    rows_float = doc_rows.astype(jnp.float32)
    doc_scores = (
        jnp.einsum("gp,gkp->gk", query_float, rows_float, precision=highest_mode) * retrieval_scale
    )
    soft_weights = jax.nn.softmax(doc_scores, axis=-1)
    target = (jnp.arange(doc_scores.shape[1]) == 0).astype(jnp.float32)
    score_grad = (soft_weights - target[None, :]) * retrieval_scale
    query_grad = jnp.einsum("gk,gkp->gp", score_grad, rows_float, precision=highest_mode).astype(
        jnp.bfloat16
    )
    row_grads = score_grad[:, :, None] * query_float[:, None, :]
    cls_grad = jnp.einsum("gp,dp->gd", query_grad, full_proj, preferred_element_type=jnp.float32)
    proj_grad = jnp.einsum("gd,gp->dp", cls_low, query_grad, preferred_element_type=jnp.float32)
    table_rows = TAB_DEV * lax.axis_size("dp")
    one_hot = (jnp.arange(table_rows)[:, None] == doc_ids.reshape(1, -1)).astype(jnp.float32)
    table_local = jnp.dot(
        one_hot, row_grads.reshape(-1, row_grads.shape[2]), precision=highest_mode
    )
    out_grad = (
        cotangent.astype(jnp.float32)
        .reshape(seq_count, seq_len, model_width)
        .at[:, 0]
        .add(cls_grad)
        .reshape(row_count, model_width)
    )
    resid_two_grad, gain_two_grad, shift_two_grad = norm_two_back(out_grad)
    outer_low = resid_two_grad.astype(jnp.bfloat16)
    active_grad = jnp.dot(outer_low, full_outer, preferred_element_type=jnp.float32)
    outer_wgrad = jnp.einsum("td,tf->df", outer_low, active_low, preferred_element_type=jnp.float32)
    (inner_grad,) = gelu_back(active_grad)
    inner_low = inner_grad.astype(jnp.bfloat16)
    inner_wgrad = jnp.einsum("td,tf->df", normed_low, inner_low, preferred_element_type=jnp.float32)
    normed_part = jnp.einsum("tf,df->td", inner_low, full_inner, preferred_element_type=jnp.float32)
    normed_grad = lax.psum(normed_part, "mp") + resid_two_grad
    resid_one_grad, gain_one_grad, shift_one_grad = norm_one_back(normed_grad)
    attn_low = resid_one_grad.astype(jnp.bfloat16)
    mixed_grad = jnp.dot(attn_low, full_attn, preferred_element_type=jnp.float32).astype(
        jnp.bfloat16
    )
    attn_wgrad = jnp.einsum("td,te->de", attn_low, mixed_low, preferred_element_type=jnp.float32)
    mixed_heads = mixed_grad.reshape(head_shape)
    scores_again = attention_scores()
    probs_again = jnp.exp(scores_again - log_total)
    probs_again_low = probs_again.astype(jnp.bfloat16)
    prob_grad = jnp.einsum(
        "gqhe,gkhe->ghqk", mixed_heads, value_heads, preferred_element_type=jnp.float32
    )
    row_delta = jnp.sum(probs_again * prob_grad, axis=-1, keepdims=True)
    score_low = (probs_again * (prob_grad - row_delta)).astype(jnp.bfloat16)
    query_back = (
        jnp.einsum("ghqk,gkhe->gqhe", score_low, key_heads, preferred_element_type=jnp.float32)
        * score_scale
    )
    key_back = (
        jnp.einsum("ghqk,gqhe->gkhe", score_low, query_heads, preferred_element_type=jnp.float32)
        * score_scale
    )
    value_back = jnp.einsum(
        "ghqk,gqhe->gkhe", probs_again_low, mixed_heads, preferred_element_type=jnp.float32
    )
    stacked = jnp.stack(
        [
            query_back.reshape(row_count, width_local),
            key_back.reshape(row_count, width_local),
            value_back.reshape(row_count, width_local),
        ]
    ).astype(jnp.bfloat16)
    qkv_wgrad = jnp.einsum("td,jte->jde", tokens, stacked, preferred_element_type=jnp.float32)
    input_part = jnp.einsum("jte,jde->td", stacked, full_qkv, preferred_element_type=jnp.float32)
    input_grad = lax.psum(input_part, "mp") + resid_one_grad
    bias_query_grad = jnp.sum(stacked[0].astype(jnp.float32), axis=0)
    bias_value_grad = jnp.sum(stacked[2].astype(jnp.float32), axis=0)
    bias_inner_grad = jnp.sum(inner_low.astype(jnp.float32), axis=0)
    head_rows = lax.dynamic_update_slice(
        jnp.zeros((2, model_width), jnp.float32),
        jnp.stack([bias_query_grad, bias_value_grad]),
        (0, head_start),
    )
    ff_flat = lax.dynamic_update_slice(
        jnp.zeros((ff_rows * model_width,), jnp.float32), bias_inner_grad, (ff_start,)
    )
    share_factor = 1.0 / mp_count
    shared_one = share_factor * jnp.stack(
        [jnp.sum(resid_one_grad, axis=0), gain_one_grad, shift_one_grad]
    )
    shared_two = share_factor * jnp.stack(
        [jnp.sum(resid_two_grad, axis=0), gain_two_grad, shift_two_grad]
    )
    vector_local = jnp.concatenate(
        [head_rows, shared_one, ff_flat.reshape(ff_rows, model_width), shared_two], axis=0
    )
    vector_grad = lax.psum_scatter(vector_local, ("dp", "mp"), scatter_dimension=1, tiled=True)
    qkv_reduced, attn_reduced, inner_reduced, outer_reduced, proj_reduced, table_grad = (
        lax.psum_scatter(qkv_wgrad, "dp", scatter_dimension=1, tiled=True),
        lax.psum_scatter(attn_wgrad, "dp", scatter_dimension=0, tiled=True),
        lax.psum_scatter(inner_wgrad, "dp", scatter_dimension=0, tiled=True),
        lax.psum_scatter(outer_wgrad, "dp", scatter_dimension=0, tiled=True),
        lax.psum_scatter(proj_grad, "dp", scatter_dimension=0, tiled=True),
        lax.psum_scatter(table_local, "dp", scatter_dimension=0, tiled=True),
    )
    local_squares = (
        squared(qkv_reduced)
        + squared(attn_reduced)
        + squared(inner_reduced)
        + squared(outer_reduced)
        + share_factor * squared(proj_reduced)
        + squared(vector_grad)
    )
    total_squares = lax.psum(local_squares, ("dp", "mp"))
    grad_norm = jnp.sqrt(total_squares)
    clip_factor = clip_norm / jnp.maximum(grad_norm, clip_norm)
    qkv_first, qkv_second, qkv_new = adamw_update(
        w_qkv, m_qkv, v_qkv, qkv_reduced * clip_factor, decay_rate, learn_rate
    )
    attn_first, attn_second, attn_new = adamw_update(
        w_attn, m_attn, v_attn, attn_reduced * clip_factor, decay_rate, learn_rate
    )
    inner_first, inner_second, inner_new = adamw_update(
        w_inner, m_inner, v_inner, inner_reduced * clip_factor, decay_rate, learn_rate
    )
    outer_first, outer_second, outer_new = adamw_update(
        w_outer, m_outer, v_outer, outer_reduced * clip_factor, decay_rate, learn_rate
    )
    proj_first, proj_second, proj_new = adamw_update(
        w_proj, m_proj, v_proj, proj_reduced * clip_factor, decay_rate, learn_rate
    )
    vector_first, vector_second, vector_new = adamw_update(
        vectors, m_vectors, v_vectors, vector_grad * clip_factor, 0.0, vector_rate
    )
    return (
        out_tokens,
        input_grad,
        grad_norm,
        qkv_first,
        qkv_second,
        qkv_new,
        attn_first,
        attn_second,
        attn_new,
        inner_first,
        inner_second,
        inner_new,
        outer_first,
        outer_second,
        outer_new,
        proj_first,
        proj_second,
        proj_new,
        vector_first,
        vector_second,
        vector_new,
        table_grad,
    )


def solution(mesh):
    placed = (
        P("dp", None),
        P("dp", None),
        P("dp"),
        P("dp", None),
        P("dp", None, None),
        P(None, "dp", "mp"),
        P(None, "dp", "mp"),
        P(None, "dp", "mp"),
        P("dp", "mp"),
        P("dp", "mp"),
        P("dp", "mp"),
        P("dp", "mp"),
        P("dp", "mp"),
        P("dp", "mp"),
        P("dp", "mp"),
        P("dp", "mp"),
        P("dp", "mp"),
        P("dp", None),
        P("dp", None),
        P("dp", None),
        P(None, ("dp", "mp")),
        P(None, ("dp", "mp")),
        P(None, ("dp", "mp")),
    )
    return jax.shard_map(
        local,
        mesh=mesh,
        in_specs=placed,
        out_specs=(
            P("dp", None),
            P("dp", None),
            P(),
            P(None, "dp", "mp"),
            P(None, "dp", "mp"),
            P(None, "dp", "mp"),
            P("dp", "mp"),
            P("dp", "mp"),
            P("dp", "mp"),
            P("dp", "mp"),
            P("dp", "mp"),
            P("dp", "mp"),
            P("dp", "mp"),
            P("dp", "mp"),
            P("dp", "mp"),
            P("dp", None),
            P("dp", None),
            P("dp", None),
            P(None, ("dp", "mp")),
            P(None, ("dp", "mp")),
            P(None, ("dp", "mp")),
            P("dp", None),
        ),
        check_vma=False,
    )
```

profile of v0, /device:TPU:0, one launch (start us, length us, event | category | flops | bytes accessed | tf_op | source)
XLA Modules:
  0.0 1251.1 jit_solution(5162571242239020056)
XLA Ops:
  9.8 71.7 %all-gather = f32[32,24,12]{1,2,0:T(8,128)S(1)} all-gather(f32[1,24,12]{1,2,0:T(8,128)} %bitcast.117), channel_id=1, replica_groups=mesh['dp'=16,'mp'=2] {'dp','mp'}, dimensions={0}, use_global_device_ids=true | all-gather | bytes 38016 | tf_op jit(solution)/shard_map/all_gather | solution.py:91
  83.3 20.4 %all_gather.20 = bf16[768,384]{1,0:T(8,128)(2,1)} all-gather(bf16[48,384]{1,0:T(8,128)(2,1)S(1)} %convert_element_type.108), channel_id=1, replica_groups=mesh['dp'=16,'mp'=2] {'dp'}, dimensions={0}, use_global_device_ids=true | all-gather | bytes 626688 | tf_op jit(solution)/shard_map/all_gather | solution.py:86
  103.7 5.2 convolution_bitcast_fusion
  115.9 4.2 copy.137
  120.1 5.4 squeeze.7
  125.5 3.0 copy.132
  128.5 4.8 squeeze.6
  133.3 3.0 add_convert_fusion.1
  136.3 3.3 fusion
  139.6 3.8 exponential_reduce_fusion
  144.4 3.4 fusion.16
  150.3 4.9 fusion.75
  158.8 107.1 %all-reduce.10.cloned.1.call-done = f32[1440,768]{1,0:T(8,128)} async-done(((f32[1440,768]{1,0:T(8,128)}), f32[1440,768]{1,0:T(8,128)}) %all-reduce.10.cloned.1.call-update) | async-done | bytes 4423696 | tf_op jit(solution)/shard_map/psum | solution.py:135
  265.9 3.0 fusion.72
  271.7 39.4 %all-gather.7.cloned.1.call-done = bf16[768,1536]{1,0:T(8,128)(2,1)} async-done(((bf16[48,1536]{1,0:T(8,128)(2,1)}), bf16[768,1536]{1,0:T(8,128)(2,1)}) %all-gather.7.cloned.1.call-update) | async-done | bytes 2359312 | tf_op jit(solution)/shard_map/all_gather | solution.py:87
  311.0 26.6 %multiply_convert_fusion.1 = (bf16[1440,1536]{1,0:T(8,128)(2,1)}, f32[1440,1536]{1,0:T(8,128)}, f32[1440,1536]{1,0:T(8,128)}) fusion(f32[1536]{0:T(1024)S(1)} %dynamic_slice.11, bf16[768,1536]{1,0:T(8,128)(2,1)} %all-gather.7.cloned.1.call-done, f32[1440,768]{1,0:T(8,128)} %copy-done.3, f32[768]{0:T(1024)S(1)} %copy-done.60, ...), kind=kOutput, calls=%fused_computation.11 | convolution fusion | flops 3548897280 | bytes 28925184 | tf_op jit(solution)/shard_map/dot_general | solution.py:139
  337.6 17.1 %all-gather.9.cloned.1.call-done = bf16[768,1536]{1,0:T(8,128)(2,1)} async-done(((bf16[48,1536]{1,0:T(8,128)(2,1)}), bf16[768,1536]{1,0:T(8,128)(2,1)}) %all-gather.9.cloned.1.call-update) | async-done | bytes 2359312 | tf_op jit(solution)/shard_map/all_gather | solution.py:88
  354.8 8.7 fusion.76
  367.6 19.7 %all_gather.23 = bf16[768,128]{1,0:T(8,128)(2,1)S(1)} all-gather(bf16[48,128]{1,0:T(8,128)(2,1)S(1)} %convert_element_type.114), channel_id=1, replica_groups=mesh['dp'=16,'mp'=2] {'dp'}, dimensions={0}, use_global_device_ids=true | all-gather | bytes 208896 | tf_op jit(solution)/shard_map/all_gather | solution.py:89
  387.3 87.9 %all-reduce.12.cloned.1.call-done = f32[1440,768]{1,0:T(8,128)} async-done(((f32[1440,768]{1,0:T(8,128)}), f32[1440,768]{1,0:T(8,128)}) %all-reduce.12.cloned.1.call-update) | async-done | bytes 4423696 | tf_op jit(solution)/shard_map/psum | solution.py:143
  475.2 4.8 fusion.70
  495.0 12.4 convert_reduce_fusion
  509.5 5.2 fusion.77
  517.6 110.1 %all-reduce.14.cloned.1.call-done = f32[1440,768]{1,0:T(8,128)} async-done(((f32[1440,768]{1,0:T(8,128)}), f32[1440,768]{1,0:T(8,128)}) %all-reduce.14.cloned.1.call-update) | async-done | bytes 4423696 | tf_op jit(solution)/shard_map/psum | solution.py:185
  627.7 7.3 multiply_reduce_fusion.1
  635.1 3.9 fusion.68
  643.4 3.3 reshape.262
  646.7 3.2 copy.145
  649.9 15.6 %multiply_reduce_fusion = (f32[5,6,288]{2,1,0:T(8,128)S(1)}, f32[5,6,288,288]{2,3,1,0:T(8,128)}) fusion(f32[5,6,288,288]{2,3,1,0:T(8,128)} %copy-done.2, f32[5,6,288]{2,1,0:T(8,128)S(1)} %copy-done.35, pred[5,288]{1,0:T(8,128)(4,1)S(1)} %copy-done.47, bf16[5,288,6,64]{1,3,2,0:T(8,128)(2,1)} %copy.145, bf16[5,288,6,64]{1,0,3,2:T(8,128)(2,1)} %copy-done.18), kind=kOutput, calls=%fused_computation.1 | convolution fusion | flops 330937920 | bytes 22188960 | tf_op jit(solution)/shard_map/gqhe,gkhe->ghqk/dot_general | solution.py:196
  668.4 13.8 %multiply_convert_fusion = bf16[5,6,288,288]{2,3,1,0:T(8,128)(2,1)} fusion(f32[5,6,288,288]{2,3,1,0:T(8,128)} %get-tuple-element.155, f32[5,6,288,288]{2,3,1,0:T(8,128)} %copy-done.2, f32[5,6,288]{2,1,0:T(8,128)S(1)} %get-tuple-element.154, f32[5,6,288]{2,1,0:T(8,128)S(1)} %copy-done.35, pred[5,288]{1,0:T(8,128)(4,1)S(1)} %copy-done.47), kind=kLoop, calls=%fused_computation | loop fusion | flops 14929920 | bytes 24953760 | tf_op jit(solution)/shard_map/convert_element_type | solution.py:200
  682.2 8.0 fusion.17
  692.7 3.3 stack_reshape.14
  697.4 4.5 fusion.18
  704.3 3.3 stack_reshape.12
  709.1 6.4 fusion.19
  715.5 4.1 copy.169
  722.5 5.7 fusion.13
  728.2 4.0 copy.159
  732.9 10.1 fusion.59
  743.1 9.7 fusion.56
  754.8 6.4 convolution_bitcast_fusion.1
  772.1 98.2 %all-reduce.18.cloned.1.call-done = (f32[3,768,384]{2,0,1:T(4,128)}, f32[128,128]{1,0:T(8,128)}) async-done(((f32[3,768,384]{2,0,1:T(4,128)}, f32[128,128]{1,0:T(8,128)}), (f32[3,768,384]{2,0,1:T(4,128)}, f32[128,128]{1,0:T(8,128)})) %all-reduce.18.cloned.1.call-update) | async-done | bytes 3604496
  873.4 76.2 %reduce-scatter.8.cloned.1.call-done = f32[48,1536]{1,0:T(8,128)} async-done(((f32[768,1536]{1,0:T(8,128)}), f32[48,1536]{1,0:T(8,128)}) %reduce-scatter.8.cloned.1.call-update) | async-done | bytes 294928 | tf_op jit(solution)/shard_map/reduce_scatter | solution.py:247
  951.8 76.7 %reduce-scatter.10.cloned.1.call-done = f32[48,1536]{1,0:T(8,128)} async-done(((f32[768,1536]{1,0:T(8,128)}), f32[48,1536]{1,0:T(8,128)}) %reduce-scatter.10.cloned.1.call-update) | async-done | bytes 294928 | tf_op jit(solution)/shard_map/reduce_scatter | solution.py:248
  1031.0 112.4 %all-reduce.16.cloned.1.call-done = f32[1440,768]{1,0:T(8,128)} async-done(((f32[1440,768]{1,0:T(8,128)}), f32[1440,768]{1,0:T(8,128)}) %all-reduce.16.cloned.1.call-update) | async-done | bytes 4423696 | tf_op jit(solution)/shard_map/psum | solution.py:221
  1143.4 6.3 add_reduce_fusion
  1149.8 40.2 %all-reduce.1 = f32[12,768]{1,0:T(8,128)} all-reduce(f32[12,768]{1,0:T(8,128)S(1)} %pad_maximum_fusion.3), channel_id=7, replica_groups=mesh['dp'=16,'mp'=2] {'dp','mp'}, use_global_device_ids=true, to_apply=%region_36.37.clone | all-reduce | flops 9216 | bytes 73728
  1193.3 41.0 %psum.39 = f32[]{:T(128)} all-reduce(f32[]{:T(128)S(6)} %add.283), channel_id=1, replica_groups=mesh['dp'=16,'mp'=2] {'dp','mp'}, use_global_device_ids=true, to_apply=%region_38.39 | all-reduce | flops 1 | bytes 8 | tf_op jit(solution)/shard_map/psum | solution.py:260
  (287 shorter events, 89.7 us)
Async XLA Ops:
  7.2 475.0 %copy-start = (bf16[5,8,128]{2,1,0:T(8,128)(2,1)S(1)}, bf16[5,8,128]{2,1,0:T(8,128)(2,1)}, u32[]{:S(2)}) copy-start(bf16[5,8,128]{2,1,0:T(8,128)(2,1)} %param.29) | copy-start | bytes 30724
  7.2 96.5 %all-gather.5.cloned.1.call-start = ((), (), s32[]{:S(2)}) async-start(), calls=%async_computation.4 | async-start | bytes 1880064 | tf_op jit(solution)/shard_map/all_gather | solution.py:85
  8.9 257.0 %all-reduce.10.cloned.1.call-start = ((), (), s32[]{:S(2)}) async-start(), calls=%async_computation.5 | async-start | bytes 8847360 | tf_op jit(solution)/shard_map/psum | solution.py:135
  81.8 27.2 %copy-start.48 = (f32[768,12]{0,1:T(8,128)}, f32[768,12]{0,1:T(8,128)S(1)}, u32[]{:S(2)}) copy-start(f32[768,12]{0,1:T(8,128)S(1)} %reshape.249) | copy-start | bytes 110596
  83.3 60.7 %copy-start.46 = (pred[5,288]{1,0:T(8,128)(4,1)}, pred[5,288]{1,0:T(8,128)(4,1)S(1)}, u32[]{:S(2)}) copy-start(pred[5,288]{1,0:T(8,128)(4,1)S(1)} %iota_compare_fusion.2) | copy-start | bytes 4324
  120.1 16.2 %copy-start.7 = (bf16[5,288,6,64]{1,3,2,0:T(8,128)(2,1)}, bf16[5,288,6,64]{1,3,2,0:T(8,128)(2,1)S(1)}, u32[]{:S(2)}) copy-start(bf16[5,288,6,64]{1,3,2,0:T(8,128)(2,1)S(1)} %copy.137) | copy-start | bytes 3317764
  133.3 10.2 slice-start.2
  155.3 110.7 %copy-start.23 = (bf16[1440,768]{1,0:T(8,128)(2,1)S(1)}, bf16[1440,768]{1,0:T(8,128)(2,1)}, u32[]{:S(2)}) copy-start(bf16[1440,768]{1,0:T(8,128)(2,1)} %param.25) | copy-start | bytes 6635524
  155.3 110.7 %copy-start.64 = (f32[768]{0:T(1024)S(1)}, f32[768]{0:T(1024)}, u32[]{:S(2)}) copy-start(f32[768]{0:T(1024)} %get-tuple-element.110) | copy-start | bytes 9220
  155.3 155.7 %all-gather.7.cloned.1.call-start = ((), (), s32[]{:S(2)}) async-start(), calls=%async_computation.6 | async-start | bytes 2506752 | tf_op jit(solution)/shard_map/all_gather | solution.py:87
  157.1 197.7 %all-gather.9.cloned.1.call-start = ((), (), s32[]{:S(2)}) async-start(), calls=%async_computation.7 | async-start | bytes 2506752 | tf_op jit(solution)/shard_map/all_gather | solution.py:88
  157.8 317.4 %all-reduce.12.cloned.1.call-start = ((), (), s32[]{:S(2)}) async-start(), calls=%async_computation.8 | async-start | bytes 8847360 | tf_op jit(solution)/shard_map/psum | solution.py:143
  268.9 42.1 %copy-start.60 = (f32[768]{0:T(1024)S(1)}, f32[768]{0:T(1024)}, u32[]{:S(2)}) copy-start(f32[768]{0:T(1024)} %get-tuple-element.108) | copy-start | bytes 9220
  268.9 366.1 %copy-start.44 = (f32[1440]{0:T(1024)}, f32[1440]{0:T(1024)S(1)}, u32[]{:S(2)}) copy-start(f32[1440]{0:T(1024)S(1)} %broadcast_multiply_fusion.1) | copy-start | bytes 17284
  271.6 363.4 %copy-start.49 = (f32[1440]{0:T(1024)}, f32[1440]{0:T(1024)S(1)}, u32[]{:S(2)}) copy-start(f32[1440]{0:T(1024)S(1)} %fusion.40) | copy-start | bytes 17284
  363.5 111.7 %copy-start.63 = (f32[768]{0:T(1024)S(1)}, f32[768]{0:T(1024)}, u32[]{:S(2)}) copy-start(f32[768]{0:T(1024)} %get-tuple-element.107) | copy-start | bytes 9220
  363.5 264.2 %all-reduce.14.cloned.1.call-start = ((), (), s32[]{:S(2)}) async-start(), calls=%async_computation.9 | async-start | bytes 8847360 | tf_op jit(solution)/shard_map/psum | solution.py:185
  495.0 12.5 copy-start.6
  495.0 14.5 %copy-start.71 = (bf16[768,1536]{1,0:T(8,128)(2,1)S(1)}, bf16[768,1536]{1,0:T(8,128)(2,1)}, u32[]{:S(2)}) copy-start(bf16[768,1536]{1,0:T(8,128)(2,1)} %all-gather.7.cloned.1.call-done) | copy-start | bytes 7077892
  514.7 252.7 %reduce-scatter.12.cloned.1.call-start = ((), (), s32[]{:S(2)}) async-start(), calls=%async_computation.14 | async-start | bytes 417792 | tf_op jit(solution)/shard_map/reduce_scatter | solution.py:249
  516.7 253.9 %reduce-scatter.6.cloned.1.call-start = ((), (), s32[]{:S(2)}) async-start(), calls=%async_computation.11 | async-start | bytes 1253376 | tf_op jit(solution)/shard_map/reduce_scatter | solution.py:246
  639.0 26.5 %copy-start.56 = (f32[1440]{0:T(1024)}, f32[1440]{0:T(1024)S(1)}, u32[]{:S(2)}) copy-start(f32[1440]{0:T(1024)S(1)} %negate_multiply_fusion.1) | copy-start | bytes 17284
  646.7 18.8 %slice-start.4 = ((s8[4423680]{0:T(1024)(128)(4,1)}), s8[229376]{0:T(1024)(128)(4,1)S(1)}, s32[]{:S(2)}) async-start(s8[4423680]{0:T(1024)(128)(4,1)} %bitcast.110), calls=%async_computation.20 | async-start | bytes 458752
  649.9 15.6 %slice-start.5 = ((s8[4423680]{0:T(1024)(128)(4,1)}), s8[4194304]{0:T(1024)(128)(4,1)S(1)}, s32[]{:S(2)}) async-start(s8[4423680]{0:T(1024)(128)(4,1)} %bitcast.110), calls=%async_computation.21 | async-start | bytes 8388608
  649.9 15.6 %copy-start.17 = (bf16[1440,384]{0,1:T(8,128)(2,1)S(1)}, bf16[1440,384]{0,1:T(8,128)(2,1)}, u32[]{:S(2)}) copy-start(bf16[1440,384]{0,1:T(8,128)(2,1)} %copy-done.16) | copy-start | bytes 3317764
  668.4 202.0 %all-reduce.18.cloned.1.call-start = ((), (), s32[]{:S(2)}) async-start(), calls=%async_computation.15 | async-start | bytes 9568256
  668.4 13.8 %copy-start.19 = (bf16[5,288,6,64]{1,3,2,0:T(8,128)(2,1)S(1)}, bf16[5,288,6,64]{1,3,2,0:T(8,128)(2,1)}, u32[]{:S(2)}) copy-start(bf16[5,288,6,64]{1,3,2,0:T(8,128)(2,1)} %copy.145) | copy-start | bytes 3317764
  732.3 217.3 %reduce-scatter.8.cloned.1.call-start = ((), (), s32[]{:S(2)}) async-start(), calls=%async_computation.12 | async-start | bytes 5013504 | tf_op jit(solution)/shard_map/reduce_scatter | solution.py:247
  743.1 285.4 %reduce-scatter.10.cloned.1.call-start = ((), (), s32[]{:S(2)}) async-start(), calls=%async_computation.13 | async-start | bytes 5013504 | tf_op jit(solution)/shard_map/reduce_scatter | solution.py:248
  752.9 390.5 %all-reduce.16.cloned.1.call-start = ((), (), s32[]{:S(2)}) async-start(), calls=%async_computation.10 | async-start | bytes 8847360 | tf_op jit(solution)/shard_map/psum | solution.py:221
  761.2 8.5 copy-start.15
  761.3 382.1 %copy-start.57 = (f32[1440]{0:T(1024)S(1)}, f32[1440]{0:T(1024)}, u32[]{:S(2)}) copy-start(f32[1440]{0:T(1024)} %copy-done.56) | copy-start | bytes 17284
  770.0 260.9 %copy-start.58 = (f32[2,768]{1,0:T(2,128)}, f32[2,768]{1,0:T(2,128)S(1)}, u32[]{:S(2)}) copy-start(f32[2,768]{1,0:T(2,128)S(1)} %maximum_dynamic-update-slice_fusion) | copy-start | bytes 18436
  1030.8 205.6 %copy-start.33 = (f32[3,48,384]{2,1,0:T(8,128)S(1)}, f32[3,48,384]{2,1,0:T(8,128)}, u32[]{:S(2)}) copy-start(f32[3,48,384]{2,1,0:T(8,128)} %param.30) | copy-start | bytes 663556
  1030.9 205.6 %copy-start.42 = (f32[3,48,384]{2,1,0:T(8,128)S(1)}, f32[3,48,384]{2,1,0:T(8,128)}, u32[]{:S(2)}) copy-start(f32[3,48,384]{2,1,0:T(8,128)} %param.32) | copy-start | bytes 663556
  1030.9 205.6 %copy-start.43 = (f32[3,48,384]{2,1,0:T(8,128)S(1)}, f32[3,48,384]{2,1,0:T(8,128)}, u32[]{:S(2)}) copy-start(f32[3,48,384]{2,1,0:T(8,128)} %param.31) | copy-start | bytes 663556
  1030.9 206.5 %copy-start.52 = (f32[48,128]{1,0:T(8,128)S(1)}, f32[48,128]{1,0:T(8,128)}, u32[]{:S(2)}) copy-start(f32[48,128]{1,0:T(8,128)} %param.42) | copy-start | bytes 73732
  1030.9 207.9 %copy-start.40 = (f32[48,384]{1,0:T(8,128)S(1)}, f32[48,384]{1,0:T(8,128)}, u32[]{:S(2)}) copy-start(f32[48,384]{1,0:T(8,128)} %param.33) | copy-start | bytes 221188
  1030.9 207.9 %copy-start.41 = (f32[48,384]{1,0:T(8,128)S(1)}, f32[48,384]{1,0:T(8,128)}, u32[]{:S(2)}) copy-start(f32[48,384]{1,0:T(8,128)} %reduce-scatter.6.cloned.1.call-done) | copy-start | bytes 221188
  1030.9 209.6 %copy-start.25 = (f32[48,1536]{1,0:T(8,128)S(1)}, f32[48,1536]{1,0:T(8,128)}, u32[]{:S(2)}) copy-start(f32[48,1536]{1,0:T(8,128)} %param.36) | copy-start | bytes 884740
  1030.9 209.6 %copy-start.28 = (f32[48,1536]{1,0:T(8,128)S(1)}, f32[48,1536]{1,0:T(8,128)}, u32[]{:S(2)}) copy-start(f32[48,1536]{1,0:T(8,128)} %reduce-scatter.8.cloned.1.call-done) | copy-start | bytes 884740
  1030.9 209.5 %copy-start.36 = (f32[48,1536]{1,0:T(8,128)S(1)}, f32[48,1536]{1,0:T(8,128)}, u32[]{:S(2)}) copy-start(f32[48,1536]{1,0:T(8,128)} %param.38) | copy-start | bytes 884740
  1030.9 209.5 %copy-start.37 = (f32[48,1536]{1,0:T(8,128)S(1)}, f32[48,1536]{1,0:T(8,128)}, u32[]{:S(2)}) copy-start(f32[48,1536]{1,0:T(8,128)} %param.37) | copy-start | bytes 884740
  1143.4 99.3 %copy-start.1 = (bf16[5,8,128]{2,1,0:T(8,128)(2,1)S(1)}, bf16[5,8,128]{2,1,0:T(8,128)(2,1)}, u32[]{:S(2)}) copy-start(bf16[5,8,128]{2,1,0:T(8,128)(2,1)} %param.29) | copy-start | bytes 30724
  1149.7 91.9 %copy-start.27 = (f32[48,1536]{1,0:T(8,128)S(1)}, f32[48,1536]{1,0:T(8,128)}, u32[]{:S(2)}) copy-start(f32[48,1536]{1,0:T(8,128)} %param.39) | copy-start | bytes 884740
  1149.7 91.9 %copy-start.29 = (f32[48,1536]{1,0:T(8,128)S(1)}, f32[48,1536]{1,0:T(8,128)}, u32[]{:S(2)}) copy-start(f32[48,1536]{1,0:T(8,128)} %reduce-scatter.10.cloned.1.call-done) | copy-start | bytes 884740
  1149.7 91.9 %copy-start.38 = (f32[48,1536]{1,0:T(8,128)S(1)}, f32[48,1536]{1,0:T(8,128)}, u32[]{:S(2)}) copy-start(f32[48,1536]{1,0:T(8,128)} %param.41) | copy-start | bytes 884740
  1149.7 91.9 %copy-start.39 = (f32[48,1536]{1,0:T(8,128)S(1)}, f32[48,1536]{1,0:T(8,128)}, u32[]{:S(2)}) copy-start(f32[48,1536]{1,0:T(8,128)} %param.40) | copy-start | bytes 884740
  (45 other events, 169.2 us)
Sparse Core Ops, SparseCore 0:
  10.9 43.3 all-gather.4
  155.4 110.4 all-reduce.9
  268.8 42.2 all-gather.6
  313.7 40.9 all-gather.8
  363.6 111.5 all-reduce.11
  514.8 112.8 all-reduce.13
  631.2 55.5 reduce-scatter.11
  690.8 57.1 reduce-scatter.5
  752.9 117.4 all-reduce.17
  874.0 75.4 reduce-scatter.7
  953.9 74.5 reduce-scatter.9
  1031.4 111.8 all-reduce.15
where the time goes:
time: 1260 us; the launch traced here: 1250 us
  waiting for transfers between devices  725 us (58%)
  blocking collectives  193 us (15%)
  matrix products  144 us (11%)
  other arithmetic  84.4 us (7%)
  local copies, waits for them, and re-layouts  81.4 us (6%)
  between operations  22.8 us (2%)
    psum x1, waiting for transfers between devices, local(): input_grad = lax.psum(input_part, 'mp') + resid_one_grad  112 us
    psum x1, waiting for transfers between devices, local(): normed_grad = lax.psum(normed_part, 'mp') + resid_two_grad  110 us
    psum x1, waiting for transfers between devices, local(): attn_sum = lax.psum(attn_part, 'mp')  107 us
    unnamed x13, waiting for transfers between devices  98.4 us
    psum x1, waiting for transfers between devices, local(): outer_sum = lax.psum(outer_part, 'mp')  87.9 us
    reduce_scatter x1, waiting for transfers between devices, local(): lax.psum_scatter(outer_wgrad, 'dp', scatter_dimension=0, tiled=True)  76.7 us
    reduce_scatter x1, waiting for transfers between devices, local(): lax.psum_scatter(inner_wgrad, 'dp', scatter_dimension=0, tiled=True)  76.2 us
    all_gather x1, blocking collectives, local(): full_vectors = lax.all_gather(vectors, ('dp', 'mp'), axis=1, tiled=True)  71.7 us
  transfers between devices with their start and end apart: 12, of which 9 were waited for; matrix products, arithmetic and copies ran while one was open for 15% of the time, Pallas kernels for 0%

commit v1 on v0

v1 whole, which is shorter than its diff:
```python
import functools

import jax
import jax.numpy as jnp
from jax import lax
from jax.experimental import pallas as pl
from jax.experimental.pallas import tpu as pltpu
from jax.sharding import PartitionSpec as P

HEAD_DIM = 64
STEP = 10
TAB_DEV = 8
MESH = pl.DeviceIdType.MESH
ANY = pl.ANY
BF = jnp.bfloat16
F32 = jnp.float32
NZ, NY, NC, NX = 4, 2, 2, 2

highest_mode = lax.Precision.HIGHEST
retrieval_scale = 0.17677669529663687
ln_epsilon = 1e-12
beta_first = 0.9
beta_second = 0.999
learn_rate = 0.05
vector_rate = 0.5
decay_rate = 0.01
adam_epsilon = 1e-08
clip_norm = 1.0


def layer_norm(values, gain_row, shift_row):
    centre = jnp.mean(values, axis=-1, keepdims=True)
    centred = values - centre
    spread = jnp.mean(centred * centred, axis=-1, keepdims=True)
    return centred * lax.rsqrt(spread + ln_epsilon) * gain_row + shift_row


def gelu_exact(values):
    return jax.nn.gelu(values, approximate=False)


def adamw_update(weight, moment, second, gradient, decay_factor, step_rate):
    moment_new = beta_first * moment + (1.0 - beta_first) * gradient
    second_new = beta_second * second + (1.0 - beta_second) * gradient * gradient
    first_hat = moment_new / (1.0 - beta_first**STEP)
    second_hat = second_new / (1.0 - beta_second**STEP)
    weight_new = weight - step_rate * (
        first_hat / (jnp.sqrt(second_hat) + adam_epsilon) + decay_factor * weight
    )
    return (moment_new, second_new, weight_new)


def squared(values):
    return jnp.sum(values * values)


class Place:
    def __init__(self):
        dp = lax.axis_index("dp")
        self.x = lax.axis_index("mp")
        self.c = lax.rem(dp, NC)
        self.y = lax.rem(dp // NC, NY)
        self.z = dp // (NC * NY)

    def dev(self, z=None, y=None, c=None, x=None):
        z = self.z if z is None else z
        y = self.y if y is None else y
        c = self.c if c is None else c
        x = self.x if x is None else x
        return ((z * NY + y) * NC + c, x)

    def others(self):
        out = [self.dev(z=lax.rem(self.z + k, NZ)) for k in range(1, NZ)]
        out.append(self.dev(x=1 - self.x))
        out.append(self.dev(y=1 - self.y))
        out.append(self.dev(c=1 - self.c))
        return out

    def eights(self):
        out = []
        for k in range(1, 8):
            dx, dy, dc = k & 1, (k >> 1) & 1, k >> 2
            out.append(
                self.dev(
                    x=self.x + dx - 2 * dx * self.x,
                    y=self.y + dy - 2 * dy * self.y,
                    c=self.c + dc - 2 * dc * self.c,
                )
            )
        return out


def greet(devices):
    barrier = pltpu.get_barrier_semaphore()
    for d in devices:
        pl.semaphore_signal(barrier, inc=1, device_id=d, device_id_type=MESH)
    pl.semaphore_wait(barrier, len(devices))


def remote(src, dst, ssem, rsem, dev):
    return pltpu.make_async_remote_copy(
        src_ref=src, dst_ref=dst, send_sem=ssem, recv_sem=rsem, device_id=dev, device_id_type=MESH
    )


def cols(x, half):
    return pl.ds(pl.multiple_of(x * half, 128), half)


def gather_kernel(n_in, n_out, index, *refs):
    ins, outs = refs[:n_in], refs[n_in : n_in + n_out]
    lsem, zs, zr, s1, r1, s2, r2, ds, dr = refs[n_in + n_out :]
    me = Place()
    greet(me.others())
    n = len(index)
    pieces = []
    for i, li, o, lo in index:
        src = ins[i] if li is None else ins[i].at[li]
        dst = outs[o] if lo is None else outs[o].at[lo]
        pieces.append((src, dst, dst.shape[-1] // 2))

    waits = []

    def go(copy):
        copy.start()
        waits.append(copy)
        return copy

    def step1(p):
        src, dst, half = pieces[p]
        blk = dst.at[me.z, me.y, me.c, :, cols(me.x, half)]
        loc = pltpu.make_async_copy(src, blk, lsem.at[p])
        loc.start()
        for k in range(1, NZ):
            go(remote(src, blk, zs.at[p, k], zr.at[p, k], me.dev(z=lax.rem(me.z + k, NZ))))
        return loc

    def part(p, stage):
        _, dst, half = pieces[p]
        own, other = cols(me.x, half), cols(1 - me.x, half)
        if stage == "z":
            return dst.at[:, me.y, me.c, :, own]
        if p % 2 == 0:
            if stage == "in1":
                return dst.at[:, me.y, me.c, :, other]
            if stage == "out2":
                return dst.at[:, me.y, me.c]
            return dst.at[:, 1 - me.y, me.c]
        if stage == "in1":
            return dst.at[:, 1 - me.y, me.c, :, own]
        if stage == "out2":
            return dst.at[:, :, me.c, :, own]
        return dst.at[:, :, me.c, :, other]

    def cross(p, stage, ref, which):
        dev = me.dev(c=1 - me.c)
        go(remote(ref, ref, ds.at[p, which], dr.at[p, which], dev))

    def step2(p, loc):
        src, dst, half = pieces[p]
        loc.wait()
        for k in range(1, NZ):
            blk = dst.at[lax.rem(me.z + NZ - k, NZ), me.y, me.c, :, cols(me.x, half)]
            remote(blk, blk, zs.at[p, k], zr.at[p, k], me.dev()).wait_recv()
        have = part(p, "z")
        dev = me.dev(x=1 - me.x) if p % 2 == 0 else me.dev(y=1 - me.y)
        go(remote(have, have, s1.at[p], r1.at[p], dev))
        cross(p, "z", have, 0)

    def step3(p):
        got = part(p, "in1")
        remote(got, got, s1.at[p], r1.at[p], me.dev()).wait_recv()
        have = part(p, "out2")
        dev = me.dev(y=1 - me.y) if p % 2 == 0 else me.dev(x=1 - me.x)
        go(remote(have, have, s2.at[p], r2.at[p], dev))
        cross(p, "in1", got, 1)

    def step4(p):
        got = part(p, "in2")
        remote(got, got, s2.at[p], r2.at[p], me.dev()).wait_recv()
        cross(p, "in2", got, 2)

    def step5(p):
        _, dst, half = pieces[p]
        own, other = cols(me.x, half), cols(1 - me.x, half)
        oc = 1 - me.c
        got = [dst.at[:, me.y, oc, :, own]]
        if p % 2 == 0:
            got += [dst.at[:, me.y, oc, :, other], dst.at[:, 1 - me.y, oc]]
        else:
            got += [dst.at[:, 1 - me.y, oc, :, own], dst.at[:, :, oc, :, other]]
        for which, ref in enumerate(got):
            remote(ref, ref, ds.at[p, which], dr.at[p, which], me.dev()).wait_recv()

    locs = {}
    ahead = 2
    for p in range(min(ahead, n)):
        locs[p] = step1(p)
    for t in range(n + 3):
        if t < n:
            step2(t, locs[t])
            if t + ahead < n:
                locs[t + ahead] = step1(t + ahead)
        if 0 <= t - 1 < n:
            step3(t - 1)
        if 0 <= t - 2 < n:
            step4(t - 2)
        if 0 <= t - 3 < n:
            step5(t - 3)
    for copy in waits:
        copy.wait_send()


def dma(*shape):
    return pltpu.SemaphoreType.DMA(shape)


def gather_fast(shards, small, rows):
    qk, va, inner, outer = shards
    width = 2 * qk.shape[2]
    ffw = 2 * inner.shape[2]
    zyc = (NZ, NY, NC)
    index = [
        (1, 0, 1, 0),
        (2, 0, 2, 0),
        (1, 1, 1, 1),
        (2, 1, 2, 1),
        (3, 0, 3, 0),
        (3, 1, 3, 1),
        (4, 0, 4, 0),
        (4, 1, 4, 1),
        (0, None, 0, None),
    ]
    n = len(index)
    outs = pl.pallas_call(
        functools.partial(gather_kernel, 5, 5, index),
        out_shape=[
            jax.ShapeDtypeStruct(zyc + (small.shape[0], 2 * small.shape[1]), F32),
            jax.ShapeDtypeStruct((2,) + zyc + (rows, width), BF),
            jax.ShapeDtypeStruct((2,) + zyc + (rows, width), BF),
            jax.ShapeDtypeStruct((2,) + zyc + (rows, ffw), BF),
            jax.ShapeDtypeStruct((2,) + zyc + (rows, ffw), BF),
        ],
        in_specs=[pl.BlockSpec(memory_space=ANY)] * 5,
        out_specs=[pl.BlockSpec(memory_space=ANY)] * 5,
        scratch_shapes=[
            dma(n), dma(n, NZ), dma(n, NZ), dma(n), dma(n), dma(n), dma(n), dma(n, 3), dma(n, 3),
        ],
        compiler_params=pltpu.CompilerParams(collective_id=1, has_side_effects=True),
        name="gather",
    )(small, qk, va, inner, outer)
    return outs


def reduce_kernel(n_in, n_out, index, *refs):
    ins, outs = refs[:n_in], refs[n_in : n_in + n_out]
    rest = refs[n_in + n_out :]
    nb = len(index)
    bufs, rest = rest[: 5 * nb], rest[5 * nb :]
    sq4, sq8, lsem, ds, dr, s1, r1, s2, r2, zs, zr, xs, xr, qs, qr, es, er = rest
    send_out, send_dx = ins[-2:]
    peer_out, peer_dx, peer_small, norm_ref = outs[-4:]
    me = Place()
    greet(me.others() + me.eights())
    n = len(index)
    waits = []

    def go(copy):
        copy.start()
        waits.append(copy)
        return copy

    oc, oy, ox = 1 - me.c, 1 - me.y, 1 - me.x
    pieces = []
    for p, (i, li, o, lo, sx) in enumerate(index):
        src = ins[i] if li is None else ins[i].at[li]
        dst = outs[o] if lo is None else outs[o].at[lo]
        pieces.append((src, dst) + tuple(bufs[5 * p : 5 * p + 5]))

    def step1(p):
        src, _, own, got1, _, _, _ = pieces[p]
        go(remote(src.at[:, :, oc], got1, ds.at[p], dr.at[p], me.dev(c=oc)))
        loc = pltpu.make_async_copy(src.at[:, :, me.c], own, lsem.at[p])
        loc.start()
        return loc

    def half(ref):
        return ref.shape[-1] // 2

    def step2(p, loc):
        _, _, own, got1, got2, got3, got4 = pieces[p]
        loc.wait()
        remote(got1, got1, ds.at[p], dr.at[p], me.dev()).wait_recv()
        own[...] = own[...] + got1[...]
        if p % 2 == 0:
            go(remote(own.at[:, oy], got2, s1.at[p], r1.at[p], me.dev(y=oy)))
        else:
            go(remote(own.at[:, :, :, cols(ox, half(own))], got2, s1.at[p], r1.at[p], me.dev(x=ox)))

    def step3(p):
        _, _, own, _, got2, got3, _ = pieces[p]
        remote(got2, got2, s1.at[p], r1.at[p], me.dev()).wait_recv()
        h = half(own)
        if p % 2 == 0:
            own[:, me.y] = own[:, me.y] + got2[...]
            go(remote(own.at[:, me.y, :, cols(ox, h)], got3, s2.at[p], r2.at[p], me.dev(x=ox)))
        else:
            own[:, :, :, cols(me.x, h)] = own[:, :, :, cols(me.x, h)] + got2[...]
            go(remote(own.at[:, oy, :, cols(me.x, h)], got3, s2.at[p], r2.at[p], me.dev(y=oy)))

    def step4(p):
        _, _, own, _, _, got3, got4 = pieces[p]
        remote(got3, got3, s2.at[p], r2.at[p], me.dev()).wait_recv()
        h = half(own)
        mine = cols(me.x, h)
        own[:, me.y, :, mine] = own[:, me.y, :, mine] + got3[...]
        for k in range(1, NZ):
            tz = lax.rem(me.z + k, NZ)
            go(remote(own.at[tz, me.y, :, mine], got4.at[k], zs.at[p, k], zr.at[p, k], me.dev(z=tz)))

    def step5(p):
        _, dst, own, _, _, _, got4 = pieces[p]
        for k in range(1, NZ):
            remote(got4.at[k], got4.at[k], zs.at[p, k], zr.at[p, k], me.dev()).wait_recv()
        total = own[me.z, me.y, :, cols(me.x, half(own))].astype(F32)
        for k in range(1, NZ):
            total = total + got4[k].astype(F32)
        dst[...] = total
        return jnp.sum(total * total, keepdims=True)

    go(remote(send_out, peer_out, xs.at[0], xr.at[0], me.dev(x=ox)))
    locs = {}
    ahead = 2
    total = jnp.zeros((1, 1), F32)
    for p in range(min(ahead, n)):
        locs[p] = step1(p)
    for t in range(n + 3):
        if t < n:
            step2(t, locs[t])
            if t + ahead < n:
                locs[t + ahead] = step1(t + ahead)
        if 0 <= t - 1 < n:
            step3(t - 1)
        if 0 <= t - 2 < n:
            step4(t - 2)
        if 0 <= t - 3 < n:
            p = t - 3
            part = step5(p)
            if index[p][4]:
                total = total + part
    go(remote(send_dx, peer_dx, xs.at[1], xr.at[1], me.dev(x=ox)))
    small = outs[index[-1][2]]
    go(remote(small, peer_small, xs.at[2], xr.at[2], me.dev(x=ox)))
    row = lax.broadcasted_iota(jnp.int32, small.shape, 0)
    keep = jnp.where(row < 36, small[...], 0.0)
    total = total + jnp.sum(keep * keep, keepdims=True)
    sq4[0] = jnp.broadcast_to(total, (8, 128))
    copies = []
    for k in range(1, NZ):
        c = remote(sq4.at[0], sq4.at[k], qs.at[k], qr.at[k], me.dev(z=lax.rem(me.z + k, NZ)))
        copies.append(go(c))
    for k in range(1, NZ):
        copies[k - 1].wait_recv()
    def at_z(z):
        out = jnp.zeros((8, 128), F32)
        for k in range(NZ):
            src = lax.rem(me.z + NZ - k, NZ)
            out = out + jnp.where(src == z, sq4[k], 0.0)
        return out
    group = at_z(0) + at_z(1) + at_z(2) + at_z(3)
    sq8[0] = group
    copies = []
    for k, dev in enumerate(me.eights(), 1):
        copies.append(go(remote(sq8.at[0], sq8.at[k], es.at[k], er.at[k], dev)))
    for copy in copies:
        copy.wait_recv()
    code = me.x + 2 * me.y + 4 * me.c

    def at_code(w):
        out = jnp.zeros((8, 128), F32)
        for k in range(8):
            dx, dy, dc = k & 1, (k >> 1) & 1, k >> 2
            src = (
                (me.x + dx - 2 * dx * me.x)
                + 2 * (me.y + dy - 2 * dy * me.y)
                + 4 * (me.c + dc - 2 * dc * me.c)
            )
            out = out + jnp.where(src == w, sq8[k], 0.0)
        return out

    whole = at_code(0)
    for w in range(1, 8):
        whole = whole + at_code(w)
    norm_ref[...] = whole
    remote(peer_out, peer_out, xs.at[0], xr.at[0], me.dev()).wait_recv()
    remote(peer_dx, peer_dx, xs.at[1], xr.at[1], me.dev()).wait_recv()
    remote(peer_small, peer_small, xs.at[2], xr.at[2], me.dev()).wait_recv()
    for copy in waits:
        copy.wait_send()


def reduce_fast(grads, small, own_out, own_dx, rows):
    zyc = (NZ, NY, NC)
    arrays = [small.reshape(zyc + small.shape[1:])]
    arrays += [g.reshape((2,) + zyc + (rows, g.shape[2])) for g in grads]
    index = [
        (4, 0, 4, 0, True),
        (4, 1, 4, 1, True),
        (3, 0, 3, 0, True),
        (3, 1, 3, 1, True),
        (2, 1, 2, 1, True),
        (1, 0, 1, 0, True),
        (1, 1, 1, 1, True),
        (2, 0, 2, 0, True),
        (0, None, 0, None, False),
    ]
    n = len(index)
    out_shape = [
        jax.ShapeDtypeStruct((small.shape[1], small.shape[2] // 2), F32),
    ] + [jax.ShapeDtypeStruct((2, rows, g.shape[2] // 2), F32) for g in grads]
    out_shape += [
        jax.ShapeDtypeStruct(own_out.shape, BF),
        jax.ShapeDtypeStruct(own_dx.shape, BF),
        jax.ShapeDtypeStruct((small.shape[1], small.shape[2] // 2), F32),
        jax.ShapeDtypeStruct((8, 128), F32),
    ]
    bufs = []
    for p, (i, _, _, _, _) in enumerate(index):
        r, w = arrays[i].shape[-2:]
        dt = arrays[i].dtype
        bufs += [pltpu.VMEM((NZ, NY, r, w), dt), pltpu.VMEM((NZ, NY, r, w), dt)]
        if p % 2 == 0:
            bufs += [pltpu.VMEM((NZ, r, w), dt)]
        else:
            bufs += [pltpu.VMEM((NZ, NY, r, w // 2), dt)]
        bufs += [pltpu.VMEM((NZ, r, w // 2), dt), pltpu.VMEM((NZ, r, w // 2), dt)]
    vm = pl.BlockSpec(memory_space=pltpu.VMEM)
    hb = pl.BlockSpec(memory_space=ANY)
    return pl.pallas_call(
        functools.partial(reduce_kernel, 7, len(out_shape), index),
        out_shape=out_shape,
        in_specs=[hb] * 7,
        out_specs=[vm] * 5 + [hb, hb, vm, vm],
        scratch_shapes=bufs
        + [
            pltpu.VMEM((NZ, 8, 128), F32), pltpu.VMEM((8, 8, 128), F32),
            dma(n), dma(n), dma(n), dma(n), dma(n), dma(n), dma(n), dma(n, NZ), dma(n, NZ),
            dma(3), dma(3), dma(NZ), dma(NZ), dma(8), dma(8),
        ],
        compiler_params=pltpu.CompilerParams(
            collective_id=2, has_side_effects=True, vmem_limit_bytes=56 * 2**20
        ),
        name="reduce",
    )(*arrays, own_out, own_dx)


def gather_plain(shards, small, rows):
    def both(v, axis):
        v = lax.all_gather(v, "dp", axis=axis, tiled=True)
        return lax.all_gather(v, "mp", axis=2, tiled=True)

    return [both(small[None], 0)] + [both(v, 1) for v in shards]


def reduce_plain(grads, small, own_out, own_dx, rows):
    def both(v, axis, wide):
        v = lax.psum_scatter(v.astype(F32), "mp", scatter_dimension=wide, tiled=True)
        return lax.psum_scatter(v, "dp", scatter_dimension=axis, tiled=True)

    small_sum = both(small, 0, 2)[0]
    sums = [both(g, 1, 2) for g in grads]
    ox = 1 - lax.axis_index("mp")
    swap = [(0, 1), (1, 0)]
    peer_out = lax.ppermute(own_out, "mp", swap)
    peer_dx = lax.ppermute(own_dx, "mp", swap)
    peer_small = lax.ppermute(small_sum, "mp", swap)
    squares = sum(squared(g) for g in sums) + squared(small_sum[:-4])
    total = lax.psum(squares, ("dp", "mp"))
    return [small_sum] + sums + [peer_out, peer_dx, peer_small, jnp.full((8, 128), total)]


def local(
    tokens, cotangent, lengths, doc_ids, doc_rows,
    w_qkv, m_qkv, v_qkv, w_attn, m_attn, v_attn, w_inner, m_inner, v_inner,
    w_outer, m_outer, v_outer, w_proj, m_proj, v_proj, vectors, m_vectors, v_vectors,
):
    mp = lax.axis_index("mp")
    n_dp, n_mp = lax.axis_size("dp"), lax.axis_size("mp")
    fast = n_dp == NZ * NY * NC and n_mp == NX
    seqs = lengths.shape[0]
    all_rows, width = tokens.shape
    seq_len = all_rows // seqs
    full = seqs // 2
    n_full, n_half = full * seq_len, seq_len // 2
    n_own = n_full + n_half
    heads = width // HEAD_DIM
    rows = w_qkv.shape[1]
    half_w, half_ff = w_qkv.shape[2], w_inner.shape[1]
    ff = 2 * half_ff
    score_scale = HEAD_DIM ** (-0.5)

    def two(v):
        return v.reshape(rows, 2, half_ff // 2).transpose(1, 0, 2)

    qk_s = w_qkv[:2].astype(BF)
    va_s = jnp.stack([w_qkv[2], w_attn]).astype(BF)
    inner_s = two(w_inner.astype(BF))
    outer_s = two(w_outer.astype(BF))
    vec_pad = jnp.pad(vectors, ((0, 16 - vectors.shape[0]), (0, 128 - vectors.shape[1])))
    half_rows = rows // 2
    proj_half = lax.dynamic_slice_in_dim(w_proj, mp * half_rows, half_rows, 0)
    small_s = jnp.concatenate([proj_half, vec_pad], axis=0)
    gather = gather_fast if fast else gather_plain
    small_g, qk, va, inner, outer = gather([qk_s, va_s, inner_s, outer_s], small_s, rows)
    small_g = small_g.reshape(n_dp, half_rows + 16, 2, 128)
    proj = small_g[:, :half_rows].transpose(0, 2, 1, 3).reshape(width, 128).astype(BF)
    nvec, vec_lanes = vectors.shape
    vec = small_g[:, half_rows : half_rows + nvec, :, :vec_lanes].transpose(1, 0, 2, 3).reshape(nvec, width)
    qk = qk.reshape(2, width, width)
    va = va.reshape(2, width, width)
    inner = inner.reshape(2, width, half_ff)
    outer = outer.reshape(2, width, half_ff)
    ff_rows = nvec - 8
    b_inner = (
        vec[5 : 5 + ff_rows].reshape(2, 2, half_ff // 2).transpose(1, 0, 2).reshape(2, half_ff)
    )
    bias_attn, gain_one, shift_one = vec[2], vec[3], vec[4]
    bias_outer, gain_two, shift_two = vec[5 + ff_rows], vec[6 + ff_rows], vec[7 + ff_rows]

    a0 = mp * n_own + mp * 0
    a0 = mp * (n_full + seq_len)
    h0 = n_full + mp * n_half
    o0 = n_full + (1 - mp) * n_half

    def own_rows(v):
        return jnp.concatenate(
            [lax.dynamic_slice_in_dim(v, a0, n_full, 0), lax.dynamic_slice_in_dim(v, h0, n_half, 0)]
        )

    x_own = own_rows(tokens)
    x_all = jnp.concatenate([x_own, lax.dynamic_slice_in_dim(tokens, o0, n_half, 0)])
    cot = own_rows(cotangent)
    my_seqs = jnp.concatenate([mp * (full + 1) + jnp.arange(full), jnp.array([full])])
    my_len = lengths[my_seqs]
    pos = jnp.arange(seq_len)
    pos_last = jnp.where(pos < n_half, pos + mp * n_half, pos - n_half + (1 - mp) * n_half)
    valid_full = pos[None, :] < my_len[:full, None]
    valid_last = pos_last[None, :] < my_len[full:, None]

    q = (jnp.dot(x_own, qk[0], preferred_element_type=F32) + vec[0]).astype(BF)
    k = jnp.dot(x_all, qk[1], preferred_element_type=F32).astype(BF)
    v = (jnp.dot(x_all, va[0], preferred_element_type=F32) + vec[1]).astype(BF)

    def split(t, first):
        return (
            t[:n_full].reshape(full, seq_len, heads, HEAD_DIM),
            t[n_full:].reshape(1, first, heads, HEAD_DIM),
        )

    qs, ks, vs = split(q, n_half), split(k, seq_len), split(v, seq_len)
    valids = (valid_full, valid_last)
    lses, outs = [], []

    def scores(qh, kh, valid):
        raw = jnp.einsum("gqhe,gkhe->ghqk", qh, kh, preferred_element_type=F32) * score_scale
        return jnp.where(valid[:, None, None, :], raw, -1000000000.0)

    for qh, kh, vh, valid in zip(qs, ks, vs, valids):
        s = scores(qh, kh, valid)
        top = jnp.max(s, axis=-1, keepdims=True)
        lse = top + jnp.log(jnp.sum(jnp.exp(s - top), axis=-1, keepdims=True))
        pb = jnp.exp(s - lse).astype(BF)
        o = jnp.einsum("ghqk,gkhe->gqhe", pb, vh, preferred_element_type=F32)
        outs.append(o.reshape(-1, width).astype(BF))
        lses.append(lse)
    mixed = jnp.concatenate(outs)
    attn = jnp.einsum("te,de->td", mixed, va[1], preferred_element_type=F32)
    z1 = x_own.astype(F32) + attn + bias_attn
    normed, norm_one_back = jax.vjp(layer_norm, z1, gain_one, shift_one)
    normed_low = normed.astype(BF)
    pre = jnp.einsum("td,hdf->htf", normed_low, inner, preferred_element_type=F32) + b_inner[:, None, :]
    act, gelu_back = jax.vjp(gelu_exact, pre)
    act_low = act.astype(BF)
    f_out = jnp.einsum("htf,hdf->td", act_low, outer, preferred_element_type=F32)
    z2 = normed + f_out + bias_outer
    output, norm_two_back = jax.vjp(layer_norm, z2, gain_two, shift_two)
    out_own = output.astype(BF)

    n_mine = full + 1
    mine = jnp.where((jnp.arange(n_mine) < full) | (mp == 0), 1.0, 0.0).astype(F32)
    cls_low = out_own[:: seq_len][:n_mine]
    docs = doc_rows[my_seqs].astype(F32)
    ids = doc_ids[my_seqs]
    query = jnp.dot(cls_low, proj, preferred_element_type=F32).astype(BF)
    query_float = query.astype(F32)
    doc_scores = jnp.einsum("gp,gkp->gk", query_float, docs, precision=highest_mode) * retrieval_scale
    soft = jax.nn.softmax(doc_scores, axis=-1)
    target = (jnp.arange(doc_scores.shape[1]) == 0).astype(F32)
    score_grad = (soft - target[None, :]) * retrieval_scale * mine[:, None]
    query_grad = jnp.einsum("gk,gkp->gp", score_grad, docs, precision=highest_mode).astype(BF)
    row_grads = score_grad[:, :, None] * query_float[:, None, :]
    cls_grad = jnp.einsum("gp,dp->gd", query_grad, proj, preferred_element_type=F32)
    proj_grad = jnp.einsum("gd,gp->dp", cls_low, query_grad, preferred_element_type=F32)
    table_rows = TAB_DEV * n_dp
    one_hot = (jnp.arange(table_rows)[:, None] == ids.reshape(1, -1)).astype(F32)
    table_local = jnp.dot(one_hot, row_grads.reshape(-1, row_grads.shape[2]), precision=highest_mode)

    dy = cot.astype(F32)
    first_rows = jnp.arange(n_mine) * seq_len
    dy = dy.at[first_rows].add(cls_grad)
    dz2, dg2, dc2 = norm_two_back(dy)
    df = dz2.astype(BF)
    dg = jnp.einsum("td,hdf->htf", df, outer, preferred_element_type=F32)
    g_outer = jnp.einsum("td,htf->hdf", df, act_low, preferred_element_type=F32).astype(BF)
    (du,) = gelu_back(dg)
    du = du.astype(BF)
    g_inner = jnp.einsum("td,htf->hdf", normed_low, du, preferred_element_type=F32).astype(BF)
    dh1 = jnp.einsum("htf,hdf->td", du, inner, preferred_element_type=F32) + dz2
    dz1, dg1, dc1 = norm_one_back(dh1)
    da = dz1.astype(BF)
    do = jnp.dot(da, va[1], preferred_element_type=F32).astype(BF)
    g_attn = jnp.einsum("td,te->de", da, mixed, preferred_element_type=F32)
    dos = split(do, n_half)
    dqs, dks, dvs = [], [], []
    for qh, kh, vh, doh, valid, lse in zip(qs, ks, vs, dos, valids, lses):
        probs = jnp.exp(scores(qh, kh, valid) - lse)
        dp_ = jnp.einsum("gqhe,gkhe->ghqk", doh, vh, preferred_element_type=F32)
        delta = jnp.sum(probs * dp_, axis=-1, keepdims=True)
        ds_ = (probs * (dp_ - delta)).astype(BF)
        dqs.append((jnp.einsum("ghqk,gkhe->gqhe", ds_, kh, preferred_element_type=F32) * score_scale).reshape(-1, width))
        dks.append((jnp.einsum("ghqk,gqhe->gkhe", ds_, qh, preferred_element_type=F32) * score_scale).reshape(-1, width))
        dvs.append(jnp.einsum("ghqk,gqhe->gkhe", probs.astype(BF), doh, preferred_element_type=F32).reshape(-1, width))
    dq = jnp.concatenate(dqs).astype(BF)
    dk = jnp.concatenate(dks).astype(BF)
    dv = jnp.concatenate(dvs).astype(BF)
    g_q = jnp.einsum("td,te->de", x_own, dq, preferred_element_type=F32)
    g_k = jnp.einsum("td,te->de", x_all, dk, preferred_element_type=F32)
    g_v = jnp.einsum("td,te->de", x_all, dv, preferred_element_type=F32)
    g_qk = jnp.stack([g_q, g_k]).astype(BF)
    g_va = jnp.stack([g_v, g_attn]).astype(BF)
    dx_own = jnp.einsum("te,de->td", dq, qk[0], preferred_element_type=F32) + dz1
    dx_all = jnp.einsum("te,de->td", dk, qk[1], preferred_element_type=F32)
    dx_all = dx_all + jnp.einsum("te,de->td", dv, va[0], preferred_element_type=F32)
    dx = jnp.concatenate([dx_all[:n_own] + dx_own, dx_all[n_own:]]).astype(BF)
    db_inner = jnp.sum(du.astype(F32), axis=1)
    db_inner = db_inner.reshape(2, 2, half_ff // 2).transpose(1, 0, 2).reshape(ff_rows, width)
    vec_grad = jnp.concatenate(
        [
            jnp.stack(
                [
                    jnp.sum(dq.astype(F32), axis=0),
                    jnp.sum(dv.astype(F32), axis=0),
                    jnp.sum(dz1, axis=0),
                    dg1,
                    dc1,
                ]
            ),
            db_inner,
            jnp.stack([jnp.sum(dz2, axis=0), dg2, dc2]),
        ]
    )
    vg = vec_grad.reshape(nvec, n_dp, 2, vec_lanes).transpose(1, 0, 2, 3)
    vg = jnp.pad(vg, ((0, 0), (0, 0), (0, 0), (0, 128 - vec_lanes))).reshape(n_dp, nvec, 256)
    pg = proj_grad.reshape(n_dp, 2, half_rows, 128).transpose(0, 2, 1, 3).reshape(n_dp, half_rows, 256)
    tg = table_local.reshape(n_dp, 2, TAB_DEV // 2, 128).transpose(0, 2, 1, 3).reshape(n_dp, TAB_DEV // 2, 256)
    small = jnp.concatenate([pg, vg, tg], axis=1)

    reduce = reduce_fast if fast else reduce_plain
    (small_r, qk_r, va_r, inner_r, outer_r, peer_out, peer_dx, peer_small, total) = reduce(
        [g_qk, g_va, g_inner, g_outer], small, out_own, dx, rows
    )

    def whole_rows(own, peer):
        lo = jnp.where(mp == 0, own[:n_own], peer[:n_own])
        hi = jnp.where(mp == 0, peer[:n_own], own[:n_own])
        return lo, hi

    lo, hi = whole_rows(out_own, peer_out)
    out_tokens = jnp.concatenate([lo, hi[n_full:], hi[:n_full]])
    lo, hi = whole_rows(dx.astype(F32), peer_dx.astype(F32))
    tail = jnp.where(mp == 0, dx[n_own:], peer_dx[n_own:]).astype(F32)
    tail_hi = jnp.where(mp == 0, peer_dx[n_own:], dx[n_own:]).astype(F32)
    input_grad = jnp.concatenate(
        [lo[:n_full], lo[n_full:] + tail_hi, hi[n_full:] + tail, hi[:n_full]]
    )

    def both_halves(at, count):
        mine_, peer_ = small_r[at : at + count], peer_small[at : at + count]
        return jnp.concatenate(
            [jnp.where(mp == 0, mine_, peer_), jnp.where(mp == 0, peer_, mine_)]
        )

    proj_r = both_halves(0, half_rows)
    table_grad = both_halves(half_rows + nvec, TAB_DEV // 2)
    vector_r = small_r[half_rows : half_rows + nvec, :vec_lanes]
    qkv_r = jnp.stack([qk_r[0], qk_r[1], va_r[0]])
    attn_r = va_r[1]

    def back(v):
        return v.transpose(1, 0, 2).reshape(rows, half_ff)

    inner_r, outer_r = back(inner_r), back(outer_r)
    grad_norm = jnp.sqrt(total[0, 0])
    clip = clip_norm / jnp.maximum(grad_norm, clip_norm)
    results = [out_tokens, input_grad, grad_norm]
    for w, m, s, g, dec, rate in (
        (w_qkv, m_qkv, v_qkv, qkv_r, decay_rate, learn_rate),
        (w_attn, m_attn, v_attn, attn_r, decay_rate, learn_rate),
        (w_inner, m_inner, v_inner, inner_r, decay_rate, learn_rate),
        (w_outer, m_outer, v_outer, outer_r, decay_rate, learn_rate),
        (w_proj, m_proj, v_proj, proj_r, decay_rate, learn_rate),
        (vectors, m_vectors, v_vectors, vector_r, 0.0, vector_rate),
    ):
        results += list(adamw_update(w, m, s, g * clip, dec, rate))
    return tuple(results) + (table_grad,)


def solution(mesh):
    mat = P("dp", "mp")
    rep = P("dp", None)
    qkv = P(None, "dp", "mp")
    vec = P(None, ("dp", "mp"))
    placed = (rep, rep, P("dp"), rep, P("dp", None, None), qkv, qkv, qkv)
    placed += (mat,) * 9 + (rep,) * 3 + (vec,) * 3
    given = (rep, rep, P(), qkv, qkv, qkv) + (mat,) * 9 + (rep,) * 3 + (vec,) * 3 + (rep,)
    return jax.shard_map(local, mesh=mesh, in_specs=placed, out_specs=given, check_vma=False)
```

time: 1260 us -> 495 us (0.39)
  waiting for transfers between devices: 725 us -> 0 us
  Pallas kernels: 0 us -> 216 us
  blocking collectives: 193 us -> 0 us
  other arithmetic: 84.4 us -> 52.6 us
  between operations: 22.8 us -> 4.58 us
  matrix products: 144 us -> 127 us
    psum x4 -> x0, waiting for transfers between devices: 417 us -> none  [the longest x1 112 us: local(): input_grad = lax.psum(input_part, 'mp') + resid_one_grad]
    pallas_call x0 -> x2, Pallas kernels: none -> 216 us  [the longest x1 133 us: reduce_fast(): pl.pallas_call(functools.partial(reduce_kernel, 7, len(out_shape), index)...]
    reduce_scatter x4 -> x0, waiting for transfers between devices: 153 us -> none  [the longest x1 76.7 us: local(): lax.psum_scatter(outer_wgrad, 'dp', scatter_dimension=0, tiled=True)]
    all_gather x3 -> x0, blocking collectives: 112 us -> none  [the longest x1 71.7 us: local(): full_vectors = lax.all_gather(vectors, ('dp', 'mp'), axis=1, tiled=True)]
    unnamed x13 -> x0, waiting for transfers between devices: 98.4 us -> none
    all_gather x3 -> x0, waiting for transfers between devices: 56.5 us -> none  [the longest x1 39.4 us: local(): lax.all_gather(w_inner.astype(jnp.bfloat16), 'dp', axis=0, tiled=True)]
    psum x1 -> x0, blocking collectives: 41 us -> none  [local(): total_squares = lax.psum(local_squares, ('dp', 'mp'))]
    unnamed x1 -> x0, blocking collectives: 40.2 us -> none
  transfers between devices with their start and end apart: 12 -> 0, of which waited for: 9 -> 0; matrix products, arithmetic and copies ran while one was open for 15% -> 0% of each run, Pallas kernels for 0% -> 0%
where the time goes in v1:
time: 495 us; the launch traced here: 492 us
  Pallas kernels  216 us (44%)
  matrix products  127 us (26%)
  local copies, waits for them, and re-layouts  92 us (19%)
  other arithmetic  52.6 us (11%)
    pallas_call x1, Pallas kernels, reduce_fast(): pl.pallas_call(functools.partial(reduce_kernel, 7, len(out_shape), index)...  133 us
    pallas_call x1, Pallas kernels, gather_fast(): pl.pallas_call(functools.partial(gather_kernel, 5, 5, index), out_shape=[...  83.1 us
    dot_general x1, matrix products, local(): jnp.einsum('td,hdf->htf', normed_low, inner, preferred_element_type=F32)  26 us
    reshape x8, local copies, waits for them, and re-layouts, split(): t[:n_full].reshape(full, seq_len, heads, HEAD_DIM)  24.4 us
    dot_general x2, matrix products, local(): o = jnp.einsum('ghqk,gkhe->gqhe', pb, vh, preferred_element_type=F32)  15.2 us
    unnamed x261, local copies, waits for them, and re-layouts  12.1 us
    dot_general x1, matrix products, local(): dg = jnp.einsum('td,hdf->htf', df, outer, preferred_element_type=F32)  12.1 us
    dot_general x2, matrix products, local(): jnp.einsum('ghqk,gqhe->gkhe', probs.astype(BF), doh, preferred_element_ty...  10.5 us

profile of v1, /device:TPU:0, one launch (start us, length us, event | category | flops | bytes accessed | tf_op | source)
XLA Modules:
  0.0 492.4 jit_solution(7872771054962994255)
XLA Ops:
  17.5 2.4 constant_dynamic-slice_fusion.1
  21.4 83.1 %gather.19 = (f32[4,2,2,40,256]{4,3,2,1,0:T(8,128)}, bf16[2,4,2,2,48,768]{5,4,3,2,1,0:T(8,128)(2,1)}, bf16[2,4,2,2,48,768]{5,4,3,2,1,0:T(8,128)(2,1)}, bf16[2,4,...) custom-call(f32[40,128]{1,0:T(8,128)} %select_maximum_fusion.refs_0_, bf16[2,48,384]{2,1,0:T(8,128)(2,1)} %slice.231.refs_1_, ...), custom_call_target="tpu_custom_call" | custom-call | tf_op jit(solution)/shard_map/gather/pallas_call | solution.py:235
  104.6 4.2 fusion.100
  108.7 1.9 reshape.528
  115.4 2.2 add_convert_fusion.2
  125.3 1.8 reshape.593
  127.1 2.5 copy.79
  129.7 3.1 reshape.591
  132.8 3.2 copy.80
  136.0 3.9 reshape.592
  139.9 3.6 copy.78
  145.8 1.6 convolution_convert_fusion.11
  147.5 2.9 fusion.22
  150.4 2.5 exponential_reduce_fusion
  154.4 13.5 %fusion.28 = bf16[2,288,12,64]{1,3,2,0:T(8,128)(2,1)S(1)} fusion(bf16[2,288,12,64]{1,3,2,0:T(8,128)(2,1)S(1)} %copy-done.18, f32[2,12,288,288]{2,3,1,0:T(8,128)S(1)} %get-tuple-element.107, f32[2,12,288]{2,1,0:T(8,128)S(1)} %log_add_fusion, pred[2,288]{1,0:T(4,128)(4,1)S(1)} %iota_compare_fusion.1), kind=kOutput, calls=%fused_computation.94 | convolution fusion | flops 263208960 | bytes 9760320 | tf_op jit(solution)/shard_map/ghqk,gkhe->gqhe/dot_general | solution.py:573
  170.0 3.2 fusion.103
  174.1 26.0 %fusion.9 = (bf16[2,720,1536]{2,1,0:T(8,128)(2,1)S(1)}, f32[2,720,1536]{2,1,0:T(8,128)}, f32[2,1536,720]{1,2,0:T(8,128)}) fusion(f32[2,1536]{1,0:T(2,128)S(1)} %bitcast.330, bf16[2,768,1536]{2,1,0:T(8,128)(2,1)} %bitcast.335, f32[720,768]{1,0:T(8,128)S(1)} %get-tuple-element.109, f32[768]{0:T(1024)S(1)} %copy-done.107, f32[768]{0:T(1024)S(1)} %mul.525, ...), kind=kOutput, calls=%fused_computation.26 | convolution fusion | flops 3546132480 | bytes 29073024 | tf_op jit(solution)/shard_map/td,hdf->htf/dot_general | solution.py:581
  200.2 3.9 fusion.104
  209.0 3.7 scatter_fusion
  213.6 2.6 multiply_reduce_fusion.2
  217.2 12.1 %convert_reduce_fusion = (f32[2,1536]{1,0:T(2,128)S(1)}, bf16[2,720,1536]{2,1,0:T(8,128)(2,1)S(1)}) fusion(f32[2,720,1536]{2,1,0:T(8,128)} %get-tuple-element.79, bf16[2,768,1536]{2,1,0:T(8,128)(2,1)} %bitcast.339, f32[720,768]{1,0:T(8,128)S(1)} %get-tuple-element.77, f32[720]{0:T(1024)S(1)} %negate_multiply_fusion.2, ...), kind=kOutput, calls=%fused_computation.27 | convolution fusion | flops 3436090368 | bytes 29076288 | tf_op jit(solution)/shard_map/td,hdf->htf/dot_general | solution.py:613
  229.4 4.2 multiply_reduce_fusion.3
  234.5 5.9 %convolution_convert_fusion.1 = bf16[2,1536,768]{1,2,0:T(8,128)(2,1)} fusion(bf16[2,720,1536]{2,1,0:T(8,128)(2,1)S(1)} %get-tuple-element.121, f32[720,768]{1,0:T(8,128)S(1)} %copy-done.13, f32[768]{0:T(1024)S(1)} %copy-done.108, f32[768]{0:T(1024)S(1)} %copy-done.94, f32[720]{0:T(1024)S(1)} %copy-done.96, f32[720]{0:T(1024)S(1)} %copy-done.85), kind=kOutput, calls=%fused_computation.44 | convolution fusion | flops 3402510336 | bytes 11366016 | tf_op jit(solution)/shard_map/td,htf->hdf/dot_general | solution.py:617
  240.5 2.5 convolution_convert_fusion.3
  244.6 5.9 %convolution_convert_fusion = bf16[2,1536,768]{1,2,0:T(8,128)(2,1)} fusion(bf16[2,720,1536]{2,1,0:T(8,128)(2,1)S(1)} %bitcast.346, f32[720,768]{1,0:T(8,128)S(1)} %get-tuple-element.77, f32[720]{0:T(1024)S(1)} %negate_multiply_fusion.2), kind=kOutput, calls=%fused_computation.43 | convolution fusion | flops 3400851456 | bytes 11356992 | tf_op jit(solution)/shard_map/td,htf->hdf/dot_general | solution.py:614
  259.5 3.5 convolution_convert_fusion.10
  262.9 2.7 reshape.594
  265.6 3.5 copy.89
  269.2 7.0 %fusion.29 = bf16[2,288,12,64]{1,3,2,0:T(8,128)(2,1)S(1)} fusion(bf16[2,288,12,64]{1,3,2,0:T(8,128)(2,1)S(1)} %copy.89, f32[2,12,288,288]{2,3,1,0:T(8,128)} %copy-done.2, f32[2,12,288]{2,1,0:T(8,128)S(1)} %copy-done.58, pred[2,288]{1,0:T(4,128)(4,1)S(1)} %copy-done.76), kind=kOutput, calls=%fused_computation.95 | convolution fusion | flops 263208960 | bytes 9760320 | tf_op jit(solution)/shard_map/ghqk,gqhe->gkhe/dot_general | solution.py:632
  276.2 2.3 copy.97
  278.5 3.1 reshape.543
  281.6 2.1 convert_reduce_fusion.1
  284.4 3.3 convolution_convert_fusion.4
  287.8 1.6 pad_maximum_fusion.2.refs_2_
  295.0 5.0 %multiply_reduce_fusion = (f32[2,12,288]{2,1,0:T(8,128)S(1)}, f32[2,12,288,288]{2,3,1,0:T(8,128)S(1)}) fusion(f32[2,12,288,288]{2,3,1,0:T(8,128)S(1)} %bitcast.288, f32[2,12,288]{2,1,0:T(8,128)S(1)} %copy-done.58, pred[2,288]{1,0:T(4,128)(4,1)S(1)} %copy-done.76, bf16[2,288,12,64]{1,3,2,0:T(8,128)(2,1)} %copy-done.20, bf16[2,288,12,64]{1,3,2,0:T(8,128)(2,1)S(1)} %copy-done.19), kind=kOutput, calls=%fused_computation.6 | convolution fusion | flops 264750336 | bytes 17750592 | tf_op jit(solution)/shard_map/gqhe,gkhe->ghqk/dot_general | solution.py:627
  300.1 3.5 multiply_convert_fusion
  303.6 3.0 fusion.31
  309.0 1.6 reshape.540
  310.7 2.5 copy.102
  313.2 2.0 reshape.546
  315.2 1.9 convert_reduce_fusion.2
  323.1 1.8 concatenate.127
  325.9 1.7 pad_maximum_fusion.15.refs_0_
  327.7 3.4 convolution_convert_fusion.5
  338.4 1.6 pad_maximum_fusion.1.refs_1_
  341.2 132.8 %reduce.7 = (f32[40,128]{1,0:T(8,128)}, f32[2,48,384]{2,1,0:T(8,128)}, f32[2,48,384]{2,1,0:T(8,128)}, f32[2,48,768]{2,1,0:T(8,128)}, f32[2,48,768]{2,1,0:T(8,128...) custom-call(f32[4,2,2,40,256]{4,3,2,1,0:T(8,128)} %pad_maximum_fusion.15.refs_0_,, ...), custom_call_target="tpu_custom_call" | custom-call | tf_op jit(solution)/shard_map/reduce/pallas_call | solution.py:439
  476.2 2.2 broadcast_select_fusion.1
  488.7 2.4 pad_maximum_fusion
  (403 shorter events, 90.6 us)
Async XLA Ops:
  0.7 6.6 %copy-start = (bf16[5,8,128]{2,1,0:T(8,128)(2,1)S(1)}, bf16[5,8,128]{2,1,0:T(8,128)(2,1)}, u32[]{:S(2)}) copy-start(bf16[5,8,128]{2,1,0:T(8,128)(2,1)} %param.28) | copy-start | bytes 30724
  0.7 15.2 %copy-start.45 = (f32[48,1536]{1,0:T(8,128)S(1)}, f32[48,1536]{1,0:T(8,128)}, u32[]{:S(2)}) copy-start(f32[48,1536]{1,0:T(8,128)} %param.38) | copy-start | bytes 884740
  0.7 15.8 %copy-start.55 = (bf16[1440,768]{1,0:T(8,128)(2,1)S(1)}, bf16[1440,768]{1,0:T(8,128)(2,1)}, u32[]{:S(2)}) copy-start(bf16[1440,768]{1,0:T(8,128)(2,1)} %param.24) | copy-start | bytes 6635524
  5.4 147.5 %copy-start.75 = (pred[2,288]{1,0:T(4,128)(4,1)}, pred[2,288]{1,0:T(4,128)(4,1)S(1)}, u32[]{:S(2)}) copy-start(pred[2,288]{1,0:T(4,128)(4,1)S(1)} %iota_compare_fusion.1) | copy-start | bytes 1732
  17.5 105.4 %copy-start.68 = (bf16[144,768]{1,0:T(8,128)(2,1)}, bf16[144,768]{1,0:T(8,128)(2,1)S(1)}, u32[]{:S(2)}) copy-start(bf16[144,768]{1,0:T(8,128)(2,1)S(1)} %get-tuple-element.88) | copy-start | bytes 663556
  17.5 105.4 %copy-start.70 = (bf16[144,768]{1,0:T(8,128)(2,1)}, bf16[144,768]{1,0:T(8,128)(2,1)S(1)}, u32[]{:S(2)}) copy-start(bf16[144,768]{1,0:T(8,128)(2,1)S(1)} %get-tuple-element.89) | copy-start | bytes 663556
  108.7 8.9 %copy-start.38 = (bf16[1,4,2,2,48,768]{5,4,3,2,1,0:T(8,128)(2,1)}, bf16[1,4,2,2,48,768]{5,4,3,2,1,0:T(8,128)(2,1)S(1)}, u32[]{:S(2)}) copy-start(bf16[1,4,2,2,48,768]{5,4,3,2,1,0:T(8,128)(2,1)S(1)} %get-tuple-element.83) | copy-start | bytes 3538948
  108.7 10.9 %copy-start.21 = (bf16[1,4,2,2,48,768]{5,4,3,2,1,0:T(8,128)(2,1)}, bf16[1,4,2,2,48,768]{5,4,3,2,1,0:T(8,128)(2,1)S(1)}, u32[]{:S(2)}) copy-start(bf16[1,4,2,2,48,768]{5,4,3,2,1,0:T(8,128)(2,1)S(1)} %get-tuple-element.125) | copy-start | bytes 3538948
  112.5 87.6 %copy-start.93 = (f32[768]{0:T(1024)}, f32[768]{0:T(1024)S(1)}, u32[]{:S(2)}) copy-start(f32[768]{0:T(1024)S(1)} %mul.525) | copy-start | bytes 9220
  129.6 17.8 %copy-start.6 = (bf16[2,288,12,64]{1,3,2,0:T(8,128)(2,1)}, bf16[2,288,12,64]{1,3,2,0:T(8,128)(2,1)S(1)}, u32[]{:S(2)}) copy-start(bf16[2,288,12,64]{1,3,2,0:T(8,128)(2,1)S(1)} %copy.79) | copy-start | bytes 2654212
  154.4 13.5 %copy-start.57 = (f32[2,12,288]{2,1,0:T(8,128)}, f32[2,12,288]{2,1,0:T(8,128)S(1)}, u32[]{:S(2)}) copy-start(f32[2,12,288]{2,1,0:T(8,128)S(1)} %log_add_fusion) | copy-start | bytes 82948
  170.0 30.1 %slice-start.6 = ((s8[4718592]{0:T(1024)(128)(4,1)}), s8[4194304]{0:T(1024)(128)(4,1)S(1)}, s32[]{:S(2)}) async-start(s8[4718592]{0:T(1024)(128)(4,1)} %bitcast.340), calls=%async_computation.6 | async-start | bytes 8388608
  173.3 26.9 %copy-start.12 = (f32[720,768]{1,0:T(8,128)}, f32[720,768]{1,0:T(8,128)S(1)}, u32[]{:S(2)}) copy-start(f32[720,768]{1,0:T(8,128)S(1)} %get-tuple-element.109) | copy-start | bytes 6635524
  173.3 26.8 %copy-start.84 = (f32[720]{0:T(1024)}, f32[720]{0:T(1024)S(1)}, u32[]{:S(2)}) copy-start(f32[720]{0:T(1024)S(1)} %broadcast_multiply_fusion.1) | copy-start | bytes 8644
  174.1 26.1 %copy-start.95 = (f32[720]{0:T(1024)}, f32[720]{0:T(1024)S(1)}, u32[]{:S(2)}) copy-start(f32[720]{0:T(1024)S(1)} %fusion.57) | copy-start | bytes 8644
  174.1 26.1 %copy-start.109 = (f32[768]{0:T(1024)S(1)}, f32[768]{0:T(1024)}, u32[]{:S(2)}) copy-start(f32[768]{0:T(1024)} %add.354) | copy-start | bytes 9220
  174.1 26.1 %slice-start.7 = ((s8[4718592]{0:T(1024)(128)(4,1)}), s8[524288]{0:T(1024)(128)(4,1)S(1)}, s32[]{:S(2)}) async-start(s8[4718592]{0:T(1024)(128)(4,1)} %bitcast.340), calls=%async_computation.7 | async-start | bytes 1048576
  205.2 11.0 %copy-start.23 = (bf16[720,768]{1,0:T(8,128)(2,1)}, bf16[720,768]{1,0:T(8,128)(2,1)S(1)}, u32[]{:S(2)}) copy-start(bf16[720,768]{1,0:T(8,128)(2,1)S(1)} %add_convert_fusion.1.refs_5_) | copy-start | bytes 3317764
  205.5 10.7 %copy-start.80 = (bf16[3,768]{1,0:T(4,128)(2,1)}, bf16[3,768]{1,0:T(4,128)(2,1)S(1)}, u32[]{:S(2)}) copy-start(bf16[3,768]{1,0:T(4,128)(2,1)S(1)} %slice.200) | copy-start | bytes 13828
  216.3 13.1 %slice-start.4 = ((s8[4718592]{0:T(1024)(128)(4,1)}), s8[4194304]{0:T(1024)(128)(4,1)S(1)}, s32[]{:S(2)}) async-start(s8[4718592]{0:T(1024)(128)(4,1)} %bitcast.336), calls=%async_computation.4 | async-start | bytes 8388608
  217.2 12.2 %copy-start.13 = (f32[720,768]{1,0:T(8,128)S(1)}, f32[720,768]{1,0:T(8,128)}, u32[]{:S(2)}) copy-start(f32[720,768]{1,0:T(8,128)} %copy-done.12) | copy-start | bytes 6635524
  217.2 12.2 %copy-start.85 = (f32[720]{0:T(1024)S(1)}, f32[720]{0:T(1024)}, u32[]{:S(2)}) copy-start(f32[720]{0:T(1024)} %copy-done.84) | copy-start | bytes 8644
  217.2 12.2 %copy-start.94 = (f32[768]{0:T(1024)S(1)}, f32[768]{0:T(1024)}, u32[]{:S(2)}) copy-start(f32[768]{0:T(1024)} %copy-done.93) | copy-start | bytes 9220
  217.2 12.2 %copy-start.96 = (f32[720]{0:T(1024)S(1)}, f32[720]{0:T(1024)}, u32[]{:S(2)}) copy-start(f32[720]{0:T(1024)} %copy-done.95) | copy-start | bytes 8644
  217.2 12.2 %slice-start.5 = ((s8[4718592]{0:T(1024)(128)(4,1)}), s8[524288]{0:T(1024)(128)(4,1)S(1)}, s32[]{:S(2)}) async-start(s8[4718592]{0:T(1024)(128)(4,1)} %bitcast.336), calls=%async_computation.5 | async-start | bytes 1048576
  234.5 9.6 %copy-start.10 = (f32[720,768]{1,0:T(8,128)}, f32[720,768]{1,0:T(8,128)S(1)}, u32[]{:S(2)}) copy-start(f32[720,768]{1,0:T(8,128)S(1)} %get-tuple-element.75) | copy-start | bytes 6635524
  234.5 5.9 %copy-start.49 = (bf16[576,768]{0,1:T(8,128)(2,1)S(1)}, bf16[576,768]{0,1:T(8,128)(2,1)}, u32[]{:S(2)}) copy-start(bf16[576,768]{0,1:T(8,128)(2,1)} %copy-done.48) | copy-start | bytes 2654212
  234.5 5.9 %copy-start.115 = (bf16[12,64,144]{2,1,0:T(8,128)(2,1)S(1)}, bf16[12,64,144]{2,1,0:T(8,128)(2,1)}, u32[]{:S(2)}) copy-start(bf16[12,64,144]{2,1,0:T(8,128)(2,1)} %convolution_convert_fusion.11) | copy-start | bytes 663556
  244.0 11.9 %copy-start.26 = (bf16[720,768]{1,0:T(8,128)(2,1)}, bf16[720,768]{1,0:T(8,128)(2,1)S(1)}, u32[]{:S(2)}) copy-start(bf16[720,768]{1,0:T(8,128)(2,1)S(1)} %convolution_convert_fusion.9) | copy-start | bytes 3317764
  244.6 9.7 %copy-start.111 = (s32[16,2,4]{0,2,1:T(4,128)S(1)}, s32[16,2,4]{0,2,1:T(4,128)}, u32[]{:S(2)}) copy-start(s32[16,2,4]{0,2,1:T(4,128)} %multiply_add_fusion.6) | copy-start | bytes 1540
  244.6 9.7 %copy-start.113 = (f32[3,128]{1,0:T(4,128)S(1)}, f32[3,128]{1,0:T(4,128)}, u32[]{:S(2)}) copy-start(f32[3,128]{1,0:T(4,128)} %get-tuple-element.113) | copy-start | bytes 4612
  244.6 9.7 %copy-start.114 = (s32[24]{0:T(128)S(1)}, s32[24]{0:T(128)}, u32[]{:S(2)}) copy-start(s32[24]{0:T(128)} %eq.61) | copy-start | bytes 292
  257.1 5.8 %copy-start.34 = (bf16[144,768]{0,1:T(8,128)(2,1)}, bf16[144,768]{0,1:T(8,128)(2,1)S(1)}, u32[]{:S(2)}) copy-start(bf16[144,768]{0,1:T(8,128)(2,1)S(1)} %copy.94) | copy-start | bytes 663556
  269.2 7.0 %copy-start.20 = (bf16[2,288,12,64]{1,3,2,0:T(8,128)(2,1)}, bf16[2,288,12,64]{1,3,2,0:T(8,128)(2,1)S(1)}, u32[]{:S(2)}) copy-start(bf16[2,288,12,64]{1,3,2,0:T(8,128)(2,1)S(1)} %copy.89) | copy-start | bytes 2654212
  281.6 6.1 %copy-start.14 = (bf16[576,768]{0,1:T(8,128)(2,1)}, bf16[576,768]{0,1:T(8,128)(2,1)S(1)}, u32[]{:S(2)}) copy-start(bf16[576,768]{0,1:T(8,128)(2,1)S(1)} %reshape.543) | copy-start | bytes 2654212
  284.4 5.0 %copy-start.4 = (f32[12,144,288]{2,1,0:T(8,128)S(1)}, f32[12,144,288]{2,1,0:T(8,128)}, u32[]{:S(2)}) copy-start(f32[12,144,288]{2,1,0:T(8,128)} %copy-done.3) | copy-start | bytes 5971972
  284.4 5.0 %copy-start.30 = (bf16[288,768]{0,1:T(8,128)(2,1)S(1)}, bf16[288,768]{0,1:T(8,128)(2,1)}, u32[]{:S(2)}) copy-start(bf16[288,768]{0,1:T(8,128)(2,1)} %copy.83) | copy-start | bytes 1327108
  287.8 7.2 %slice-start = ((s8[10616832]{0:T(1024)(128)(4,1)}), s8[4194304]{0:T(1024)(128)(4,1)S(1)}, s32[]{:S(2)}) async-start(s8[10616832]{0:T(1024)(128)(4,1)} %bitcast.287), calls=%async_computation | async-start | bytes 8388608
  289.5 5.5 %slice-start.1 = ((s8[10616832]{0:T(1024)(128)(4,1)}), s8[4194304]{0:T(1024)(128)(4,1)S(1)}, s32[]{:S(2)}) async-start(s8[10616832]{0:T(1024)(128)(4,1)} %bitcast.287), calls=%async_computation.1 | async-start | bytes 8388608
  290.7 4.3 slice-start.2
  313.1 9.1 %copy-start.79 = (f32[1,16,2,24]{3,2,1,0:T(2,128)S(1)}, f32[1,16,2,24]{3,2,1,0:T(2,128)}, u32[]{:S(2)}) copy-start(f32[1,16,2,24]{3,2,1,0:T(2,128)} %concatenate.125) | copy-start | bytes 9220
  315.2 10.8 %copy-start.36 = (f32[4,2,2,24,256]{4,3,2,1,0:T(8,128)S(1)}, f32[4,2,2,24,256]{4,3,2,1,0:T(8,128)}, u32[]{:S(2)}) copy-start(f32[4,2,2,24,256]{4,3,2,1,0:T(8,128)} %concatenate.113) | copy-start | bytes 1179652
  315.2 12.5 %copy-start.52 = (bf16[576,768]{1,0:T(8,128)(2,1)S(1)}, bf16[576,768]{1,0:T(8,128)(2,1)}, u32[]{:S(2)}) copy-start(bf16[576,768]{1,0:T(8,128)(2,1)} %get-tuple-element.128) | copy-start | bytes 2654212
  335.2 4.9 copy-start.25
  341.2 134.8 %copy-start.83 = (f32[768]{0:T(1024)S(1)}, f32[768]{0:T(1024)}, u32[]{:S(2)}) copy-start(f32[768]{0:T(1024)} %add.358) | copy-start | bytes 9220
  476.1 4.2 copy-start.73
  476.1 4.2 copy-start.59
  476.1 4.2 copy-start.77
  (79 other events, 188.7 us)

commit v2 on v1

--- a/solution.py
+++ b/solution.py
@@ -107,149 +107,423 @@
     return pl.ds(pl.multiple_of(x * half, 128), half)
 
 
-def gather_kernel(n_in, n_out, index, *refs):
-    ins, outs = refs[:n_in], refs[n_in : n_in + n_out]
-    lsem, zs, zr, s1, r1, s2, r2, ds, dr = refs[n_in + n_out :]
-    me = Place()
-    greet(me.others())
-    n = len(index)
-    pieces = []
-    for i, li, o, lo in index:
-        src = ins[i] if li is None else ins[i].at[li]
-        dst = outs[o] if lo is None else outs[o].at[lo]
-        pieces.append((src, dst, dst.shape[-1] // 2))
-
-    waits = []
-
-    def go(copy):
+def dma(*shape):
+    return pltpu.SemaphoreType.DMA(shape)
+
+
+def mm(a, b):
+    return jnp.dot(a, b, preferred_element_type=F32)
+
+
+def mm_nt(a, b):
+    return lax.dot_general(a, b, (((1,), (1,)), ((), ())), preferred_element_type=F32)
+
+
+def mm_tn(a, b):
+    return lax.dot_general(a, b, (((0,), (0,)), ((), ())), preferred_element_type=F32)
+
+
+def flat(value):
+    return value.reshape(-1, value.shape[-1])
+
+
+def lanes(i, n=128):
+    return pl.ds(pl.multiple_of(i * n, 128), n)
+
+
+def rows_at(i, n, at=0):
+    return pl.ds(pl.multiple_of(at + i * n, 16), n)
+
+
+def each(n, body):
+    lax.fori_loop(0, n, lambda i, c: (body(i), c)[1], 0)
+
+
+class Gather:
+    def __init__(self, me, pieces, sems):
+        self.me, self.pieces = me, pieces
+        self.lsem, self.zs, self.zr, self.s1, self.r1, self.s2, self.r2, self.ds, self.dr = sems
+        self.waits, self.locs = [], {}
+
+    def go(self, copy):
         copy.start()
-        waits.append(copy)
-        return copy
-
-    def step1(p):
-        src, dst, half = pieces[p]
-        blk = dst.at[me.z, me.y, me.c, :, cols(me.x, half)]
-        loc = pltpu.make_async_copy(src, blk, lsem.at[p])
+        self.waits.append(copy)
+
+    def step1(self, p):
+        me = self.me
+        src, dst = self.pieces[p]
+        blk = dst.at[me.z, me.y, me.c, :, cols(me.x, dst.shape[-1] // 2)]
+        loc = pltpu.make_async_copy(src, blk, self.lsem.at[p])
         loc.start()
+        self.locs[p] = loc
         for k in range(1, NZ):
-            go(remote(src, blk, zs.at[p, k], zr.at[p, k], me.dev(z=lax.rem(me.z + k, NZ))))
-        return loc
-
-    def part(p, stage):
-        _, dst, half = pieces[p]
+            dev = me.dev(z=lax.rem(me.z + k, NZ))
+            self.go(remote(src, blk, self.zs.at[p, k], self.zr.at[p, k], dev))
+
+    def part(self, p, stage, c):
+        me, dst = self.me, self.pieces[p][1]
+        half = dst.shape[-1] // 2
         own, other = cols(me.x, half), cols(1 - me.x, half)
         if stage == "z":
-            return dst.at[:, me.y, me.c, :, own]
+            return dst.at[:, me.y, c, :, own]
         if p % 2 == 0:
             if stage == "in1":
-                return dst.at[:, me.y, me.c, :, other]
+                return dst.at[:, me.y, c, :, other]
             if stage == "out2":
-                return dst.at[:, me.y, me.c]
-            return dst.at[:, 1 - me.y, me.c]
+                return dst.at[:, me.y, c]
+            return dst.at[:, 1 - me.y, c]
         if stage == "in1":
-            return dst.at[:, 1 - me.y, me.c, :, own]
+            return dst.at[:, 1 - me.y, c, :, own]
         if stage == "out2":
-            return dst.at[:, :, me.c, :, own]
-        return dst.at[:, :, me.c, :, other]
-
-    def cross(p, stage, ref, which):
-        dev = me.dev(c=1 - me.c)
-        go(remote(ref, ref, ds.at[p, which], dr.at[p, which], dev))
-
-    def step2(p, loc):
-        src, dst, half = pieces[p]
-        loc.wait()
+            return dst.at[:, :, c, :, own]
+        return dst.at[:, :, c, :, other]
+
+    def first(self, p):
+        return self.me.dev(x=1 - self.me.x) if p % 2 == 0 else self.me.dev(y=1 - self.me.y)
+
+    def second(self, p):
+        return self.me.dev(y=1 - self.me.y) if p % 2 == 0 else self.me.dev(x=1 - self.me.x)
+
+    def cross(self, p, ref, which):
+        self.go(remote(ref, ref, self.ds.at[p, which], self.dr.at[p, which], self.me.dev(c=1 - self.me.c)))
+
+    def arrived(self, ref, ssem, rsem):
+        remote(ref, ref, ssem, rsem, self.me.dev(c=1 - self.me.c)).wait_recv()
+
+    def step2(self, p):
+        me, dst = self.me, self.pieces[p][1]
+        self.locs[p].wait()
         for k in range(1, NZ):
-            blk = dst.at[lax.rem(me.z + NZ - k, NZ), me.y, me.c, :, cols(me.x, half)]
-            remote(blk, blk, zs.at[p, k], zr.at[p, k], me.dev()).wait_recv()
-        have = part(p, "z")
-        dev = me.dev(x=1 - me.x) if p % 2 == 0 else me.dev(y=1 - me.y)
-        go(remote(have, have, s1.at[p], r1.at[p], dev))
-        cross(p, "z", have, 0)
-
-    def step3(p):
-        got = part(p, "in1")
-        remote(got, got, s1.at[p], r1.at[p], me.dev()).wait_recv()
-        have = part(p, "out2")
-        dev = me.dev(y=1 - me.y) if p % 2 == 0 else me.dev(x=1 - me.x)
-        go(remote(have, have, s2.at[p], r2.at[p], dev))
-        cross(p, "in1", got, 1)
-
-    def step4(p):
-        got = part(p, "in2")
-        remote(got, got, s2.at[p], r2.at[p], me.dev()).wait_recv()
-        cross(p, "in2", got, 2)
-
-    def step5(p):
-        _, dst, half = pieces[p]
-        own, other = cols(me.x, half), cols(1 - me.x, half)
-        oc = 1 - me.c
-        got = [dst.at[:, me.y, oc, :, own]]
-        if p % 2 == 0:
-            got += [dst.at[:, me.y, oc, :, other], dst.at[:, 1 - me.y, oc]]
-        else:
-            got += [dst.at[:, 1 - me.y, oc, :, own], dst.at[:, :, oc, :, other]]
-        for which, ref in enumerate(got):
-            remote(ref, ref, ds.at[p, which], dr.at[p, which], me.dev()).wait_recv()
-
-    locs = {}
-    ahead = 2
-    for p in range(min(ahead, n)):
-        locs[p] = step1(p)
-    for t in range(n + 3):
+            blk = dst.at[lax.rem(me.z + NZ - k, NZ), me.y, me.c, :, cols(me.x, dst.shape[-1] // 2)]
+            self.arrived(blk, self.zs.at[p, k], self.zr.at[p, k])
+        have = self.part(p, "z", me.c)
+        self.go(remote(have, have, self.s1.at[p], self.r1.at[p], self.first(p)))
+        self.cross(p, have, 0)
+
+    def step3(self, p):
+        got = self.part(p, "in1", self.me.c)
+        self.arrived(got, self.s1.at[p], self.r1.at[p])
+        have = self.part(p, "out2", self.me.c)
+        self.go(remote(have, have, self.s2.at[p], self.r2.at[p], self.second(p)))
+        self.cross(p, got, 1)
+
+    def step4(self, p):
+        got = self.part(p, "in2", self.me.c)
+        self.arrived(got, self.s2.at[p], self.r2.at[p])
+        self.cross(p, got, 2)
+
+    def step5(self, p):
+        for which, stage in enumerate(("z", "in1", "in2")):
+            self.arrived(self.part(p, stage, 1 - self.me.c), self.ds.at[p, which], self.dr.at[p, which])
+
+    def tick(self, t, ahead):
+        n = len(self.pieces)
         if t < n:
-            step2(t, locs[t])
+            self.step2(t)
             if t + ahead < n:
-                locs[t + ahead] = step1(t + ahead)
+                self.step1(t + ahead)
         if 0 <= t - 1 < n:
-            step3(t - 1)
+            self.step3(t - 1)
         if 0 <= t - 2 < n:
-            step4(t - 2)
+            self.step4(t - 2)
         if 0 <= t - 3 < n:
-            step5(t - 3)
-    for copy in waits:
-        copy.wait_send()
-
-
-def dma(*shape):
-    return pltpu.SemaphoreType.DMA(shape)
-
-
-def gather_fast(shards, small, rows):
-    qk, va, inner, outer = shards
-    width = 2 * qk.shape[2]
-    ffw = 2 * inner.shape[2]
+            self.step5(t - 3)
+
+    def end(self):
+        for copy in self.waits:
+            copy.wait_send()
+
+
+def norm_rows(z_ref, r_ref, n_rows, put):
+    step = 48
+
+    def body(i):
+        at = rows_at(i, step)
+        z = z_ref[at, :]
+        centred = z - jnp.mean(z, axis=-1, keepdims=True)
+        spread = jnp.mean(centred * centred, axis=-1, keepdims=True)
+        root = lax.rsqrt(spread + ln_epsilon)
+        hat = centred * root
+        z_ref[at, :] = hat
+        r_ref[at, :] = jnp.broadcast_to(root, (step, 128))
+        put(at, hat)
+
+    each(n_rows // step, body)
+
+
+def forward_kernel(*refs):
+    (lens, tokens, w_qkv, w_attn, w_inner, w_outer, w_proj, vectors) = refs[:8]
+    outs = refs[8:28]
+    scr = refs[28:]
+    (small_s, qk_s, va_s, inner_s, outer_s, small_g, qk, va, inner, outer) = scr[:10]
+    (x_all, q, k, v, p_ab, p_c, o, xh1, r1, g, gp, xh2, r2, out_own, proj, vec, h1b, vecp, bias_ff) = scr[10:29]
+    gsems, tsem, osem = scr[29:38], scr[38], scr[39]
+    me = Place()
+    mp = me.x
+    n_all, width = x_all.shape
+    n_own = q.shape[0]
+    seq = p_ab.shape[1]
+    half_seq = seq // 2
+    full = (n_own - half_seq) // seq
+    n_full = full * seq
+    half_ff = inner.shape[-1]
+    rows = qk_s.shape[1]
+    half_rows = rows // 2
+
+    starts = (
+        (mp * (n_full + seq), 0, n_full),
+        (n_full + mp * half_seq, n_full, half_seq),
+        (n_full + (1 - mp) * half_seq, n_own, half_seq),
+    )
+    loads = []
+    for i, (at, to, n) in enumerate(starts):
+        cp = pltpu.make_async_copy(
+            tokens.at[pl.ds(pl.multiple_of(at, 16), n)], x_all.at[pl.ds(to, n)], tsem.at[i]
+        )
+        cp.start()
+        loads.append(cp)
+
+    vecp[...] = jnp.zeros_like(vecp)
+    nvec, nlane = vectors.shape
+    vecp[0:nvec, 0:nlane] = vectors[...]
+    small_s[0:half_rows] = w_proj[pl.ds(pl.multiple_of(mp * half_rows, 8), half_rows), :]
+    small_s[half_rows : half_rows + nlane] = jnp.transpose(vecp[...])[0:nlane]
+    qk_s[...] = w_qkv[0:2].astype(BF)
+    va_s[0] = w_qkv[2].astype(BF)
+    va_s[1] = w_attn[...].astype(BF)
+    hf = half_ff // 2
+    for h in range(2):
+        inner_s[h] = w_inner[:, h * hf : (h + 1) * hf].astype(BF)
+        outer_s[h] = w_outer[:, h * hf : (h + 1) * hf].astype(BF)
+
+    greet(me.others())
+    pieces = [
+        (small_s, small_g),
+        (qk_s.at[0], qk.at[0]),
+        (qk_s.at[1], qk.at[1]),
+        (va_s.at[0], va.at[0]),
+        (va_s.at[1], va.at[1]),
+        (inner_s.at[0], inner.at[0]),
+        (inner_s.at[1], inner.at[1]),
+        (outer_s.at[0], outer.at[0]),
+        (outer_s.at[1], outer.at[1]),
+    ]
+    net = Gather(me, pieces, gsems)
+    ahead = 3
+    for p in range(ahead):
+        net.step1(p)
+    tick = lambda t: net.tick(t, ahead)
+    saves = []
+
+    def save(i, ref):
+        cp = pltpu.make_async_copy(ref, outs[i], osem.at[i])
+        cp.start()
+        saves.append(cp)
+
+    for cp in loads:
+        cp.wait()
+    save(4, x_all)
+    for t in range(4):
+        tick(t)
+    big = []
+    for z in range(NZ):
+        for y in range(NY):
+            for c in range(NC):
+                for x in range(NX):
+                    blk = small_g[z, y, c, :, x * 128 : (x + 1) * 128]
+                    d = ((z * NY + y) * NC + c) * NX + x
+                    proj[d * half_rows : (d + 1) * half_rows] = blk[:half_rows]
+                    big.append(blk[half_rows : half_rows + nlane])
+    vec[...] = jnp.transpose(jnp.concatenate(big, axis=0))[0 : vec.shape[0]]
+    for h in range(2):
+        for x in range(NX):
+            bias_ff[h : h + 1, x * width : (x + 1) * width] = vec[5 + NX * x + h : 6 + NX * x + h, :]
+    save(17, proj)
+    save(18, vec)
+
+    def project(w_ref, src_rows, dst, bias):
+        n_tile = 256
+
+        def body(i):
+            w = flat(w_ref[:, :, :, :, lanes(i, n_tile)])
+            r = mm(x_all[0:src_rows], w)
+            if bias is not None:
+                r = r + vec[bias : bias + 1, lanes(i, n_tile)]
+            dst[:, lanes(i, n_tile)] = r.astype(BF)
+
+        each(width // n_tile, body)
+
+    tick(4)
+    project(qk.at[0], n_own, q, 0)
+    tick(5)
+    project(qk.at[1], n_all, k, None)
+    save(0, qk)
+    tick(6)
+    project(va.at[0], n_all, v, 1)
+    save(5, q)
+    save(6, k)
+    save(7, v)
+
+    lane = lax.broadcasted_iota(jnp.int32, (1, 128), 1)
+    head_lo = jnp.where(lane < HEAD_DIM, 1.0, 0.0)
+    head_mask = (head_lo.astype(BF), (1.0 - head_lo).astype(BF))
+    pos = lax.broadcasted_iota(jnp.int32, (1, seq), 1)
+
+    def attend(q0, nq, k0, hp, length, place, p_ref, p_at):
+        qp = q[pl.ds(pl.multiple_of(q0, 16), nq), lanes(hp)]
+        kp = k[pl.ds(pl.multiple_of(k0, 16), seq), lanes(hp)]
+        vp = v[pl.ds(pl.multiple_of(k0, 16), seq), lanes(hp)]
+        got = []
+        for h in range(2):
+            s = mm_nt(qp * head_mask[h], kp) * (HEAD_DIM**-0.5)
+            s = jnp.where(place < length, s, -1000000000.0)
+            e = jnp.exp(s - jnp.max(s, axis=-1, keepdims=True))
+            pb = (e * (1.0 / jnp.sum(e, axis=-1, keepdims=True))).astype(BF)
+            p_ref[p_at + h] = pb
+            got.append(mm(pb, vp))
+        mixed = jnp.where(lane < HEAD_DIM, got[0], got[1])
+        o[pl.ds(pl.multiple_of(q0, 16), nq), lanes(hp)] = mixed.astype(BF)
+
+    pairs = width // 128
+    for s in range(full):
+        length = lens[mp * (full + 1) + s]
+        each(pairs, lambda hp: attend(s * seq, seq, s * seq, hp, length, pos, p_ab, s * 2 * pairs + 2 * hp))
+        tick(7 + s)
+    length = lens[full]
+    pos_c = jnp.where(pos < half_seq, pos + mp * half_seq, pos - half_seq + (1 - mp) * half_seq)
+    each(pairs, lambda hp: attend(n_full, half_seq, n_full, hp, length, pos_c, p_c, 2 * hp))
+    save(8, p_ab)
+    save(9, p_c)
+    save(10, o)
+    tick(7 + full)
+
+    tile = 240
+    tiles = n_own // tile
+
+    def attn_out(i):
+        a = mm_nt(o[rows_at(i, tile), :], flat(va[1]))
+        xh1[rows_at(i, tile), :] = x_all[rows_at(i, tile), :].astype(F32) + a + vec[2:3, :]
+
+    each(tiles, attn_out)
+    save(1, va)
+
+    def put_h1(at, hat):
+        h1b[at, :] = (hat * vec[3:4, :] + vec[4:5, :]).astype(BF)
+
+    norm_rows(xh1, r1, n_own, put_h1)
+    save(11, xh1)
+    save(12, r1)
+    tick(8 + full)
+
+    def feed(h):
+        n_tile = 256
+
+        def body(i):
+            w = flat(inner[h, :, :, :, :, lanes(i, n_tile)])
+            for t in range(tiles):
+                at = pl.ds(t * tile, tile)
+                u = mm(h1b[at, :], w)
+                u = u + bias_ff[h : h + 1, lanes(i, n_tile)]
+                tail = 0.5 * (1.0 + lax.erf(u * 0.7071067811865476))
+                g[h, at, lanes(i, n_tile)] = (u * tail).astype(BF)
+                slope = tail + u * (0.3989422804014327 * jnp.exp(-0.5 * u * u))
+                gp[h, at, lanes(i, n_tile)] = slope.astype(BF)
+
+        each(half_ff // n_tile, body)
+
+    feed(0)
+    tick(9 + full)
+    feed(1)
+    for t in range(10 + full, len(pieces) + 3):
+        tick(t)
+    save(2, inner)
+    save(13, g)
+    save(14, gp)
+
+    def ff_out(i):
+        at = rows_at(i, tile)
+        f = mm_nt(g[0, at, :], flat(outer[0])) + mm_nt(g[1, at, :], flat(outer[1]))
+        h1 = xh1[at, :] * vec[3:4, :] + vec[4:5, :]
+        xh2[at, :] = h1 + f + vec[9:10, :]
+
+    each(tiles, ff_out)
+    save(3, outer)
+
+    def put_y(at, hat):
+        out_own[at, :] = (hat * vec[10:11, :] + vec[11:12, :]).astype(BF)
+
+    norm_rows(xh2, r2, n_own, put_y)
+    save(15, xh2)
+    save(16, r2)
+    save(19, out_own)
+    net.end()
+    for cp in saves:
+        cp.wait()
+
+
+def forward_fast(lengths, tokens, w_qkv, w_attn, w_inner, w_outer, w_proj, vectors):
+    seqs = lengths.shape[0]
+    all_rows, width = tokens.shape
+    seq = all_rows // seqs
+    full = seqs // 2
+    n_own = full * seq + seq // 2
+    n_all = n_own + seq // 2
+    rows, half_ff = w_qkv.shape[1], w_inner.shape[1]
+    heads = width // HEAD_DIM
     zyc = (NZ, NY, NC)
-    index = [
-        (1, 0, 1, 0),
-        (2, 0, 2, 0),
-        (1, 1, 1, 1),
-        (2, 1, 2, 1),
-        (3, 0, 3, 0),
-        (3, 1, 3, 1),
-        (4, 0, 4, 0),
-        (4, 1, 4, 1),
-        (0, None, 0, None),
+    small_rows = rows // 2 + vectors.shape[1]
+    weights = [
+        ((2,) + zyc + (rows, width), BF),
+        ((2,) + zyc + (rows, width), BF),
+        ((2,) + zyc + (rows, half_ff), BF),
+        ((2,) + zyc + (rows, half_ff), BF),
     ]
-    n = len(index)
-    outs = pl.pallas_call(
-        functools.partial(gather_kernel, 5, 5, index),
-        out_shape=[
-            jax.ShapeDtypeStruct(zyc + (small.shape[0], 2 * small.shape[1]), F32),
-            jax.ShapeDtypeStruct((2,) + zyc + (rows, width), BF),
-            jax.ShapeDtypeStruct((2,) + zyc + (rows, width), BF),
-            jax.ShapeDtypeStruct((2,) + zyc + (rows, ffw), BF),
-            jax.ShapeDtypeStruct((2,) + zyc + (rows, ffw), BF),
+    kept = [
+        ((n_all, width), BF),
+        ((n_own, width), BF),
+        ((n_all, width), BF),
+        ((n_all, width), BF),
+        ((full * heads, seq, seq), BF),
+        ((heads, seq // 2, seq), BF),
+        ((n_own, width), BF),
+        ((n_own, width), F32),
+        ((n_own, 128), F32),
+        ((2, n_own, half_ff), BF),
+        ((2, n_own, half_ff), BF),
+        ((n_own, width), F32),
+        ((n_own, 128), F32),
+        ((width, 128), F32),
+        ((16, width), F32),
+        ((n_own, width), BF),
+    ]
+    order = kept[:13] + [kept[15], kept[13], kept[14]]
+    scratch = [
+        ((small_rows, 128), F32),
+        ((2, rows, width // 2), BF),
+        ((2, rows, width // 2), BF),
+        ((2, rows, half_ff // 2), BF),
+        ((2, rows, half_ff // 2), BF),
+        (zyc + (small_rows, 256), F32),
+    ] + weights + order + [((n_own, width), BF), ((128, 128), F32), ((8, half_ff), F32)]
+    n = 9
+    vm = pl.BlockSpec(memory_space=pltpu.VMEM)
+    hb = pl.BlockSpec(memory_space=ANY)
+    sm = pl.BlockSpec(memory_space=pltpu.SMEM)
+    return pl.pallas_call(
+        forward_kernel,
+        out_shape=[jax.ShapeDtypeStruct(s, d) for s, d in weights + kept],
+        in_specs=[sm, hb] + [vm] * 6,
+        out_specs=[hb] * 20,
+        scratch_shapes=[pltpu.VMEM(s, d) for s, d in scratch]
+        + [
+            dma(n), dma(n, NZ), dma(n, NZ), dma(n), dma(n), dma(n), dma(n), dma(n, 3), dma(n, 3),
+            dma(3), dma(20),
         ],
-        in_specs=[pl.BlockSpec(memory_space=ANY)] * 5,
-        out_specs=[pl.BlockSpec(memory_space=ANY)] * 5,
-        scratch_shapes=[
-            dma(n), dma(n, NZ), dma(n, NZ), dma(n), dma(n), dma(n), dma(n), dma(n, 3), dma(n, 3),
-        ],
-        compiler_params=pltpu.CompilerParams(collective_id=1, has_side_effects=True),
-        name="gather",
-    )(small, qk, va, inner, outer)
-    return outs
+        compiler_params=pltpu.CompilerParams(
+            collective_id=1, has_side_effects=True, vmem_limit_bytes=60 * 2**20
+        ),
+        name="forward",
+    )(lengths, tokens, w_qkv, w_attn, w_inner, w_outer, w_proj, vectors)
 
 
 def reduce_kernel(n_in, n_out, index, *refs):
@@ -479,6 +753,96 @@
     return [small_sum] + sums + [peer_out, peer_dx, peer_small, jnp.full((8, 128), total)]
 
 
+def forward_plain(lengths, tokens, w_qkv, w_attn, w_inner, w_outer, w_proj, vectors):
+    mp = lax.axis_index("mp")
+    n_dp = lax.axis_size("dp")
+    seqs = lengths.shape[0]
+    all_rows, width = tokens.shape
+    seq_len = all_rows // seqs
+    full = seqs // 2
+    n_full, n_half = full * seq_len, seq_len // 2
+    n_own = n_full + n_half
+    heads = width // HEAD_DIM
+    rows, half_ff = w_qkv.shape[1], w_inner.shape[1]
+    nvec, vec_lanes = vectors.shape
+    half_rows = rows // 2
+    score_scale = HEAD_DIM ** (-0.5)
+
+    def two(v):
+        return v.reshape(rows, 2, half_ff // 2).transpose(1, 0, 2)
+
+    qk_s = w_qkv[:2].astype(BF)
+    va_s = jnp.stack([w_qkv[2], w_attn]).astype(BF)
+    vec_pad = jnp.pad(vectors, ((0, 0), (0, 128 - vec_lanes)))
+    proj_half = lax.dynamic_slice_in_dim(w_proj, mp * half_rows, half_rows, 0)
+    small_s = jnp.concatenate([proj_half, vec_pad], axis=0)
+    small_g, qk, va, inner, outer = gather_plain(
+        [qk_s, va_s, two(w_inner.astype(BF)), two(w_outer.astype(BF))], small_s, rows
+    )
+    small_g = small_g.reshape(n_dp, half_rows + nvec, 2, 128)
+    proj = small_g[:, :half_rows].transpose(0, 2, 1, 3).reshape(width, 128)
+    vec = small_g[:, half_rows:, :, :vec_lanes].transpose(1, 0, 2, 3).reshape(nvec, width)
+    ff_rows = nvec - 8
+    b_inner = vec[5 : 5 + ff_rows].reshape(2, 2, half_ff // 2).transpose(1, 0, 2).reshape(2, half_ff)
+
+    a0 = mp * (n_full + seq_len)
+    h0 = n_full + mp * n_half
+    o0 = n_full + (1 - mp) * n_half
+    x_all = jnp.concatenate(
+        [
+            lax.dynamic_slice_in_dim(tokens, a0, n_full, 0),
+            lax.dynamic_slice_in_dim(tokens, h0, n_half, 0),
+            lax.dynamic_slice_in_dim(tokens, o0, n_half, 0),
+        ]
+    )
+    x_own = x_all[:n_own]
+    my_seqs = jnp.concatenate([mp * (full + 1) + jnp.arange(full), jnp.array([full])])
+    my_len = lengths[my_seqs]
+    pos = jnp.arange(seq_len)
+    pos_last = jnp.where(pos < n_half, pos + mp * n_half, pos - n_half + (1 - mp) * n_half)
+    valids = (pos[None, :] < my_len[:full, None], pos_last[None, :] < my_len[full:, None])
+
+    q = (jnp.dot(x_own, qk[0], preferred_element_type=F32) + vec[0]).astype(BF)
+    k = jnp.dot(x_all, qk[1], preferred_element_type=F32).astype(BF)
+    v = (jnp.dot(x_all, va[0], preferred_element_type=F32) + vec[1]).astype(BF)
+    probs, outs = [], []
+    for qh, kh, vh, valid in zip(*(halves(t, n_full, seq_len) for t in (q, k, v)), valids):
+        s = jnp.einsum("gqhe,gkhe->ghqk", qh, kh, preferred_element_type=F32) * score_scale
+        s = jnp.where(valid[:, None, None, :], s, -1000000000.0)
+        pb = jax.nn.softmax(s, axis=-1).astype(BF)
+        o = jnp.einsum("ghqk,gkhe->gqhe", pb, vh, preferred_element_type=F32)
+        outs.append(o.reshape(-1, width).astype(BF))
+        probs.append(pb.reshape((-1,) + pb.shape[2:]))
+    mixed = jnp.concatenate(outs)
+
+    def norm(z):
+        centred = z - jnp.mean(z, axis=-1, keepdims=True)
+        root = lax.rsqrt(jnp.mean(centred * centred, axis=-1, keepdims=True) + ln_epsilon)
+        return centred * root, jnp.broadcast_to(root, (n_own, 128))
+
+    attn = jnp.einsum("te,de->td", mixed, va[1], preferred_element_type=F32)
+    xh1, r1 = norm(x_own.astype(F32) + attn + vec[2])
+    h1 = xh1 * vec[3] + vec[4]
+    u = jnp.einsum("td,hdf->htf", h1.astype(BF), inner, preferred_element_type=F32) + b_inner[:, None, :]
+    tail = 0.5 * (1.0 + lax.erf(u * 0.7071067811865476))
+    g = (u * tail).astype(BF)
+    gp = (tail + u * (0.3989422804014327 * jnp.exp(-0.5 * u * u))).astype(BF)
+    f = jnp.einsum("htf,hdf->td", g, outer, preferred_element_type=F32)
+    xh2, r2 = norm(h1 + f + vec[5 + ff_rows])
+    out_own = (xh2 * vec[6 + ff_rows] + vec[7 + ff_rows]).astype(BF)
+    vec = jnp.pad(vec, ((0, 16 - nvec), (0, 0)))
+    return [qk, va, inner, outer, x_all, q, k, v, *probs, mixed, xh1, r1, g, gp, xh2, r2, proj, vec, out_own]
+
+
+def halves(t, n_full, seq_len):
+    heads = t.shape[1] // HEAD_DIM
+    last = t.shape[0] - n_full
+    return (
+        t[:n_full].reshape(n_full // seq_len, seq_len, heads, HEAD_DIM),
+        t[n_full:].reshape(1, last, heads, HEAD_DIM),
+    )
+
+
 def local(
     tokens, cotangent, lengths, doc_ids, doc_rows,
     w_qkv, m_qkv, v_qkv, w_attn, m_attn, v_attn, w_inner, m_inner, v_inner,
@@ -493,98 +857,27 @@
     full = seqs // 2
     n_full, n_half = full * seq_len, seq_len // 2
     n_own = n_full + n_half
-    heads = width // HEAD_DIM
-    rows = w_qkv.shape[1]
-    half_w, half_ff = w_qkv.shape[2], w_inner.shape[1]
-    ff = 2 * half_ff
+    rows, half_ff = w_qkv.shape[1], w_inner.shape[1]
+    half_rows = rows // 2
+    nvec, vec_lanes = vectors.shape
+    ff_rows = nvec - 8
     score_scale = HEAD_DIM ** (-0.5)
 
-    def two(v):
-        return v.reshape(rows, 2, half_ff // 2).transpose(1, 0, 2)
-
-    qk_s = w_qkv[:2].astype(BF)
-    va_s = jnp.stack([w_qkv[2], w_attn]).astype(BF)
-    inner_s = two(w_inner.astype(BF))
-    outer_s = two(w_outer.astype(BF))
-    vec_pad = jnp.pad(vectors, ((0, 16 - vectors.shape[0]), (0, 128 - vectors.shape[1])))
-    half_rows = rows // 2
-    proj_half = lax.dynamic_slice_in_dim(w_proj, mp * half_rows, half_rows, 0)
-    small_s = jnp.concatenate([proj_half, vec_pad], axis=0)
-    gather = gather_fast if fast else gather_plain
-    small_g, qk, va, inner, outer = gather([qk_s, va_s, inner_s, outer_s], small_s, rows)
-    small_g = small_g.reshape(n_dp, half_rows + 16, 2, 128)
-    proj = small_g[:, :half_rows].transpose(0, 2, 1, 3).reshape(width, 128).astype(BF)
-    nvec, vec_lanes = vectors.shape
-    vec = small_g[:, half_rows : half_rows + nvec, :, :vec_lanes].transpose(1, 0, 2, 3).reshape(nvec, width)
+    forward = forward_fast if fast else forward_plain
+    saved = forward(lengths, tokens, w_qkv, w_attn, w_inner, w_outer, w_proj, vectors)
+    (qk, va, inner, outer, x_all, q, k, v, p_ab, p_c, mixed, xh1, r1, act_low, slope, xh2, r2, proj, vec, out_own) = saved
     qk = qk.reshape(2, width, width)
     va = va.reshape(2, width, width)
     inner = inner.reshape(2, width, half_ff)
     outer = outer.reshape(2, width, half_ff)
-    ff_rows = nvec - 8
-    b_inner = (
-        vec[5 : 5 + ff_rows].reshape(2, 2, half_ff // 2).transpose(1, 0, 2).reshape(2, half_ff)
-    )
-    bias_attn, gain_one, shift_one = vec[2], vec[3], vec[4]
-    bias_outer, gain_two, shift_two = vec[5 + ff_rows], vec[6 + ff_rows], vec[7 + ff_rows]
-
-    a0 = mp * n_own + mp * 0
+    x_own = x_all[:n_own]
+    proj = proj.astype(BF)
     a0 = mp * (n_full + seq_len)
     h0 = n_full + mp * n_half
-    o0 = n_full + (1 - mp) * n_half
-
-    def own_rows(v):
-        return jnp.concatenate(
-            [lax.dynamic_slice_in_dim(v, a0, n_full, 0), lax.dynamic_slice_in_dim(v, h0, n_half, 0)]
-        )
-
-    x_own = own_rows(tokens)
-    x_all = jnp.concatenate([x_own, lax.dynamic_slice_in_dim(tokens, o0, n_half, 0)])
-    cot = own_rows(cotangent)
+    cot = jnp.concatenate(
+        [lax.dynamic_slice_in_dim(cotangent, a0, n_full, 0), lax.dynamic_slice_in_dim(cotangent, h0, n_half, 0)]
+    )
     my_seqs = jnp.concatenate([mp * (full + 1) + jnp.arange(full), jnp.array([full])])
-    my_len = lengths[my_seqs]
-    pos = jnp.arange(seq_len)
-    pos_last = jnp.where(pos < n_half, pos + mp * n_half, pos - n_half + (1 - mp) * n_half)
-    valid_full = pos[None, :] < my_len[:full, None]
-    valid_last = pos_last[None, :] < my_len[full:, None]
-
-    q = (jnp.dot(x_own, qk[0], preferred_element_type=F32) + vec[0]).astype(BF)
-    k = jnp.dot(x_all, qk[1], preferred_element_type=F32).astype(BF)
-    v = (jnp.dot(x_all, va[0], preferred_element_type=F32) + vec[1]).astype(BF)
-
-    def split(t, first):
-        return (
-            t[:n_full].reshape(full, seq_len, heads, HEAD_DIM),
-            t[n_full:].reshape(1, first, heads, HEAD_DIM),
-        )
-
-    qs, ks, vs = split(q, n_half), split(k, seq_len), split(v, seq_len)
-    valids = (valid_full, valid_last)
-    lses, outs = [], []
-
-    def scores(qh, kh, valid):
-        raw = jnp.einsum("gqhe,gkhe->ghqk", qh, kh, preferred_element_type=F32) * score_scale
-        return jnp.where(valid[:, None, None, :], raw, -1000000000.0)
-
-    for qh, kh, vh, valid in zip(qs, ks, vs, valids):
-        s = scores(qh, kh, valid)
-        top = jnp.max(s, axis=-1, keepdims=True)
-        lse = top + jnp.log(jnp.sum(jnp.exp(s - top), axis=-1, keepdims=True))
-        pb = jnp.exp(s - lse).astype(BF)
-        o = jnp.einsum("ghqk,gkhe->gqhe", pb, vh, preferred_element_type=F32)
-        outs.append(o.reshape(-1, width).astype(BF))
-        lses.append(lse)
-    mixed = jnp.concatenate(outs)
-    attn = jnp.einsum("te,de->td", mixed, va[1], preferred_element_type=F32)
-    z1 = x_own.astype(F32) + attn + bias_attn
-    normed, norm_one_back = jax.vjp(layer_norm, z1, gain_one, shift_one)
-    normed_low = normed.astype(BF)
-    pre = jnp.einsum("td,hdf->htf", normed_low, inner, preferred_element_type=F32) + b_inner[:, None, :]
-    act, gelu_back = jax.vjp(gelu_exact, pre)
-    act_low = act.astype(BF)
-    f_out = jnp.einsum("htf,hdf->td", act_low, outer, preferred_element_type=F32)
-    z2 = normed + f_out + bias_outer
-    output, norm_two_back = jax.vjp(layer_norm, z2, gain_two, shift_two)
-    out_own = output.astype(BF)
 
     n_mine = full + 1
     mine = jnp.where((jnp.arange(n_mine) < full) | (mp == 0), 1.0, 0.0).astype(F32)
@@ -605,31 +898,36 @@
     one_hot = (jnp.arange(table_rows)[:, None] == ids.reshape(1, -1)).astype(F32)
     table_local = jnp.dot(one_hot, row_grads.reshape(-1, row_grads.shape[2]), precision=highest_mode)
 
+    def norm_back(dy, hat, root, gain):
+        e = dy * gain
+        back_ = e - jnp.mean(e, axis=-1, keepdims=True) - hat * jnp.mean(e * hat, axis=-1, keepdims=True)
+        return back_ * root[:, :1], jnp.sum(dy * hat, axis=0), jnp.sum(dy, axis=0)
+
     dy = cot.astype(F32)
     first_rows = jnp.arange(n_mine) * seq_len
     dy = dy.at[first_rows].add(cls_grad)
-    dz2, dg2, dc2 = norm_two_back(dy)
+    dz2, dg2, dc2 = norm_back(dy, xh2, r2, vec[6 + ff_rows])
     df = dz2.astype(BF)
     dg = jnp.einsum("td,hdf->htf", df, outer, preferred_element_type=F32)
     g_outer = jnp.einsum("td,htf->hdf", df, act_low, preferred_element_type=F32).astype(BF)
-    (du,) = gelu_back(dg)
-    du = du.astype(BF)
+    du = (dg * slope.astype(F32)).astype(BF)
+    normed_low = (xh1 * vec[3] + vec[4]).astype(BF)
     g_inner = jnp.einsum("td,htf->hdf", normed_low, du, preferred_element_type=F32).astype(BF)
     dh1 = jnp.einsum("htf,hdf->td", du, inner, preferred_element_type=F32) + dz2
-    dz1, dg1, dc1 = norm_one_back(dh1)
+    dz1, dg1, dc1 = norm_back(dh1, xh1, r1, vec[3])
     da = dz1.astype(BF)
     do = jnp.dot(da, va[1], preferred_element_type=F32).astype(BF)
     g_attn = jnp.einsum("td,te->de", da, mixed, preferred_element_type=F32)
-    dos = split(do, n_half)
     dqs, dks, dvs = [], [], []
-    for qh, kh, vh, doh, valid, lse in zip(qs, ks, vs, dos, valids, lses):
-        probs = jnp.exp(scores(qh, kh, valid) - lse)
+    probs_of = (p_ab.reshape(full, -1, seq_len, seq_len), p_c.reshape(1, -1, n_half, seq_len))
+    for qh, kh, vh, doh, pb in zip(*(halves(t, n_full, seq_len) for t in (q, k, v, do)), probs_of):
+        probs = pb.astype(F32)
         dp_ = jnp.einsum("gqhe,gkhe->ghqk", doh, vh, preferred_element_type=F32)
         delta = jnp.sum(probs * dp_, axis=-1, keepdims=True)
         ds_ = (probs * (dp_ - delta)).astype(BF)
         dqs.append((jnp.einsum("ghqk,gkhe->gqhe", ds_, kh, preferred_element_type=F32) * score_scale).reshape(-1, width))
         dks.append((jnp.einsum("ghqk,gqhe->gkhe", ds_, qh, preferred_element_type=F32) * score_scale).reshape(-1, width))
-        dvs.append(jnp.einsum("ghqk,gqhe->gkhe", probs.astype(BF), doh, preferred_element_type=F32).reshape(-1, width))
+        dvs.append(jnp.einsum("ghqk,gqhe->gkhe", pb, doh, preferred_element_type=F32).reshape(-1, width))
     dq = jnp.concatenate(dqs).astype(BF)
     dk = jnp.concatenate(dks).astype(BF)
     dv = jnp.concatenate(dvs).astype(BF)

time: 495 us -> 423 us (0.85); the launches traced: 492 us -> 415 us
  matrix products: 127 us -> 63.1 us
  Pallas kernels: 216 us -> 240 us
  local copies, waits for them, and re-layouts: 92 us -> 73.1 us
  other arithmetic: 52.6 us -> 34.7 us
    dot_general x12 -> x2, matrix products: 67 us -> 5.51 us  [local(): jnp.einsum('ghqk,gqhe->gkhe', pb, doh, preferred_element_type=F32)]
    pallas_call x1, Pallas kernels: 83.1 us -> 107 us  [forward_fast(): pl.pallas_call(forward_kernel, out_shape=[jax.ShapeDtypeStruct(s, d) for...]
    unnamed x261 -> x152, local copies, waits for them, and re-layouts: 12.1 us -> 4.94 us
    reduce_sum x7 -> x1, other arithmetic: 8.74 us -> 2.47 us  [norm_back(): return (back_ * root[:, :1], jnp.sum(dy * hat, axis=0), jnp.sum(dy, axis=0))]
    dot_general x1, matrix products: 12.1 us -> 6 us  [local(): dg = jnp.einsum('td,hdf->htf', df, outer, preferred_element_type=F32)]
    convert_element_type x2, other arithmetic: 4.38 us -> 10 us  [local(): ds_ = (probs * (dp_ - delta)).astype(BF)]
    slice x20 -> x15, local copies, waits for them, and re-layouts: 12.5 us -> 16.3 us  [the longest x8 5.39 us: halves(): t[n_full:].reshape(1, last, heads, HEAD_DIM)]
    reshape x13 -> x7, local copies, waits for them, and re-layouts: 31.5 us -> 28.5 us  [the longest x5 17.3 us: halves(): t[:n_full].reshape(n_full // seq_len, seq_len, heads, HEAD_DIM)]
where the time goes in v2:
time: 423 us; the launch traced here: 415 us
  Pallas kernels  240 us (57%)
  local copies, waits for them, and re-layouts  73.1 us (17%)
  matrix products  63.1 us (15%)
  other arithmetic  34.7 us (8%)
    pallas_call x1, Pallas kernels, reduce_fast(): pl.pallas_call(functools.partial(reduce_kernel, 7, len(out_shape), index)...  133 us
    pallas_call x1, Pallas kernels, forward_fast(): pl.pallas_call(forward_kernel, out_shape=[jax.ShapeDtypeStruct(s, d) for...  107 us
    reshape x5, local copies, waits for them, and re-layouts, halves(): t[:n_full].reshape(n_full // seq_len, seq_len, heads, HEAD_DIM)  17.3 us
    convert_element_type x2, other arithmetic, local(): ds_ = (probs * (dp_ - delta)).astype(BF)  10 us

profile of v2, /device:TPU:0, one launch (start us, length us, event | category | flops | bytes accessed | tf_op | source)
XLA Modules:
  0.0 415.2 jit_solution(14332695561473311207)
XLA Ops:
  0.8 1.4 gather_fusion.1
  2.3 1.3 gather_fusion
  3.8 107.4 %forward.1 = (bf16[2,4,2,2,48,768]{5,4,3,2,1,0:T(8,128)(2,1)}, bf16[2,4,2,2,48,768]{5,4,3,2,1,0:T(8,128)(2,1)}, bf16[2,4,2,2,48,1536]{5,4,3,2,1,0:T(8,128)(2,1)}...) custom-call(s32[5]{0:T(128)} %refs_0_.1, ...), custom_call_target="tpu_custom_call" | custom-call | tf_op jit(solution)/shard_map/forward/pallas_call | solution.py:512
  111.2 1.3 slice.134
  114.3 1.2 fusion.40
  115.5 1.4 scatter_fusion
  117.0 1.4 slice_reduce_fusion
  119.3 2.5 multiply_reduce_fusion
  123.0 6.0 %convert_reduce_fusion = (f32[2,1536]{1,0:T(2,128)S(1)}, bf16[2,720,1536]{2,1,0:T(8,128)(2,1)S(1)}) fusion(bf16[2,720,1536]{2,1,0:T(8,128)(2,1)} %get-tuple-element.59, bf16[2,768,1536]{2,1,0:T(8,128)(2,1)S(1)} %bitcast.193, f32[720,768]{1,0:T(8,128)S(1)} %get-tuple-element.110), kind=kOutput, calls=%fused_computation.9 | convolution fusion | flops 3408995328 | bytes 15790080 | tf_op jit(solution)/shard_map/td,hdf->htf/dot_general | solution.py:911
  129.0 4.1 multiply_reduce_fusion.1
  133.1 5.6 %convolution_convert_fusion = bf16[2,1536,768]{1,2,0:T(8,128)(2,1)} fusion(bf16[2,720,1536]{2,1,0:T(8,128)(2,1)S(1)} %bitcast.195, f32[720,768]{1,0:T(8,128)S(1)} %get-tuple-element.110), kind=kOutput, calls=%fused_computation.10 | convolution fusion | flops 3400298496 | bytes 11354112 | tf_op jit(solution)/shard_map/td,htf->hdf/dot_general | solution.py:912
  139.3 5.6 %convolution_convert_fusion.1 = bf16[2,1536,768]{1,2,0:T(8,128)(2,1)} fusion(bf16[2,720,1536]{2,1,0:T(8,128)(2,1)S(1)} %get-tuple-element.135, f32[720,768]{1,0:T(8,128)S(1)} %copy-done.23, f32[768]{0:T(1024)S(1)} %get-tuple-element.88, f32[768]{0:T(1024)S(1)} %get-tuple-element.89), kind=kOutput, calls=%fused_computation.11 | convolution fusion | flops 3401404416 | bytes 11360256 | tf_op jit(solution)/shard_map/td,htf->hdf/dot_general | solution.py:915
  150.3 3.5 convolution_convert_fusion.2
  157.4 2.2 slice.135
  161.7 2.1 slice.142
  164.9 4.0 reshape.421
  168.9 4.4 %reshape.420 = bf16[2,288,12,64]{3,2,1,0:T(8,128)(2,1)} reshape(bf16[576,768]{1,0:T(8,128)(2,1)} %slice.135) | data formatting | bytes 1769472 | tf_op jit(solution)/shard_map/reshape | solution.py:841
  173.2 2.8 reshape.422
  176.0 4.3 %fusion.78 = (bf16[1,4,2,2,48,768]{5,4,3,2,1,0:T(8,128)(2,1)}, bf16[1,4,2,2,48,768]{5,4,3,2,1,0:T(8,128)(2,1)}, bf16[1,4,2,2,48,768]{5,4,3,2,1,0:T(8,128)(2,1)S(1)}, bf16[1,4,2,2,48,768]{5,4,3,2,1,0:T(8,128)(2,1)}) fusion(bf16[2,4,2,2,48,768]{5,4,3,2,1,0:T(8,128)(2,1)} %get-tuple-element.70, bf16[2,4,2,2,48,768]{5,4,3,2,1,0:T(8,128)(2,1)} %get-tuple-element.63), kind=kLoop, calls=%fused_computation.179 | loop fusion | bytes 9437184 | tf_op jit(solution)/shard_map/slice | solution.py:939
  183.0 2.7 reshape.423
  185.7 3.5 copy.69
  189.2 5.1 %fusion.22 = bf16[2,288,12,64]{1,3,2,0:T(8,128)(2,1)} fusion(bf16[2,288,12,64]{1,3,2,0:T(8,128)(2,1)S(1)} %copy.69, bf16[2,12,288,288]{3,2,1,0:T(8,128)(2,1)} %bitcast.158), kind=kOutput, calls=%fused_computation.54 | convolution fusion | flops 255246336 | bytes 5750784 | tf_op jit(solution)/shard_map/ghqk,gqhe->gkhe/dot_general | solution.py:930
  194.4 8.1 %copy.66 = bf16[2,12,288,288]{2,3,1,0:T(8,128)(2,1)} copy(bf16[2,12,288,288]{3,2,1,0:T(8,128)(2,1)} %bitcast.159) | data formatting | bytes 7962624 | tf_op jit(solution)/shard_map/reshape | solution.py:922
  202.4 3.6 copy.78
  206.0 3.1 reshape.379
  210.5 3.0 convolution_convert_fusion.3
  213.5 1.6 pad_maximum_fusion.2.refs_2_
  216.4 1.5 fusion.24
  217.8 1.2 fusion.23
  220.0 5.7 %fusion = (f32[2,12,288]{2,1,0:T(8,128)S(1)}, f32[2,12,288,288]{2,3,1,0:T(8,128)}) fusion(bf16[2,12,288,288]{2,3,1,0:T(8,128)(2,1)S(1)} %bitcast.157, bf16[2,288,12,64]{1,3,2,0:T(8,128)(2,1)S(1)} %copy-done.6, bf16[2,288,12,64]{3,2,1,0:T(8,128)(2,1)S(1)} %copy-done.13), kind=kOutput, calls=%fused_computation.5 | convolution fusion | flops 260769024 | bytes 13741056 | tf_op jit(solution)/shard_map/gqhe,gkhe->ghqk/dot_general | solution.py:925
  225.7 9.6 %fusion.1 = bf16[2,12,288,288]{2,3,1,0:T(8,128)(2,1)} fusion(bf16[2,12,288,288]{2,3,1,0:T(8,128)(2,1)} %copy.66, f32[2,12,288,288]{2,3,1,0:T(8,128)} %get-tuple-element.133, f32[2,12,288]{2,1,0:T(8,128)S(1)} %get-tuple-element.132), kind=kLoop, calls=%fused_computation.6 | loop fusion | flops 7962624 | bytes 15952896 | tf_op jit(solution)/shard_map/convert_element_type | solution.py:927
  235.4 6.3 %fusion.19 = bf16[2,288,12,64]{1,3,2,0:T(8,128)(2,1)} fusion(bf16[2,12,288,288]{2,3,1,0:T(8,128)(2,1)} %fusion.1, bf16[2,288,12,64]{3,2,1,0:T(8,128)(2,1)} %reshape.422), kind=kOutput, calls=%fused_computation.52 | convolution fusion | flops 255688704 | bytes 5750784 | tf_op jit(solution)/shard_map/ghqk,gqhe->gkhe/dot_general | solution.py:929
  241.6 1.5 fusion.16
  243.1 1.2 copy.73
  245.2 2.5 copy.84
  247.8 1.8 reshape.383
  251.9 3.2 convolution_convert_fusion.4
  255.1 1.3 convolution_convert_fusion.5
  256.5 1.5 fusion.32
  258.2 1.5 convolution_add_fusion
  260.2 1.3 fusion.5
  261.6 1.6 pad_maximum_fusion.1.refs_1_
  263.3 1.1 pad_maximum_fusion.6.refs_6_
  264.4 132.9 %reduce.13 = (f32[40,128]{1,0:T(8,128)}, f32[2,48,384]{2,1,0:T(8,128)}, f32[2,48,384]{2,1,0:T(8,128)}, f32[2,48,768]{2,1,0:T(8,128)}, f32[2,48,768]{2,1,0:T(8,12...) custom-call(f32[4,2,2,40,256]{4,3,2,1,0:T(8,128)} %pad_maximum_fusion.10.refs_0_, ...), custom_call_target="tpu_custom_call" | custom-call | tf_op jit(solution)/shard_map/reduce/pallas_call | solution.py:713
  397.3 1.2 slice.166
  399.4 1.5 broadcast_select_fusion.1
  403.7 1.5 pad_maximum_fusion.3
  411.2 2.4 pad_maximum_fusion
  (238 shorter events, 35.9 us)
Async XLA Ops:
  0.7 2.9 copy-start
  119.3 2.5 copy-start.9
  119.3 3.7 copy-start.64
  121.8 7.2 %slice-start.2 = ((s8[4718592]{0:T(1024)(128)(4,1)}), s8[4194304]{0:T(1024)(128)(4,1)S(1)}, s32[]{:S(2)}) async-start(s8[4718592]{0:T(1024)(128)(4,1)} %bitcast.190), calls=%async_computation.2 | async-start | bytes 8388608
  123.0 6.0 %copy-start.23 = (f32[720,768]{1,0:T(8,128)S(1)}, f32[720,768]{1,0:T(8,128)}, u32[]{:S(2)}) copy-start(f32[720,768]{1,0:T(8,128)} %get-tuple-element.61) | copy-start | bytes 6635524
  123.0 6.0 %slice-start.3 = ((s8[4718592]{0:T(1024)(128)(4,1)}), s8[524288]{0:T(1024)(128)(4,1)S(1)}, s32[]{:S(2)}) async-start(s8[4718592]{0:T(1024)(128)(4,1)} %bitcast.190), calls=%async_computation.3 | async-start | bytes 1048576
  123.0 10.2 %slice-start.4 = ((s8[4423680]{0:T(1024)(128)(4,1)}), s8[229376]{0:T(1024)(128)(4,1)S(1)}, s32[]{:S(2)}) async-start(s8[4423680]{0:T(1024)(128)(4,1)} %bitcast.194), calls=%async_computation.4 | async-start | bytes 458752
  129.0 4.1 slice-start.5
  139.3 40.9 %copy-start.7 = (f32[720,768]{1,0:T(8,128)}, f32[720,768]{1,0:T(8,128)S(1)}, u32[]{:S(2)}) copy-start(f32[720,768]{1,0:T(8,128)S(1)} %get-tuple-element.112) | copy-start | bytes 6635524
  150.3 3.5 copy-start.31
  183.0 27.5 %copy-start.14 = (bf16[12,64,288]{2,1,0:T(8,128)(2,1)}, bf16[12,64,288]{2,1,0:T(8,128)(2,1)S(1)}, u32[]{:S(2)}) copy-start(bf16[12,64,288]{2,1,0:T(8,128)(2,1)S(1)} %convolution_convert_fusion.8) | copy-start | bytes 1327108
  189.2 5.1 %copy-start.5 = (bf16[2,288,12,64]{1,3,2,0:T(8,128)(2,1)}, bf16[2,288,12,64]{1,3,2,0:T(8,128)(2,1)S(1)}, u32[]{:S(2)}) copy-start(bf16[2,288,12,64]{1,3,2,0:T(8,128)(2,1)S(1)} %copy.69) | copy-start | bytes 2654212
  209.1 4.4 %copy-start.10 = (bf16[576,768]{0,1:T(8,128)(2,1)}, bf16[576,768]{0,1:T(8,128)(2,1)S(1)}, u32[]{:S(2)}) copy-start(bf16[576,768]{0,1:T(8,128)(2,1)S(1)} %reshape.379) | copy-start | bytes 2654212
  210.5 3.0 copy-start.28
  215.9 3.2 slice-start
  215.9 3.2 slice-start.1
  216.3 2.7 copy-start.6
  216.4 3.7 copy-start.13
  235.4 6.3 %copy-start.2 = (bf16[2,12,288,288]{2,3,1,0:T(8,128)(2,1)S(1)}, bf16[2,12,288,288]{2,3,1,0:T(8,128)(2,1)}, u32[]{:S(2)}) copy-start(bf16[2,12,288,288]{2,3,1,0:T(8,128)(2,1)} %fusion.1) | copy-start | bytes 11943940
  235.4 6.3 %copy-start.12 = (bf16[2,288,12,64]{3,2,1,0:T(8,128)(2,1)S(1)}, bf16[2,288,12,64]{3,2,1,0:T(8,128)(2,1)}, u32[]{:S(2)}) copy-start(bf16[2,288,12,64]{3,2,1,0:T(8,128)(2,1)} %reshape.420) | copy-start | bytes 2654212
  245.2 4.5 %copy-start.19 = (bf16[12,64,144]{2,1,0:T(8,128)(2,1)S(1)}, bf16[12,64,144]{2,1,0:T(8,128)(2,1)}, u32[]{:S(2)}) copy-start(bf16[12,64,144]{2,1,0:T(8,128)(2,1)} %fusion.24) | copy-start | bytes 663556
  247.7 2.5 copy-start.56
  247.8 2.5 copy-start.54
  247.8 2.6 copy-start.53
  247.8 2.6 copy-start.55
  247.8 2.6 copy-start.42
  247.8 2.6 copy-start.51
  247.8 2.6 copy-start.52
  247.8 3.1 copy-start.25
  247.8 3.1 copy-start.43
  249.7 2.2 copy-start.32
  251.9 3.2 copy-start.65
  260.2 3.0 copy-start.4
  264.4 134.8 %copy-start.18 = (bf16[720,768]{1,0:T(8,128)(2,1)S(1)}, bf16[720,768]{1,0:T(8,128)(2,1)}, u32[]{:S(2)}) copy-start(bf16[720,768]{1,0:T(8,128)(2,1)} %get-tuple-element.51.refs_5_) | copy-start | bytes 3317764
  399.2 2.3 copy-start.57
  399.3 2.3 copy-start.62
  399.3 2.2 copy-start.63
  399.3 2.9 copy-start.48
  399.3 2.9 copy-start.59
  399.3 2.9 copy-start.60
  399.3 3.5 copy-start.46
  399.3 3.5 copy-start.41
  399.3 3.5 copy-start.49
  399.3 3.5 copy-start.50
  405.3 3.1 copy-start.30
  405.3 3.1 copy-start.39
  405.3 3.1 copy-start.40
  411.2 2.5 copy-start.1
  (24 other events, 38.6 us)

commit v3 on v2

--- a/solution.py
+++ b/solution.py
@@ -253,17 +253,17 @@
 
 def forward_kernel(*refs):
     (lens, tokens, w_qkv, w_attn, w_inner, w_outer, w_proj, vectors) = refs[:8]
-    outs = refs[8:28]
-    scr = refs[28:]
+    outs = refs[8:27]
+    scr = refs[27:]
     (small_s, qk_s, va_s, inner_s, outer_s, small_g, qk, va, inner, outer) = scr[:10]
-    (x_all, q, k, v, p_ab, p_c, o, xh1, r1, g, gp, xh2, r2, out_own, proj, vec, h1b, vecp, bias_ff) = scr[10:29]
+    (xt, q, k, v, p, o, xh1, r1, g, gp, xh2, r2, out_own, proj, vec, x_all, h1b, vecp, bias_ff) = scr[10:29]
     gsems, tsem, osem = scr[29:38], scr[38], scr[39]
     me = Place()
     mp = me.x
     n_all, width = x_all.shape
     n_own = q.shape[0]
-    seq = p_ab.shape[1]
-    half_seq = seq // 2
+    half_seq = n_all - n_own
+    seq = 2 * half_seq
     full = (n_own - half_seq) // seq
     n_full = full * seq
     half_ff = inner.shape[-1]
@@ -310,8 +310,8 @@
     ]
     net = Gather(me, pieces, gsems)
     ahead = 3
-    for p in range(ahead):
-        net.step1(p)
+    for i in range(ahead):
+        net.step1(i)
     tick = lambda t: net.tick(t, ahead)
     saves = []
 
@@ -322,7 +322,12 @@
 
     for cp in loads:
         cp.wait()
-    save(4, x_all)
+
+    def x_turn(i):
+        xt[rows_at(i, 256), :] = jnp.transpose(x_all[:, lanes(i, 256)])
+
+    each(width // 256, x_turn)
+    save(4, xt)
     for t in range(4):
         tick(t)
     big = []
@@ -338,8 +343,8 @@
     for h in range(2):
         for x in range(NX):
             bias_ff[h : h + 1, x * width : (x + 1) * width] = vec[5 + NX * x + h : 6 + NX * x + h, :]
-    save(17, proj)
-    save(18, vec)
+    save(16, proj)
+    save(17, vec)
 
     def project(w_ref, src_rows, dst, bias):
         n_tile = 256
@@ -369,32 +374,33 @@
     head_mask = (head_lo.astype(BF), (1.0 - head_lo).astype(BF))
     pos = lax.broadcasted_iota(jnp.int32, (1, seq), 1)
 
-    def attend(q0, nq, k0, hp, length, place, p_ref, p_at):
-        qp = q[pl.ds(pl.multiple_of(q0, 16), nq), lanes(hp)]
-        kp = k[pl.ds(pl.multiple_of(k0, 16), seq), lanes(hp)]
-        vp = v[pl.ds(pl.multiple_of(k0, 16), seq), lanes(hp)]
-        got = []
-        for h in range(2):
-            s = mm_nt(qp * head_mask[h], kp) * (HEAD_DIM**-0.5)
-            s = jnp.where(place < length, s, -1000000000.0)
-            e = jnp.exp(s - jnp.max(s, axis=-1, keepdims=True))
-            pb = (e * (1.0 / jnp.sum(e, axis=-1, keepdims=True))).astype(BF)
-            p_ref[p_at + h] = pb
-            got.append(mm(pb, vp))
-        mixed = jnp.where(lane < HEAD_DIM, got[0], got[1])
-        o[pl.ds(pl.multiple_of(q0, 16), nq), lanes(hp)] = mixed.astype(BF)
-
-    pairs = width // 128
+    def attend(q0, nq, k0, slab, length, place):
+        at_q = pl.ds(pl.multiple_of(q0, 16), nq)
+        at_k = pl.ds(pl.multiple_of(k0, 16), seq)
+        for pair in range(2):
+            l = lanes(2 * slab + pair)
+            qp, kp, vp = q[at_q, l], k[at_k, l], v[at_k, l]
+            got = []
+            for h in range(2):
+                s = mm_nt(qp * head_mask[h], kp) * (HEAD_DIM**-0.5)
+                s = jnp.where(place < length, s, -1000000000.0)
+                e = jnp.exp(s - jnp.max(s, axis=-1, keepdims=True))
+                pb = (e * (1.0 / jnp.sum(e, axis=-1, keepdims=True))).astype(BF)
+                j = 384 * (2 * pair + h)
+                p[slab, at_q, j : j + seq] = pb
+                got.append(mm(pb, vp))
+            o[at_q, l] = jnp.where(lane < HEAD_DIM, got[0], got[1]).astype(BF)
+
+    slabs = p.shape[0]
     for s in range(full):
         length = lens[mp * (full + 1) + s]
-        each(pairs, lambda hp: attend(s * seq, seq, s * seq, hp, length, pos, p_ab, s * 2 * pairs + 2 * hp))
+        each(slabs, lambda i: attend(s * seq, seq, s * seq, i, length, pos))
         tick(7 + s)
     length = lens[full]
     pos_c = jnp.where(pos < half_seq, pos + mp * half_seq, pos - half_seq + (1 - mp) * half_seq)
-    each(pairs, lambda hp: attend(n_full, half_seq, n_full, hp, length, pos_c, p_c, 2 * hp))
-    save(8, p_ab)
-    save(9, p_c)
-    save(10, o)
+    each(slabs, lambda i: attend(n_full, half_seq, n_full, i, length, pos_c))
+    save(8, p)
+    save(9, o)
     tick(7 + full)
 
     tile = 240
@@ -411,8 +417,8 @@
         h1b[at, :] = (hat * vec[3:4, :] + vec[4:5, :]).astype(BF)
 
     norm_rows(xh1, r1, n_own, put_h1)
-    save(11, xh1)
-    save(12, r1)
+    save(10, xh1)
+    save(11, r1)
     tick(8 + full)
 
     def feed(h):
@@ -437,8 +443,8 @@
     for t in range(10 + full, len(pieces) + 3):
         tick(t)
     save(2, inner)
-    save(13, g)
-    save(14, gp)
+    save(12, g)
+    save(13, gp)
 
     def ff_out(i):
         at = rows_at(i, tile)
@@ -453,9 +459,9 @@
         out_own[at, :] = (hat * vec[10:11, :] + vec[11:12, :]).astype(BF)
 
     norm_rows(xh2, r2, n_own, put_y)
-    save(15, xh2)
-    save(16, r2)
-    save(19, out_own)
+    save(14, xh2)
+    save(15, r2)
+    save(18, out_own)
     net.end()
     for cp in saves:
         cp.wait()
@@ -479,12 +485,11 @@
         ((2,) + zyc + (rows, half_ff), BF),
     ]
     kept = [
-        ((n_all, width), BF),
+        ((width, n_all), BF),
         ((n_own, width), BF),
         ((n_all, width), BF),
         ((n_all, width), BF),
-        ((full * heads, seq, seq), BF),
-        ((heads, seq // 2, seq), BF),
+        ((heads // 4, n_own, 4 * 384), BF),
         ((n_own, width), BF),
         ((n_own, width), F32),
         ((n_own, 128), F32),
@@ -496,7 +501,7 @@
         ((16, width), F32),
         ((n_own, width), BF),
     ]
-    order = kept[:13] + [kept[15], kept[13], kept[14]]
+    order = kept[:12] + [kept[14], kept[12], kept[13]]
     scratch = [
         ((small_rows, 128), F32),
         ((2, rows, width // 2), BF),
@@ -504,7 +509,9 @@
         ((2, rows, half_ff // 2), BF),
         ((2, rows, half_ff // 2), BF),
         (zyc + (small_rows, 256), F32),
-    ] + weights + order + [((n_own, width), BF), ((128, 128), F32), ((8, half_ff), F32)]
+    ]
+    scratch += weights + order
+    scratch += [((n_all, width), BF), ((n_own, width), BF), ((128, 128), F32), ((8, half_ff), F32)]
     n = 9
     vm = pl.BlockSpec(memory_space=pltpu.VMEM)
     hb = pl.BlockSpec(memory_space=ANY)
@@ -513,7 +520,7 @@
         forward_kernel,
         out_shape=[jax.ShapeDtypeStruct(s, d) for s, d in weights + kept],
         in_specs=[sm, hb] + [vm] * 6,
-        out_specs=[hb] * 20,
+        out_specs=[hb] * 19,
         scratch_shapes=[pltpu.VMEM(s, d) for s, d in scratch]
         + [
             dma(n), dma(n, NZ), dma(n, NZ), dma(n), dma(n), dma(n), dma(n), dma(n, 3), dma(n, 3),
@@ -526,129 +533,125 @@
     )(lengths, tokens, w_qkv, w_attn, w_inner, w_outer, w_proj, vectors)
 
 
-def reduce_kernel(n_in, n_out, index, *refs):
-    ins, outs = refs[:n_in], refs[n_in : n_in + n_out]
-    rest = refs[n_in + n_out :]
-    nb = len(index)
-    bufs, rest = rest[: 5 * nb], rest[5 * nb :]
-    sq4, sq8, lsem, ds, dr, s1, r1, s2, r2, zs, zr, xs, xr, qs, qr, es, er = rest
-    send_out, send_dx = ins[-2:]
-    peer_out, peer_dx, peer_small, norm_ref = outs[-4:]
-    me = Place()
-    greet(me.others() + me.eights())
-    n = len(index)
-    waits = []
-
-    def go(copy):
+class Reduce:
+    def __init__(self, me, pieces, sems):
+        self.me, self.pieces = me, pieces
+        self.ds, self.dr, self.s1, self.r1, self.s2, self.r2, self.zs, self.zr = sems
+        self.waits = []
+        self.squares = jnp.zeros((1, 1), F32)
+
+    def go(self, copy):
         copy.start()
-        waits.append(copy)
-        return copy
-
-    oc, oy, ox = 1 - me.c, 1 - me.y, 1 - me.x
-    pieces = []
-    for p, (i, li, o, lo, sx) in enumerate(index):
-        src = ins[i] if li is None else ins[i].at[li]
-        dst = outs[o] if lo is None else outs[o].at[lo]
-        pieces.append((src, dst) + tuple(bufs[5 * p : 5 * p + 5]))
-
-    def step1(p):
-        src, _, own, got1, _, _, _ = pieces[p]
-        go(remote(src.at[:, :, oc], got1, ds.at[p], dr.at[p], me.dev(c=oc)))
-        loc = pltpu.make_async_copy(src.at[:, :, me.c], own, lsem.at[p])
-        loc.start()
-        return loc
-
-    def half(ref):
-        return ref.shape[-1] // 2
-
-    def step2(p, loc):
-        _, _, own, got1, got2, got3, got4 = pieces[p]
-        loc.wait()
-        remote(got1, got1, ds.at[p], dr.at[p], me.dev()).wait_recv()
-        own[...] = own[...] + got1[...]
-        if p % 2 == 0:
-            go(remote(own.at[:, oy], got2, s1.at[p], r1.at[p], me.dev(y=oy)))
+        self.waits.append(copy)
+
+    def arrived(self, ref, ssem, rsem):
+        remote(ref, ref, ssem, rsem, self.me.dev(c=1 - self.me.c)).wait_recv()
+
+    def step1(self, p):
+        src, got1 = self.pieces[p][2], self.pieces[p][3]
+        oc = 1 - self.me.c
+        self.go(remote(src.at[:, :, oc], got1, self.ds.at[p], self.dr.at[p], self.me.dev(c=oc)))
+
+    def step2(self, p):
+        route, _, src, got1, got2, _, _ = self.pieces[p]
+        me = self.me
+        c, half = me.c, src.shape[-1] // 2
+        self.arrived(got1, self.ds.at[p], self.dr.at[p])
+
+        def add(z):
+            for y in range(NY):
+                src[z, y, c] = src[z, y, c] + got1[z, y]
+
+        each(NZ, add)
+        if route == "y":
+            part, dev = src.at[:, 1 - me.y, c], me.dev(y=1 - me.y)
         else:
-            go(remote(own.at[:, :, :, cols(ox, half(own))], got2, s1.at[p], r1.at[p], me.dev(x=ox)))
-
-    def step3(p):
-        _, _, own, _, got2, got3, _ = pieces[p]
-        remote(got2, got2, s1.at[p], r1.at[p], me.dev()).wait_recv()
-        h = half(own)
-        if p % 2 == 0:
-            own[:, me.y] = own[:, me.y] + got2[...]
-            go(remote(own.at[:, me.y, :, cols(ox, h)], got3, s2.at[p], r2.at[p], me.dev(x=ox)))
+            part, dev = src.at[:, :, c, :, cols(1 - me.x, half)], me.dev(x=1 - me.x)
+        self.go(remote(part, got2, self.s1.at[p], self.r1.at[p], dev))
+
+    def step3(self, p):
+        route, _, src, _, got2, got3, _ = self.pieces[p]
+        me = self.me
+        c, half = me.c, src.shape[-1] // 2
+        mine = cols(me.x, half)
+        self.arrived(got2, self.s1.at[p], self.r1.at[p])
+        if route == "y":
+
+            def add(z):
+                src[z, me.y, c] = src[z, me.y, c] + got2[z]
+
+            each(NZ, add)
+            part, dev = src.at[:, me.y, c, :, cols(1 - me.x, half)], me.dev(x=1 - me.x)
         else:
-            own[:, :, :, cols(me.x, h)] = own[:, :, :, cols(me.x, h)] + got2[...]
-            go(remote(own.at[:, oy, :, cols(me.x, h)], got3, s2.at[p], r2.at[p], me.dev(y=oy)))
-
-    def step4(p):
-        _, _, own, _, _, got3, got4 = pieces[p]
-        remote(got3, got3, s2.at[p], r2.at[p], me.dev()).wait_recv()
-        h = half(own)
-        mine = cols(me.x, h)
-        own[:, me.y, :, mine] = own[:, me.y, :, mine] + got3[...]
+
+            def add(z):
+                for y in range(NY):
+                    src[z, y, c, :, mine] = src[z, y, c, :, mine] + got2[z, y]
+
+            each(NZ, add)
+            part, dev = src.at[:, 1 - me.y, c, :, mine], me.dev(y=1 - me.y)
+        self.go(remote(part, got3, self.s2.at[p], self.r2.at[p], dev))
+
+    def step4(self, p):
+        _, _, src, _, _, got3, got4 = self.pieces[p]
+        me = self.me
+        c, mine = me.c, cols(me.x, src.shape[-1] // 2)
+        self.arrived(got3, self.s2.at[p], self.r2.at[p])
+
+        def add(z):
+            src[z, me.y, c, :, mine] = src[z, me.y, c, :, mine] + got3[z]
+
+        each(NZ, add)
         for k in range(1, NZ):
             tz = lax.rem(me.z + k, NZ)
-            go(remote(own.at[tz, me.y, :, mine], got4.at[k], zs.at[p, k], zr.at[p, k], me.dev(z=tz)))
-
-    def step5(p):
-        _, dst, own, _, _, _, got4 = pieces[p]
+            part = src.at[tz, me.y, c, :, mine]
+            self.go(remote(part, got4.at[k], self.zs.at[p, k], self.zr.at[p, k], me.dev(z=tz)))
+
+    def step5(self, p, counted=True):
+        _, dst, src, _, _, _, got4 = self.pieces[p]
+        me = self.me
         for k in range(1, NZ):
-            remote(got4.at[k], got4.at[k], zs.at[p, k], zr.at[p, k], me.dev()).wait_recv()
-        total = own[me.z, me.y, :, cols(me.x, half(own))].astype(F32)
+            self.arrived(got4.at[k], self.zs.at[p, k], self.zr.at[p, k])
+        total = src[me.z, me.y, me.c, :, cols(me.x, src.shape[-1] // 2)].astype(F32)
         for k in range(1, NZ):
             total = total + got4[k].astype(F32)
         dst[...] = total
-        return jnp.sum(total * total, keepdims=True)
-
-    go(remote(send_out, peer_out, xs.at[0], xr.at[0], me.dev(x=ox)))
-    locs = {}
-    ahead = 2
-    total = jnp.zeros((1, 1), F32)
-    for p in range(min(ahead, n)):
-        locs[p] = step1(p)
-    for t in range(n + 3):
-        if t < n:
-            step2(t, locs[t])
-            if t + ahead < n:
-                locs[t + ahead] = step1(t + ahead)
-        if 0 <= t - 1 < n:
-            step3(t - 1)
-        if 0 <= t - 2 < n:
-            step4(t - 2)
-        if 0 <= t - 3 < n:
-            p = t - 3
-            part = step5(p)
-            if index[p][4]:
-                total = total + part
-    go(remote(send_dx, peer_dx, xs.at[1], xr.at[1], me.dev(x=ox)))
-    small = outs[index[-1][2]]
-    go(remote(small, peer_small, xs.at[2], xr.at[2], me.dev(x=ox)))
-    row = lax.broadcasted_iota(jnp.int32, small.shape, 0)
-    keep = jnp.where(row < 36, small[...], 0.0)
-    total = total + jnp.sum(keep * keep, keepdims=True)
+        if counted:
+            self.squares = self.squares + jnp.sum(total * total, keepdims=True)
+
+    def end(self):
+        for copy in self.waits:
+            copy.wait_send()
+
+
+routes = ("x", "y", "x", "x", "x", "y", "y", "y", "y")
+
+
+def all_squares(me, net, total, sq4, sq8, sems):
+    qs, qr, es, er = sems
     sq4[0] = jnp.broadcast_to(total, (8, 128))
     copies = []
     for k in range(1, NZ):
-        c = remote(sq4.at[0], sq4.at[k], qs.at[k], qr.at[k], me.dev(z=lax.rem(me.z + k, NZ)))
-        copies.append(go(c))
-    for k in range(1, NZ):
-        copies[k - 1].wait_recv()
+        copies.append(remote(sq4.at[0], sq4.at[k], qs.at[k], qr.at[k], me.dev(z=lax.rem(me.z + k, NZ))))
+    for copy in copies:
+        net.go(copy)
+    for copy in copies:
+        copy.wait_recv()
+
     def at_z(z):
         out = jnp.zeros((8, 128), F32)
         for k in range(NZ):
-            src = lax.rem(me.z + NZ - k, NZ)
-            out = out + jnp.where(src == z, sq4[k], 0.0)
+            out = out + jnp.where(lax.rem(me.z + NZ - k, NZ) == z, sq4[k], 0.0)
         return out
-    group = at_z(0) + at_z(1) + at_z(2) + at_z(3)
-    sq8[0] = group
+
+    sq8[0] = at_z(0) + at_z(1) + at_z(2) + at_z(3)
     copies = []
     for k, dev in enumerate(me.eights(), 1):
-        copies.append(go(remote(sq8.at[0], sq8.at[k], es.at[k], er.at[k], dev)))
+        copies.append(remote(sq8.at[0], sq8.at[k], es.at[k], er.at[k], dev))
+    for copy in copies:
+        net.go(copy)
     for copy in copies:
         copy.wait_recv()
-    code = me.x + 2 * me.y + 4 * me.c
 
     def at_code(w):
         out = jnp.zeros((8, 128), F32)
@@ -665,67 +668,430 @@
     whole = at_code(0)
     for w in range(1, 8):
         whole = whole + at_code(w)
-    norm_ref[...] = whole
-    remote(peer_out, peer_out, xs.at[0], xr.at[0], me.dev()).wait_recv()
-    remote(peer_dx, peer_dx, xs.at[1], xr.at[1], me.dev()).wait_recv()
-    remote(peer_small, peer_small, xs.at[2], xr.at[2], me.dev()).wait_recv()
-    for copy in waits:
-        copy.wait_send()
-
-
-def reduce_fast(grads, small, own_out, own_dx, rows):
+    return whole
+
+
+def fold(value):
+    return jnp.sum(value.reshape(-1, 8, value.shape[-1]), axis=0)
+
+
+def norm_back_rows(n_rows, get_dy, hat_ref, root_ref, gain, put, acc):
+    step = 48
+
+    def body(i):
+        at = rows_at(i, step)
+        dy, hat = get_dy(i, at), hat_ref[at, :]
+        e = dy * gain
+        root = root_ref[at, 0:1]
+        m1 = jnp.mean(e, axis=-1, keepdims=True)
+        m2 = jnp.mean(e * hat, axis=-1, keepdims=True)
+        dz = (e - m1 - hat * m2) * root
+        acc[0] = acc[0] + fold(dy * hat)
+        acc[1] = acc[1] + fold(dy)
+        acc[2] = acc[2] + fold(dz)
+        hat_ref[at, :] = dz
+        put(at, dz)
+
+    each(n_rows // step, body)
+
+
+def backward_kernel(*refs):
+    doc_ids, cotangent, doc_rows = refs[:3]
+    (qk_h, va_h, inner_h, outer_h, xt_h, q_h, k_h, v_h, p_h, o_h, xh1_h, r1_h, g_h, gp_h, xh2_h, r2_h, proj_h, vec_h, out_h) = refs[3:22]
+    outs = refs[22:32]
+    small_r, qk_r, va_r, inner_r, outer_r, dx, peer_out, peer_dx, peer_small, norm_ref = outs
+    scr = list(refs[32:])
+
+    def take(n):
+        got = scr[:n]
+        del scr[:n]
+        return got
+
+    (inner, outer, attn, xt, q, k, v, o, xh1, gg, xh2, r2, proj, vec, cls_in, cot, df, dft) = take(18)
+    (cls_grad, acc1, acc2, ffacc, vg, small) = take(6)
+    grads = take(4)
+    bufs = take(9 * 4)
+    sq4, sq8 = take(2)
+    lsem, rsems, xs, xr, qsems = take(1)[0], take(8), *take(2), take(4)
+    do, da, dat, h1t, r1 = cot, df, dft, dft, r2
+    me = Place()
+    mp = me.x
+    n_all, width = dx.shape
+    n_own = q.shape[0]
+    half_seq = n_all - n_own
+    seq = 2 * half_seq
+    n_full = n_own - half_seq
+    full = n_full // seq
+    half_ff = inner.shape[-1]
+    other = me.dev(x=1 - mp)
+
+    for i in range(4):
+        grads.append(inner.at[i // 2, :, :, :, :, pl.ds(width * (i % 2), width)])
+    copies = {}
+
+    def load(name, i, src, dst):
+        cp = pltpu.make_async_copy(src, dst, lsem.at[i])
+        cp.start()
+        copies[name] = cp
+
+    def need(*names):
+        for name in names:
+            copies[name].wait()
+
+    load("vec", 0, vec_h, vec)
+    load("proj", 1, proj_h, proj)
+    for s in range(full + 1):
+        load("cls%d" % s, 2 + s, out_h.at[pl.ds(s * seq, 16)], cls_in.at[s])
+    load("cot0", 5, cotangent.at[pl.ds(pl.multiple_of(mp * (n_full + seq), 16), n_full)], cot.at[pl.ds(0, n_full)])
+    load("cot1", 6, cotangent.at[pl.ds(pl.multiple_of(n_full + mp * half_seq, 16), half_seq)], cot.at[pl.ds(n_full, half_seq)])
+    load("xh2", 7, xh2_h, xh2)
+    load("r2", 8, r2_h, r2)
+    load("g", 9, g_h, gg.at[pl.ds(0, 2)])
+    load("outer", 10, outer_h, outer)
+    load("gp", 11, gp_h, gg.at[pl.ds(2, 2)])
+    load("xh1", 12, xh1_h, xh1)
+    load("inner", 14, inner_h, inner)
+    load("attn", 15, va_h.at[1], attn)
+    load("o", 16, o_h, o)
+    load("q", 17, q_h, q)
+    load("k", 18, k_h, k)
+    load("v", 19, v_h, v)
+    load("xt", 20, xt_h, xt)
+
+    greet(me.others() + me.eights())
+    pieces = []
+    dsts = [outer_r.at[0], outer_r.at[1], inner_r.at[0], inner_r.at[1], va_r.at[1], va_r.at[0], qk_r.at[0], qk_r.at[1], small_r]
+    for p in range(9):
+        src = grads[p] if p < 8 else small
+        pieces.append((routes[p], dsts[p], src) + tuple(bufs[4 * p : 4 * p + 4]))
+    net = Reduce(me, pieces, rsems)
+    send_out = remote(out_h, peer_out, xs.at[0], xr.at[0], other)
+    net.go(send_out)
+
+    vg[...] = jnp.zeros_like(vg)
+    small[...] = jnp.zeros_like(small)
+    acc1[...] = jnp.zeros_like(acc1)
+    acc2[...] = jnp.zeros_like(acc2)
+    ffacc[...] = jnp.zeros_like(ffacc)
+    need("vec", "proj", *["cls%d" % s for s in range(full + 1)])
+    row16 = lax.broadcasted_iota(jnp.int32, (16, 1), 0)
+    cls = jnp.zeros((16, width), F32)
+    for s in range(full + 1):
+        cls = jnp.where(row16 == s, cls_in[s].astype(F32)[0:1], cls)
+    cls = cls.astype(BF)
+    proj_low = proj[...].astype(BF)
+    query = mm(cls, proj_low).astype(BF).astype(F32)
+    row8 = lax.broadcasted_iota(jnp.int32, (8, 1), 0)
+    dcq = jnp.zeros((16, 128), F32)
+    row_grads = []
+    cands = doc_ids.shape[1]
+    seq_ids = [mp * (full + 1) + s for s in range(full)] + [full]
+    for s in range(full + 1):
+        docs = doc_rows[seq_ids[s]].astype(F32)
+        mine = 1.0 if s < full else jnp.where(mp == 0, 1.0, 0.0)
+        query_s = query[s : s + 1]
+        score = jnp.sum(query_s * docs, axis=-1, keepdims=True) * retrieval_scale
+        e = jnp.exp(score - jnp.max(score, axis=0, keepdims=True))
+        soft = e / jnp.sum(e, axis=0, keepdims=True)
+        sg = (soft - jnp.where(row8 == 0, 1.0, 0.0)) * (retrieval_scale * mine)
+        dcq = jnp.where(row16 == s, jnp.sum(sg * docs, axis=0, keepdims=True), dcq)
+        row_grads.append(sg * query_s)
+    dcq = dcq.astype(BF)
+    cls_grad[...] = mm_nt(dcq, proj_low)
+    proj[...] = mm_tn(cls, dcq)
+
+    per = seq // 48
+    row48 = lax.broadcasted_iota(jnp.int32, (48, 1), 0)
+
+    def get_dy(i, at):
+        first = (row48 == 0) & (lax.rem(i, per) == 0)
+        return cot[at, :].astype(F32) + jnp.where(first, cls_grad[pl.ds(i // per, 1), :], 0.0)
+
+    def put_df(at, dz):
+        df[at, :] = dz.astype(BF)
+
+    need("cot0", "cot1", "xh2", "r2")
+    norm_back_rows(n_own, get_dy, xh2, r2, vec[10:11, :], put_df, acc2)
+
+    def turn(src, dst, n_rows):
+        def body(i):
+            dst[rows_at(i, 256), 0:n_rows] = jnp.transpose(src[:, lanes(i, 256)])
+
+        each(width // 256, body)
+
+    load("r1", 13, r1_h, r1)
+    turn(df, dft, n_own)
+    n_tile = 256
+    shape5 = (NZ, NY, NC, width // (NZ * NY * NC))
+
+    def weight_grad(left, right, dst, n):
+        def body(i):
+            r = mm(left(), right(lanes(i, n_tile)))
+            dst[:, :, :, :, lanes(i, n_tile)] = r.astype(BF).reshape(shape5 + (n_tile,))
+
+        each(n // n_tile, body)
+
+    need("g")
+    for h in range(2):
+        weight_grad(lambda: dft[:, 0:n_own], lambda l: gg[h, :, l], grads[h], half_ff)
+        net.step1(h)
+
+    need("outer", "gp")
+    tile = 240
+    tiles = n_own // tile
+
+    def hidden(h):
+        def body(i):
+            w = flat(outer[h, :, :, :, :, lanes(i, n_tile)])
+            for t in range(tiles):
+                at = pl.ds(t * tile, tile)
+                du = (mm(df[at, :], w) * gg[2 + h, at, lanes(i, n_tile)].astype(F32)).astype(BF)
+                gg[2 + h, at, lanes(i, n_tile)] = du
+                ffacc[h, :, lanes(i, n_tile)] = ffacc[h, :, lanes(i, n_tile)] + fold(du.astype(F32))
+
+        each(half_ff // n_tile, body)
+
+    hidden(0)
+    net.step2(0)
+    hidden(1)
+    net.step2(1)
+    net.step3(0)
+    load("p0", 21, p_h.at[0], gg.at[0])
+    load("p1", 22, p_h.at[1], gg.at[1])
+    load("wq", 23, qk_h.at[0], outer.at[0, :, :, :, :, pl.ds(0, width)])
+    load("wk", 24, qk_h.at[1], outer.at[0, :, :, :, :, pl.ds(width, width)])
+    load("wv", 25, va_h.at[0], outer.at[1, :, :, :, :, pl.ds(0, width)])
+    need("xh1", "r1")
+
+    def h1_turn(i):
+        l = lanes(i, 256)
+        h1 = (xh1[:, l] * vec[3:4, l] + vec[4:5, l]).astype(BF)
+        h1t[rows_at(i, 256), 0:n_own] = jnp.transpose(h1)
+
+    each(width // 256, h1_turn)
+    for h in range(2):
+        weight_grad(lambda: h1t[:, 0:n_own], lambda l: gg[2 + h, :, l], grads[2 + h], half_ff)
+        net.step1(2 + h)
+    net.step2(2)
+    net.step3(1)
+    net.step4(0)
+    need("inner")
+
+    def hidden_back(i):
+        at = rows_at(i, tile)
+        d = mm_nt(gg[2, at, :], flat(inner[0])) + mm_nt(gg[3, at, :], flat(inner[1]))
+        xh2[at, :] = d + xh2[at, :]
+
+    each(tiles, hidden_back)
+    load("p2", 26, p_h.at[2], gg.at[2])
+    net.step2(3)
+    net.step3(2)
+    net.step4(1)
+    net.step5(0)
+
+    norm_back_rows(n_own, lambda i, at: xh2[at, :], xh1, r1, vec[3:4, :], put_df, acc1)
+    need("attn", "o")
+
+    def mixed_back(i):
+        do[:, lanes(i, n_tile)] = mm(da[...], flat(attn[:, :, :, :, lanes(i, n_tile)])).astype(BF)
+
+    each(width // n_tile, mixed_back)
+    turn(da, dat, n_own)
+    weight_grad(lambda: dat[:, 0:n_own], lambda l: o[:, l], grads[4], width)
+    net.step1(4)
+
+    need("q", "k", "v", "p0", "p1", "p2")
+    lane = lax.broadcasted_iota(jnp.int32, (1, 128), 1)
+    head_lo = jnp.where(lane < HEAD_DIM, 1.0, 0.0)
+    head_mask = (head_lo.astype(BF), (1.0 - head_lo).astype(BF))
+    scale = HEAD_DIM**-0.5
+
+    def attend(q0, nq, k0, slab):
+        at_q = pl.ds(pl.multiple_of(q0, 16), nq)
+        at_k = pl.ds(pl.multiple_of(k0, 16), seq)
+        for pair in range(2):
+            l = lanes(2 * slab + pair)
+            qp, kp, vp, dop = q[at_q, l], k[at_k, l], v[at_k, l], do[at_q, l]
+            got = []
+            for h in range(2):
+                j = 384 * (2 * pair + h)
+                pb = gg[slab, at_q, j : j + seq]
+                p = pb.astype(F32)
+                pd = p * mm_nt(dop * head_mask[h], vp)
+                ds = (pd - p * jnp.sum(pd, axis=-1, keepdims=True)).astype(BF)
+                got.append((mm(ds, kp) * scale, mm_tn(ds, qp) * scale, mm_tn(pb, dop)))
+            low = lane < HEAD_DIM
+            q[at_q, l] = jnp.where(low, got[0][0], got[1][0]).astype(BF)
+            k[at_k, l] = jnp.where(low, got[0][1], got[1][1]).astype(BF)
+            v[at_k, l] = jnp.where(low, got[0][2], got[1][2]).astype(BF)
+
+    slabs = p_h.shape[0]
+
+    def tokens_back(at, own):
+        d = mm_nt(k[at, :], flat(outer[0, :, :, :, :, width : 2 * width]))
+        d = d + mm_nt(v[at, :], flat(outer[1, :, :, :, :, 0:width]))
+        if own:
+            d = d + mm_nt(q[at, :], flat(outer[0, :, :, :, :, 0:width])) + xh1[at, :]
+            o[at, :] = d.astype(BF)
+        else:
+            df[0:half_seq, :] = d.astype(BF)
+
+    keeps = []
+
+    def send_dx(i, src, at):
+        net.go(remote(src, peer_dx.at[at], xs.at[1 + i], xr.at[1 + i], other))
+        cp = pltpu.make_async_copy(src, dx.at[at], lsem.at[27 + i])
+        cp.start()
+        keeps.append(cp)
+
+    need("wq", "wk", "wv")
+    for s in range(full):
+        each(slabs, lambda i: attend(s * seq, seq, s * seq, i))
+        tokens_back(pl.ds(s * seq, seq), True)
+        send_dx(s, o.at[pl.ds(s * seq, seq)], pl.ds(s * seq, seq))
+        if s == 0:
+            net.step2(4)
+            net.step3(3)
+            net.step4(2)
+            net.step5(1)
+        else:
+            net.step3(4)
+            net.step4(3)
+            net.step5(2)
+    each(slabs, lambda i: attend(n_full, half_seq, n_full, i))
+    need("xt")
+    weight_grad(lambda: xt[...], lambda l: v[:, l], grads[5], width)
+    net.step1(5)
+    weight_grad(lambda: xt[:, 0:n_own], lambda l: q[:, l], grads[6], width)
+    net.step1(6)
+    net.step2(5)
+    net.step4(4)
+    net.step5(3)
+    weight_grad(lambda: xt[...], lambda l: k[:, l], grads[7], width)
+    net.step1(7)
+    net.step2(6)
+    net.step3(5)
+    net.step5(4)
+    tokens_back(pl.ds(n_full, half_seq), True)
+    tokens_back(pl.ds(n_own, half_seq), False)
+    send_dx(full, o.at[pl.ds(n_full, half_seq)], pl.ds(n_full, half_seq))
+    send_dx(full + 1, df.at[pl.ds(0, half_seq)], pl.ds(n_own, half_seq))
+
+    vg[0:1, :] = jnp.sum(q[...].astype(F32), axis=0, keepdims=True)
+    vg[1:2, :] = jnp.sum(v[...].astype(F32), axis=0, keepdims=True)
+    vg[2:3, :] = jnp.sum(acc1[2], axis=0, keepdims=True)
+    vg[3:4, :] = jnp.sum(acc1[0], axis=0, keepdims=True)
+    vg[4:5, :] = jnp.sum(acc1[1], axis=0, keepdims=True)
+    for h in range(2):
+        both = jnp.sum(ffacc[h], axis=0, keepdims=True)
+        for x in range(NX):
+            vg[5 + NX * x + h : 6 + NX * x + h, :] = both[:, x * width : (x + 1) * width]
+    vg[9:10, :] = jnp.sum(acc2[2], axis=0, keepdims=True)
+    vg[10:11, :] = jnp.sum(acc2[0], axis=0, keepdims=True)
+    vg[11:12, :] = jnp.sum(acc2[1], axis=0, keepdims=True)
+    turned = jnp.transpose(vg[...])
+    n_dev = NZ * NY * NC * NX
+    table_row = lax.broadcasted_iota(jnp.int32, (TAB_DEV * n_dev // NX, 1), 0)
+    table = jnp.zeros((TAB_DEV * n_dev // NX, 128), F32)
+    for s in range(full + 1):
+        for i in range(cands):
+            table = table + jnp.where(table_row == doc_ids[seq_ids[s], i], row_grads[s][i : i + 1], 0.0)
+    hr = width // n_dev
+    for z in range(NZ):
+        for y in range(NY):
+            for c in range(NC):
+                dp = (z * NY + y) * NC + c
+                for x in range(NX):
+                    d = dp * NX + x
+                    l = slice(x * 128, (x + 1) * 128)
+                    small[z, y, c, 0:hr, l] = proj[d * hr : (d + 1) * hr]
+                    small[z, y, c, hr : 2 * hr, l] = turned[d * hr : (d + 1) * hr]
+                    t0 = dp * TAB_DEV + x * (TAB_DEV // NX)
+                    small[z, y, c, 2 * hr : 2 * hr + TAB_DEV // NX, l] = table[t0 : t0 + TAB_DEV // NX]
+    net.step1(8)
+    net.step2(7)
+    net.step3(6)
+    net.step4(5)
+    net.step2(8)
+    net.step3(7)
+    net.step4(6)
+    net.step3(8)
+    net.step4(7)
+    net.step5(5)
+    net.step4(8)
+    net.step5(6)
+    net.step5(7)
+    net.step5(8, False)
+    net.go(remote(small_r, peer_small, xs.at[5], xr.at[5], other))
+    count = small_r[0 : 2 * hr, :]
+    total = net.squares + jnp.sum(count * count, keepdims=True)
+    norm_ref[...] = all_squares(me, net, total, sq4, sq8, qsems)
+    parts = [pl.ds(0, seq), pl.ds(seq, seq), pl.ds(n_full, half_seq), pl.ds(n_own, half_seq)]
+    for i, ref in enumerate([peer_out] + [peer_dx.at[at] for at in parts] + [peer_small]):
+        net.arrived(ref, xs.at[i], xr.at[i])
+    for cp in keeps:
+        cp.wait()
+    net.end()
+
+
+def backward_fast(doc_ids, cotangent, doc_rows, saved, rows):
+    (qk, va, inner, outer, xt, q, k, v, p, o, xh1, r1, g, gp, xh2, r2, proj, vec, out_own) = saved
+    n_own, width = q.shape
+    n_all = k.shape[0]
+    half_ff = inner.shape[-1]
     zyc = (NZ, NY, NC)
-    arrays = [small.reshape(zyc + small.shape[1:])]
-    arrays += [g.reshape((2,) + zyc + (rows, g.shape[2])) for g in grads]
-    index = [
-        (4, 0, 4, 0, True),
-        (4, 1, 4, 1, True),
-        (3, 0, 3, 0, True),
-        (3, 1, 3, 1, True),
-        (2, 1, 2, 1, True),
-        (1, 0, 1, 0, True),
-        (1, 1, 1, 1, True),
-        (2, 0, 2, 0, True),
-        (0, None, 0, None, False),
+    hr = rows // NX
+    small_rows = 2 * hr + 8
+    ins = [doc_ids, cotangent, doc_rows] + list(saved)
+    out_shape = [
+        ((small_rows, 128), F32),
+        ((2, rows, width // 2), F32),
+        ((2, rows, width // 2), F32),
+        ((2, rows, half_ff // 2), F32),
+        ((2, rows, half_ff // 2), F32),
+        ((n_all, width), BF),
+        ((n_own, width), BF),
+        ((n_all, width), BF),
+        ((small_rows, 128), F32),
+        ((8, 128), F32),
     ]
-    n = len(index)
-    out_shape = [
-        jax.ShapeDtypeStruct((small.shape[1], small.shape[2] // 2), F32),
-    ] + [jax.ShapeDtypeStruct((2, rows, g.shape[2] // 2), F32) for g in grads]
-    out_shape += [
-        jax.ShapeDtypeStruct(own_out.shape, BF),
-        jax.ShapeDtypeStruct(own_dx.shape, BF),
-        jax.ShapeDtypeStruct((small.shape[1], small.shape[2] // 2), F32),
-        jax.ShapeDtypeStruct((8, 128), F32),
+    like = lambda a: (a.shape, a.dtype)
+    wide = width // 128 * 128
+    scratch = [
+        like(inner), like(outer), (va.shape[1:], BF), like(xt), like(q), like(k), like(v), like(o),
+        like(xh1), ((4,) + g.shape[1:], BF), like(xh2), like(r2), like(proj), like(vec),
+        ((3, 16, width), BF), ((n_own, width), BF), ((n_own, width), BF),
+        ((width, wide), BF),
+        ((16, width), F32), ((3, 8, width), F32), ((3, 8, width), F32), ((2, 8, half_ff), F32),
+        ((128, width), F32), (zyc + (small_rows, 256), F32),
     ]
-    bufs = []
-    for p, (i, _, _, _, _) in enumerate(index):
-        r, w = arrays[i].shape[-2:]
-        dt = arrays[i].dtype
-        bufs += [pltpu.VMEM((NZ, NY, r, w), dt), pltpu.VMEM((NZ, NY, r, w), dt)]
-        if p % 2 == 0:
-            bufs += [pltpu.VMEM((NZ, r, w), dt)]
-        else:
-            bufs += [pltpu.VMEM((NZ, NY, r, w // 2), dt)]
-        bufs += [pltpu.VMEM((NZ, r, w // 2), dt), pltpu.VMEM((NZ, r, w // 2), dt)]
+    sizes = [half_ff] * 4 + [width] * 4
+    scratch += [(zyc + (rows, w), BF) for w in sizes[:4]]
+    for i, (r, w, dt) in enumerate([(rows, w, BF) for w in sizes] + [(small_rows, 256, F32)]):
+        scratch.append(((NZ, NY, r, w), dt))
+        scratch.append((((NZ, r, w) if routes[i] == "y" else (NZ, NY, r, w // 2)), dt))
+        scratch.append(((NZ, r, w // 2), dt))
+        scratch.append(((NZ, r, w // 2), dt))
+    scratch += [((NZ, 8, 128), F32), ((8, 8, 128), F32)]
     vm = pl.BlockSpec(memory_space=pltpu.VMEM)
     hb = pl.BlockSpec(memory_space=ANY)
+    sm = pl.BlockSpec(memory_space=pltpu.SMEM)
+    n = 9
     return pl.pallas_call(
-        functools.partial(reduce_kernel, 7, len(out_shape), index),
-        out_shape=out_shape,
-        in_specs=[hb] * 7,
-        out_specs=[vm] * 5 + [hb, hb, vm, vm],
-        scratch_shapes=bufs
+        backward_kernel,
+        out_shape=[jax.ShapeDtypeStruct(s, d) for s, d in out_shape],
+        in_specs=[sm, hb, vm] + [hb] * 19,
+        out_specs=[vm] * 5 + [hb, hb, hb, vm, vm],
+        scratch_shapes=[pltpu.VMEM(s, d) for s, d in scratch]
         + [
-            pltpu.VMEM((NZ, 8, 128), F32), pltpu.VMEM((8, 8, 128), F32),
-            dma(n), dma(n), dma(n), dma(n), dma(n), dma(n), dma(n), dma(n, NZ), dma(n, NZ),
-            dma(3), dma(3), dma(NZ), dma(NZ), dma(8), dma(8),
+            dma(31), dma(n), dma(n), dma(n), dma(n), dma(n), dma(n), dma(n, NZ), dma(n, NZ),
+            dma(6), dma(6), dma(NZ), dma(NZ), dma(8), dma(8),
         ],
         compiler_params=pltpu.CompilerParams(
-            collective_id=2, has_side_effects=True, vmem_limit_bytes=56 * 2**20
+            collective_id=2, has_side_effects=True, vmem_limit_bytes=63 * 2**20
         ),
-        name="reduce",
-    )(*arrays, own_out, own_dx)
+        name="backward",
+    )(*ins)
 
 
 def gather_plain(shards, small, rows):
@@ -843,14 +1209,9 @@
     )
 
 
-def local(
-    tokens, cotangent, lengths, doc_ids, doc_rows,
-    w_qkv, m_qkv, v_qkv, w_attn, m_attn, v_attn, w_inner, m_inner, v_inner,
-    w_outer, m_outer, v_outer, w_proj, m_proj, v_proj, vectors, m_vectors, v_vectors,
-):
+def pass_plain(lengths, tokens, cotangent, doc_ids, doc_rows, w_qkv, w_attn, w_inner, w_outer, w_proj, vectors):
     mp = lax.axis_index("mp")
     n_dp, n_mp = lax.axis_size("dp"), lax.axis_size("mp")
-    fast = n_dp == NZ * NY * NC and n_mp == NX
     seqs = lengths.shape[0]
     all_rows, width = tokens.shape
     seq_len = all_rows // seqs
@@ -863,8 +1224,7 @@
     ff_rows = nvec - 8
     score_scale = HEAD_DIM ** (-0.5)
 
-    forward = forward_fast if fast else forward_plain
-    saved = forward(lengths, tokens, w_qkv, w_attn, w_inner, w_outer, w_proj, vectors)
+    saved = forward_plain(lengths, tokens, w_qkv, w_attn, w_inner, w_outer, w_proj, vectors)
     (qk, va, inner, outer, x_all, q, k, v, p_ab, p_c, mixed, xh1, r1, act_low, slope, xh2, r2, proj, vec, out_own) = saved
     qk = qk.reshape(2, width, width)
     va = va.reshape(2, width, width)
@@ -963,10 +1323,43 @@
     tg = table_local.reshape(n_dp, 2, TAB_DEV // 2, 128).transpose(0, 2, 1, 3).reshape(n_dp, TAB_DEV // 2, 256)
     small = jnp.concatenate([pg, vg, tg], axis=1)
 
-    reduce = reduce_fast if fast else reduce_plain
-    (small_r, qk_r, va_r, inner_r, outer_r, peer_out, peer_dx, peer_small, total) = reduce(
-        [g_qk, g_va, g_inner, g_outer], small, out_own, dx, rows
-    )
+    return out_own, dx, *reduce_plain([g_qk, g_va, g_inner, g_outer], small, out_own, dx, rows)
+
+
+def local(
+    tokens, cotangent, lengths, doc_ids, doc_rows,
+    w_qkv, m_qkv, v_qkv, w_attn, m_attn, v_attn, w_inner, m_inner, v_inner,
+    w_outer, m_outer, v_outer, w_proj, m_proj, v_proj, vectors, m_vectors, v_vectors,
+):
+    mp = lax.axis_index("mp")
+    n_dp, n_mp = lax.axis_size("dp"), lax.axis_size("mp")
+    fast = n_dp == NZ * NY * NC and n_mp == NX
+    seqs = lengths.shape[0]
+    all_rows, width = tokens.shape
+    seq_len = all_rows // seqs
+    full = seqs // 2
+    n_full, n_half = full * seq_len, seq_len // 2
+    n_own = n_full + n_half
+    rows, half_ff = w_qkv.shape[1], w_inner.shape[1]
+    half_rows = rows // 2
+    nvec, vec_lanes = vectors.shape
+    ff_rows = nvec - 8
+    score_scale = HEAD_DIM ** (-0.5)
+
+    if fast:
+        saved = forward_fast(lengths, tokens, w_qkv, w_attn, w_inner, w_outer, w_proj, vectors)
+        out_own = saved[-1]
+        (small_r, qk_r, va_r, inner_r, outer_r, dx, peer_out, peer_dx, peer_small, total) = backward_fast(
+            doc_ids, cotangent, doc_rows, saved, rows
+        )
+        vector_r = small_r[half_rows : half_rows + vec_lanes, :nvec].T
+        table_at = half_rows + vec_lanes
+    else:
+        (out_own, dx, small_r, qk_r, va_r, inner_r, outer_r, peer_out, peer_dx, peer_small, total) = pass_plain(
+            lengths, tokens, cotangent, doc_ids, doc_rows, w_qkv, w_attn, w_inner, w_outer, w_proj, vectors
+        )
+        vector_r = small_r[half_rows : half_rows + nvec, :vec_lanes]
+        table_at = half_rows + nvec
 
     def whole_rows(own, peer):
         lo = jnp.where(mp == 0, own[:n_own], peer[:n_own])
@@ -989,8 +1382,7 @@
         )
 
     proj_r = both_halves(0, half_rows)
-    table_grad = both_halves(half_rows + nvec, TAB_DEV // 2)
-    vector_r = small_r[half_rows : half_rows + nvec, :vec_lanes]
+    table_grad = both_halves(table_at, TAB_DEV // 2)
     qkv_r = jnp.stack([qk_r[0], qk_r[1], va_r[0]])
     attn_r = va_r[1]
 

time: 423 us -> 288 us (0.68); the launches traced: 415 us -> 287 us
  local copies, waits for them, and re-layouts: 73.1 us -> 3.97 us
  matrix products: 63.1 us -> 0 us
  Pallas kernels: 240 us -> 268 us
  other arithmetic: 34.7 us -> 12.8 us
    dot_general x26 -> x0, matrix products: 63.1 us -> none  [the longest x2 7.49 us: local(): jnp.einsum('ghqk,gqhe->gkhe', ds_, qh, preferred_element_type=F32)]
    reshape x10 -> x0, local copies, waits for them, and re-layouts: 31.4 us -> none  [the longest x5 17.3 us: halves(): t[:n_full].reshape(n_full // seq_len, seq_len, heads, HEAD_DIM)]
    pallas_call x1, Pallas kernels: 133 us -> 161 us  [backward_fast(): pl.pallas_call(backward_kernel, out_shape=[jax.ShapeDtypeStruct(s, d) for...]
    slice x17 -> x0, local copies, waits for them, and re-layouts: 17.6 us -> none  [the longest x8 5.39 us: halves(): t[n_full:].reshape(1, last, heads, HEAD_DIM)]
    convert_element_type x4 -> x0, other arithmetic: 10.2 us -> none  [the longest x2 10 us: local(): ds_ = (probs * (dp_ - delta)).astype(BF)]
    concatenate x14 -> x0, local copies, waits for them, and re-layouts: 7.3 us -> none  [the longest x10 5.2 us: local(): jnp.concatenate([jnp.stack([jnp.sum(dq.astype(F32), axis=0), jnp.sum(dv.a...]
    reduce_sum x6 -> x0, other arithmetic: 4.8 us -> none  [the longest x1 2.47 us: norm_back(): return (back_ * root[:, :1], jnp.sum(dy * hat, axis=0), jnp.sum(dy, axis=0))]
where the time goes in v3:
time: 288 us; the launch traced here: 287 us
  Pallas kernels  268 us (93%)
  other arithmetic  12.8 us (4%)
  local copies, waits for them, and re-layouts  3.97 us (1%)
  between operations  2.89 us (1%)
    pallas_call x1, Pallas kernels, backward_fast(): pl.pallas_call(backward_kernel, out_shape=[jax.ShapeDtypeStruct(s, d) for...  161 us
    pallas_call x1, Pallas kernels, forward_fast(): pl.pallas_call(forward_kernel, out_shape=[jax.ShapeDtypeStruct(s, d) for...  106 us

profile of v3, /device:TPU:0, one launch (start us, length us, event | category | flops | bytes accessed | tf_op | source)
XLA Modules:
  0.0 287.4 jit_solution(844373867076782161)
XLA Ops:
  0.7 106.5 %forward.1 = (bf16[2,4,2,2,48,768]{5,4,3,2,1,0:T(8,128)(2,1)}, bf16[2,4,2,2,48,768]{5,4,3,2,1,0:T(8,128)(2,1)}, bf16[2,4,2,2,48,1536]{5,4,3,2,1,0:T(8,128)(2,1)}...) custom-call(s32[5]{0:T(128)} %refs_0_.2, ...), custom_call_target="tpu_custom_call" | custom-call | tf_op jit(solution)/shard_map/forward/pallas_call | solution.py:519
  107.1 0.0 copy-start.22
  107.1 0.0 copy-start.23
  107.2 0.0 copy-start.19
  107.2 0.0 copy-start.16
  107.2 0.0 copy-start.20
  107.2 0.0 copy-start.21
  107.2 161.2 %backward.1 = (f32[56,128]{1,0:T(8,128)}, f32[2,48,384]{2,1,0:T(8,128)}, f32[2,48,384]{2,1,0:T(8,128)}, f32[2,48,768]{2,1,0:T(8,128)}, f32[2,48,768]{2,1,0:T(8,1...) custom-call(s32[5,8]{1,0:T(8,128)} %refs_0_.3, ...), custom_call_target="tpu_custom_call" | custom-call | tf_op jit(solution)/shard_map/backward/pallas_call | solution.py:1080
  268.4 0.0 copy-start.3
  268.5 0.0 copy-start.7
  268.5 0.0 copy-start.8
  268.5 0.8 slice_select_fusion.3
  269.2 0.6 pad_maximum_fusion.2
  269.8 1.2 slice.79
  271.8 0.0 copy-done.22
  271.8 0.1 copy.63
  271.9 0.0 copy-done.23
  271.9 0.1 copy.65
  271.9 0.0 copy-done.19
  271.9 0.1 copy.67
  272.0 0.7 multiply_subtract_fusion.5
  272.8 0.7 copy.68
  273.4 0.7 copy.69
  274.1 0.7 copy.70
  274.8 0.7 slice_select_fusion.1
  275.5 0.6 multiply_subtract_fusion.4
  276.2 1.2 multiply_bitcast_fusion
  277.4 0.0 copy-start.11
  277.4 0.0 copy-start.17
  277.4 0.0 copy-start.18
  277.5 0.0 copy-start.6
  277.5 0.0 copy-start.12
  277.5 0.0 copy-start.13
  277.5 0.0 copy-start.15
  277.5 1.0 multiply_subtract_fusion
  278.6 1.0 multiply_subtract_fusion.1
  279.7 0.0 copy-done.14
  279.7 0.7 multiply_subtract_fusion.3
  280.4 0.9 multiply_subtract_fusion.2
  281.4 0.3 convert_select_fusion.1
  281.7 0.1 slice_add_fusion.1
  281.8 0.1 slice.89
  281.9 0.1 slice.92
  282.1 2.4 pad_maximum_fusion
  284.5 0.0 copy-done.5
  284.5 0.1 broadcast_select_fusion.1
  284.6 0.1 slice.88
  284.7 1.5 pad_maximum_fusion.1
  (31 shorter events, 0.1 us)
Async XLA Ops:
  107.1 164.6 %copy-start.22 = (f32[12,24]{1,0:T(8,128)S(1)}, f32[12,24]{1,0:T(8,128)}, u32[]{:S(2)}) copy-start(f32[12,24]{1,0:T(8,128)} %param.44) | copy-start | bytes 3460
  107.1 164.7 %copy-start.23 = (f32[12,24]{1,0:T(8,128)S(1)}, f32[12,24]{1,0:T(8,128)}, u32[]{:S(2)}) copy-start(f32[12,24]{1,0:T(8,128)} %param.45) | copy-start | bytes 3460
  107.2 164.8 %copy-start.19 = (f32[12,24]{1,0:T(8,128)S(1)}, f32[12,24]{1,0:T(8,128)}, u32[]{:S(2)}) copy-start(f32[12,24]{1,0:T(8,128)} %refs_7_.1) | copy-start | bytes 3460
  107.2 168.4 %copy-start.16 = (f32[48,128]{1,0:T(8,128)S(1)}, f32[48,128]{1,0:T(8,128)}, u32[]{:S(2)}) copy-start(f32[48,128]{1,0:T(8,128)} %refs_6_.1) | copy-start | bytes 73732
  107.2 168.3 %copy-start.20 = (f32[48,128]{1,0:T(8,128)S(1)}, f32[48,128]{1,0:T(8,128)}, u32[]{:S(2)}) copy-start(f32[48,128]{1,0:T(8,128)} %param.42) | copy-start | bytes 73732
  107.2 168.3 %copy-start.21 = (f32[48,128]{1,0:T(8,128)S(1)}, f32[48,128]{1,0:T(8,128)}, u32[]{:S(2)}) copy-start(f32[48,128]{1,0:T(8,128)} %param.41) | copy-start | bytes 73732
  268.4 8.9 %copy-start.3 = (f32[48,1536]{1,0:T(8,128)S(1)}, f32[48,1536]{1,0:T(8,128)}, u32[]{:S(2)}) copy-start(f32[48,1536]{1,0:T(8,128)} %refs_5_.1) | copy-start | bytes 884740
  268.5 8.9 %copy-start.7 = (f32[48,1536]{1,0:T(8,128)S(1)}, f32[48,1536]{1,0:T(8,128)}, u32[]{:S(2)}) copy-start(f32[48,1536]{1,0:T(8,128)} %param.39) | copy-start | bytes 884740
  268.5 8.9 %copy-start.8 = (f32[48,1536]{1,0:T(8,128)S(1)}, f32[48,1536]{1,0:T(8,128)}, u32[]{:S(2)}) copy-start(f32[48,1536]{1,0:T(8,128)} %param.38) | copy-start | bytes 884740
  276.2 2.4 copy-start.4
  276.2 2.4 copy-start.9
  276.2 2.4 copy-start.10
  277.4 2.3 copy-start.11
  277.4 2.3 copy-start.14
  277.4 2.2 copy-start.17
  277.4 2.2 copy-start.18
  277.5 3.0 %copy-start.6 = (f32[3,48,384]{2,1,0:T(8,128)S(1)}, f32[3,48,384]{2,1,0:T(8,128)}, u32[]{:S(2)}) copy-start(f32[3,48,384]{2,1,0:T(8,128)} %refs_2_.2) | copy-start | bytes 663556
  277.5 2.9 %copy-start.12 = (f32[3,48,384]{2,1,0:T(8,128)S(1)}, f32[3,48,384]{2,1,0:T(8,128)}, u32[]{:S(2)}) copy-start(f32[3,48,384]{2,1,0:T(8,128)} %param.30) | copy-start | bytes 663556
  277.5 2.9 %copy-start.13 = (f32[3,48,384]{2,1,0:T(8,128)S(1)}, f32[3,48,384]{2,1,0:T(8,128)}, u32[]{:S(2)}) copy-start(f32[3,48,384]{2,1,0:T(8,128)} %param.29) | copy-start | bytes 663556
  277.5 2.9 %copy-start.15 = (f32[2,48,384]{2,1,0:T(8,128)S(1)}, f32[2,48,384]{2,1,0:T(8,128)}, u32[]{:S(2)}) copy-start(f32[2,48,384]{2,1,0:T(8,128)} %get-tuple-element.74) | copy-start | bytes 442372
  278.6 2.8 copy-start.1
  278.6 2.8 copy-start.2
  282.1 2.4 copy-start
  282.1 2.4 copy-start.5

commit v4 on v3

--- a/solution.py
+++ b/solution.py
@@ -139,6 +139,9 @@
     lax.fori_loop(0, n, lambda i, c: (body(i), c)[1], 0)
 
 
+gather_routes = "xxyxyxyxy"
+
+
 class Gather:
     def __init__(self, me, pieces, sems):
         self.me, self.pieces = me, pieces
@@ -166,7 +169,7 @@
         own, other = cols(me.x, half), cols(1 - me.x, half)
         if stage == "z":
             return dst.at[:, me.y, c, :, own]
-        if p % 2 == 0:
+        if gather_routes[p] == "x":
             if stage == "in1":
                 return dst.at[:, me.y, c, :, other]
             if stage == "out2":
@@ -179,10 +182,10 @@
         return dst.at[:, :, c, :, other]
 
     def first(self, p):
-        return self.me.dev(x=1 - self.me.x) if p % 2 == 0 else self.me.dev(y=1 - self.me.y)
+        return self.me.dev(x=1 - self.me.x) if gather_routes[p] == "x" else self.me.dev(y=1 - self.me.y)
 
     def second(self, p):
-        return self.me.dev(y=1 - self.me.y) if p % 2 == 0 else self.me.dev(x=1 - self.me.x)
+        return self.me.dev(y=1 - self.me.y) if gather_routes[p] == "x" else self.me.dev(x=1 - self.me.x)
 
     def cross(self, p, ref, which):
         self.go(remote(ref, ref, self.ds.at[p, which], self.dr.at[p, which], self.me.dev(c=1 - self.me.c)))
@@ -215,19 +218,6 @@
     def step5(self, p):
         for which, stage in enumerate(("z", "in1", "in2")):
             self.arrived(self.part(p, stage, 1 - self.me.c), self.ds.at[p, which], self.dr.at[p, which])
-
-    def tick(self, t, ahead):
-        n = len(self.pieces)
-        if t < n:
-            self.step2(t)
-            if t + ahead < n:
-                self.step1(t + ahead)
-        if 0 <= t - 1 < n:
-            self.step3(t - 1)
-        if 0 <= t - 2 < n:
-            self.step4(t - 2)
-        if 0 <= t - 3 < n:
-            self.step5(t - 3)
 
     def end(self):
         for copy in self.waits:
@@ -309,10 +299,14 @@
         (outer_s.at[1], outer.at[1]),
     ]
     net = Gather(me, pieces, gsems)
-    ahead = 3
-    for i in range(ahead):
-        net.step1(i)
-    tick = lambda t: net.tick(t, ahead)
+    groups = ((0, 1, 2), (3, 4), (5, 6), (7, 8))
+
+    def go(step, i):
+        for piece in groups[i]:
+            (net.step1, net.step2, net.step3, net.step4, net.step5)[step - 1](piece)
+
+    go(1, 0)
+    go(1, 1)
     saves = []
 
     def save(i, ref):
@@ -328,8 +322,15 @@
 
     each(width // 256, x_turn)
     save(4, xt)
-    for t in range(4):
-        tick(t)
+    go(2, 0)
+    go(1, 2)
+    go(3, 0)
+    go(2, 1)
+    go(1, 3)
+    go(4, 0)
+    go(3, 1)
+    go(2, 2)
+    go(5, 0)
     big = []
     for z in range(NZ):
         for y in range(NY):
@@ -358,12 +359,12 @@
 
         each(width // n_tile, body)
 
-    tick(4)
     project(qk.at[0], n_own, q, 0)
-    tick(5)
     project(qk.at[1], n_all, k, None)
     save(0, qk)
-    tick(6)
+    go(4, 1)
+    go(2, 3)
+    go(5, 1)
     project(va.at[0], n_all, v, 1)
     save(5, q)
     save(6, k)
@@ -395,13 +396,12 @@
     for s in range(full):
         length = lens[mp * (full + 1) + s]
         each(slabs, lambda i: attend(s * seq, seq, s * seq, i, length, pos))
-        tick(7 + s)
+        go(3, 2 + s)
     length = lens[full]
     pos_c = jnp.where(pos < half_seq, pos + mp * half_seq, pos - half_seq + (1 - mp) * half_seq)
     each(slabs, lambda i: attend(n_full, half_seq, n_full, i, length, pos_c))
     save(8, p)
     save(9, o)
-    tick(7 + full)
 
     tile = 240
     tiles = n_own // tile
@@ -419,7 +419,8 @@
     norm_rows(xh1, r1, n_own, put_h1)
     save(10, xh1)
     save(11, r1)
-    tick(8 + full)
+    go(4, 2)
+    go(5, 2)
 
     def feed(h):
         n_tile = 256
@@ -438,10 +439,9 @@
         each(half_ff // n_tile, body)
 
     feed(0)
-    tick(9 + full)
     feed(1)
-    for t in range(10 + full, len(pieces) + 3):
-        tick(t)
+    go(4, 3)
+    go(5, 3)
     save(2, inner)
     save(12, g)
     save(13, gp)
@@ -624,7 +624,7 @@
             copy.wait_send()
 
 
-routes = ("x", "y", "x", "x", "x", "y", "y", "y", "y")
+routes = "yyyyyyyyy"
 
 
 def all_squares(me, net, total, sq4, sq8, sems):
@@ -1092,6 +1092,113 @@
         ),
         name="backward",
     )(*ins)
+
+
+def finish_kernel(*refs):
+    small_r, peer_small, qk_r, va_r, inner_r, outer_r, total = refs[:7]
+    out_own, peer_out, dx, peer_dx = refs[7:11]
+    params = [refs[11 + 3 * i : 14 + 3 * i] for i in range(6)]
+    outs = refs[29:51]
+    turn, sem, lo, hi, mid = refs[51:]
+    out_tokens, input_grad, norm = outs[0:3]
+    news = [outs[3 + 3 * i : 6 + 3 * i] for i in range(6)]
+    table_grad = outs[21]
+    mp = lax.axis_index("mp")
+    n_own = out_own.shape[0]
+    n_all = dx.shape[0]
+    half_seq = n_all - n_own
+    n_full = n_own - half_seq
+    seq = 2 * half_seq
+    copies = []
+    for i, (src, first) in enumerate(((out_own, mp), (peer_out, 1 - mp))):
+        at = pl.multiple_of(first * (n_full + seq), 16)
+        copies.append((src.at[pl.ds(0, n_full)], out_tokens.at[pl.ds(at, n_full)]))
+        at = pl.multiple_of(n_full + first * half_seq, 16)
+        copies.append((src.at[pl.ds(n_full, half_seq)], out_tokens.at[pl.ds(at, half_seq)]))
+    copies = [pltpu.make_async_copy(s, d, sem.at[i]) for i, (s, d) in enumerate(copies)]
+    for cp in copies:
+        cp.start()
+    lo[...] = dx[0:n_full].astype(F32)
+    hi[...] = peer_dx[0:n_full].astype(F32)
+    own_mid = dx[n_full:n_own].astype(F32) + peer_dx[n_own:n_all].astype(F32)
+    peer_mid = peer_dx[n_full:n_own].astype(F32) + dx[n_own:n_all].astype(F32)
+    mid[pl.ds(pl.multiple_of(mp * half_seq, 16), half_seq)] = own_mid
+    mid[pl.ds(pl.multiple_of((1 - mp) * half_seq, 16), half_seq)] = peer_mid
+    grads = (
+        (lo, pl.multiple_of(mp * (n_full + seq), 16), n_full),
+        (hi, pl.multiple_of((1 - mp) * (n_full + seq), 16), n_full),
+        (mid, n_full, seq),
+    )
+    for i, (src, at, n) in enumerate(grads):
+        cp = pltpu.make_async_copy(src, input_grad.at[pl.ds(at, n)], sem.at[4 + i])
+        cp.start()
+        copies.append(cp)
+
+    root = jnp.sqrt(total[...])
+    norm[0, 0] = jnp.max(root)
+    clip = clip_norm / jnp.maximum(root[0:1, 0:1], clip_norm)
+    hf = inner_r.shape[-1]
+    hr = params[4][0].shape[0] // 2
+    nvec, nlane = params[5][0].shape
+    tr = table_grad.shape[0] // 2
+
+    def adam(which, at, g, dec, rate):
+        w, m, s = (ref[at] for ref in params[which])
+        for ref, new in zip(news[which], adamw_update(w, m, s, g * clip, dec, rate)):
+            ref[at] = new
+
+    for j in range(3):
+        g = qk_r[j] if j < 2 else va_r[0]
+        adam(0, (j,), g, decay_rate, learn_rate)
+    adam(1, (slice(None), slice(None)), va_r[1], decay_rate, learn_rate)
+    for which, ref in ((2, inner_r), (3, outer_r)):
+        for h in range(2):
+            adam(which, (slice(None), slice(h * hf, (h + 1) * hf)), ref[h], decay_rate, learn_rate)
+    turn[...] = jnp.zeros_like(turn)
+    turn[0:nlane] = small_r[hr : hr + nlane]
+    adam(5, (slice(None), slice(None)), jnp.transpose(turn[...])[0:nvec, 0:nlane], 0.0, vector_rate)
+    for block, first in ((small_r, mp), (peer_small, 1 - mp)):
+        at = pl.ds(pl.multiple_of(first * hr, 8), hr)
+        adam(4, (at, slice(None)), block[0:hr], decay_rate, learn_rate)
+    own_t, peer_t = small_r[hr + nlane : hr + nlane + tr], peer_small[hr + nlane : hr + nlane + tr]
+    table_grad[0:tr] = jnp.where(mp == 0, own_t, peer_t)
+    table_grad[tr : 2 * tr] = jnp.where(mp == 0, peer_t, own_t)
+    for cp in copies:
+        cp.wait()
+
+
+def finish_fast(reduced, out_own, params, n_rows):
+    (small_r, qk_r, va_r, inner_r, outer_r, dx, peer_out, peer_dx, peer_small, total) = reduced
+    n_own, width = out_own.shape
+    n_all = dx.shape[0]
+    half_seq = n_all - n_own
+    like = lambda a: jax.ShapeDtypeStruct(a.shape, a.dtype)
+    vm = pl.BlockSpec(memory_space=pltpu.VMEM)
+    hb = pl.BlockSpec(memory_space=ANY)
+    sm = pl.BlockSpec(memory_space=pltpu.SMEM)
+    out_shape = [
+        jax.ShapeDtypeStruct((n_rows, width), BF),
+        jax.ShapeDtypeStruct((n_rows, width), F32),
+        jax.ShapeDtypeStruct((1, 1), F32),
+    ]
+    out_shape += [like(a) for a in params] + [jax.ShapeDtypeStruct((TAB_DEV, 128), F32)]
+    n_full = n_own - half_seq
+    outs = pl.pallas_call(
+        finish_kernel,
+        out_shape=out_shape,
+        in_specs=[vm] * 29,
+        out_specs=[hb, hb, sm] + [vm] * 19,
+        scratch_shapes=[
+            pltpu.VMEM((128, 128), F32),
+            dma(7),
+            pltpu.VMEM((n_full, width), F32),
+            pltpu.VMEM((n_full, width), F32),
+            pltpu.VMEM((2 * half_seq, width), F32),
+        ],
+        compiler_params=pltpu.CompilerParams(vmem_limit_bytes=63 * 2**20),
+        name="finish",
+    )(small_r, peer_small, qk_r, va_r, inner_r, outer_r, total, out_own, peer_out, dx, peer_dx, *params)
+    return tuple(outs[:2]) + (outs[2].reshape(()),) + tuple(outs[3:])
 
 
 def gather_plain(shards, small, rows):
@@ -1348,13 +1455,11 @@
 
     if fast:
         saved = forward_fast(lengths, tokens, w_qkv, w_attn, w_inner, w_outer, w_proj, vectors)
-        out_own = saved[-1]
-        (small_r, qk_r, va_r, inner_r, outer_r, dx, peer_out, peer_dx, peer_small, total) = backward_fast(
-            doc_ids, cotangent, doc_rows, saved, rows
-        )
-        vector_r = small_r[half_rows : half_rows + vec_lanes, :nvec].T
-        table_at = half_rows + vec_lanes
-    else:
+        reduced = backward_fast(doc_ids, cotangent, doc_rows, saved, rows)
+        params = (w_qkv, m_qkv, v_qkv, w_attn, m_attn, v_attn, w_inner, m_inner, v_inner)
+        params += (w_outer, m_outer, v_outer, w_proj, m_proj, v_proj, vectors, m_vectors, v_vectors)
+        return finish_fast(reduced, saved[-1], params, all_rows)
+    if not fast:
         (out_own, dx, small_r, qk_r, va_r, inner_r, outer_r, peer_out, peer_dx, peer_small, total) = pass_plain(
             lengths, tokens, cotangent, doc_ids, doc_rows, w_qkv, w_attn, w_inner, w_outer, w_proj, vectors
         )

time: 288 us -> 248 us (0.86)
  Pallas kernels: 268 us -> 247 us
  other arithmetic: 12.8 us -> 0 us
  local copies, waits for them, and re-layouts: 3.97 us -> 0 us
    pallas_call x1, Pallas kernels: 161 us -> 146 us  [backward_fast(): pl.pallas_call(backward_kernel, out_shape=[jax.ShapeDtypeStruct(s, d) for...]
    pallas_call x1, Pallas kernels: 106 us -> 93.1 us  [forward_fast(): pl.pallas_call(forward_kernel, out_shape=[jax.ShapeDtypeStruct(s, d) for...]
    pallas_call x0 -> x1, Pallas kernels: none -> 7.99 us  [finish_fast(): pl.pallas_call(finish_kernel, out_shape=out_shape, in_specs=[vm] * 29, ou...]
    sub x6 -> x0, other arithmetic: 5.12 us -> none  [adamw_update(): weight - step_rate * (first_hat / (jnp.sqrt(second_hat) + adam_epsilon) +...]
    concatenate x3 -> x0, other arithmetic: 4.48 us -> none  [the longest x1 2.37 us: local(): jnp.concatenate([lo[:n_full], lo[n_full:] + tail_hi, hi[n_full:] + tail,...]
where the time goes in v4:
time: 248 us
  Pallas kernels  247 us (100%)
    pallas_call x1, Pallas kernels, backward_fast(): pl.pallas_call(backward_kernel, out_shape=[jax.ShapeDtypeStruct(s, d) for...  146 us
    pallas_call x1, Pallas kernels, forward_fast(): pl.pallas_call(forward_kernel, out_shape=[jax.ShapeDtypeStruct(s, d) for...  93.1 us
    pallas_call x1, Pallas kernels, finish_fast(): pl.pallas_call(finish_kernel, out_shape=out_shape, in_specs=[vm] * 29, ou...  7.99 us

profile of v4, /device:TPU:0, one launch (start us, length us, event | category | flops | bytes accessed | tf_op | source)
XLA Modules:
  0.0 247.9 jit_solution(1561434514818073216)
XLA Ops:
  0.7 93.1 %forward.1 = (bf16[2,4,2,2,48,768]{5,4,3,2,1,0:T(8,128)(2,1)}, bf16[2,4,2,2,48,768]{5,4,3,2,1,0:T(8,128)(2,1)}, bf16[2,4,2,2,48,1536]{5,4,3,2,1,0:T(8,128)(2,1)}...) custom-call(s32[5]{0:T(128)} %refs_0_.2, ...), custom_call_target="tpu_custom_call" | custom-call | tf_op jit(solution)/shard_map/forward/pallas_call | solution.py:519
  93.7 146.0 %backward.1 = (f32[56,128]{1,0:T(8,128)}, f32[2,48,384]{2,1,0:T(8,128)}, f32[2,48,384]{2,1,0:T(8,128)}, f32[2,48,768]{2,1,0:T(8,128)}, f32[2,48,768]{2,1,0:T(8,1...) custom-call(s32[5,8]{1,0:T(8,128)} %refs_0_.3, ...), custom_call_target="tpu_custom_call" | custom-call | tf_op jit(solution)/shard_map/backward/pallas_call | solution.py:1080
  239.8 8.0 %finish.1 = (bf16[1440,768]{1,0:T(8,128)(2,1)}, f32[1440,768]{1,0:T(8,128)}, f32[1,1]{1,0:T(1,128)}, f32[3,48,384]{2,1,0:T(8,128)}, f32[3,48,384]{2,1,0:T(8,128)...) custom-call(f32[56,128]{1,0:T(8,128)} %get-tuple-element.92.refs_0_,, ...), custom_call_target="tpu_custom_call" | custom-call | tf_op jit(solution)/shard_map/finish/pallas_call | solution.py:1186

commit v5 on v4

--- a/solution.py
+++ b/solution.py
@@ -97,6 +97,16 @@
     pl.semaphore_wait(barrier, len(devices))
 
 
+def greet_send(devices):
+    barrier = pltpu.get_barrier_semaphore()
+    for d in devices:
+        pl.semaphore_signal(barrier, inc=1, device_id=d, device_id_type=MESH)
+
+
+def greet_wait(count):
+    pl.semaphore_wait(pltpu.get_barrier_semaphore(), count)
+
+
 def remote(src, dst, ssem, rsem, dev):
     return pltpu.make_async_remote_copy(
         src_ref=src, dst_ref=dst, send_sem=ssem, recv_sem=rsem, device_id=dev, device_id_type=MESH
@@ -139,89 +149,100 @@
     lax.fori_loop(0, n, lambda i, c: (body(i), c)[1], 0)
 
 
-gather_routes = "xxyxyxyxy"
+gather_orders = ("zxy", "zxy", "zyx", "zxy", "zyx", "zxy", "zyx", "zxy", "zyx", "zxy", "zyx", "zxy", "xyz", "yxz", "zyx")
 
 
 class Gather:
     def __init__(self, me, pieces, sems):
         self.me, self.pieces = me, pieces
-        self.lsem, self.zs, self.zr, self.s1, self.r1, self.s2, self.r2, self.ds, self.dr = sems
+        self.lsem, self.ss, self.rs, self.ds, self.dr = sems
         self.waits, self.locs = [], {}
 
-    def go(self, copy):
-        copy.start()
-        self.waits.append(copy)
+    def region(self, p, stage, c, **at):
+        dst, me, done = self.pieces[p][1], self.me, gather_orders[p][:stage]
+        half = dst.shape[-1] // 2
+        z = at.get("z", None if "z" in done else me.z)
+        y = at.get("y", None if "y" in done else me.y)
+        x = at.get("x", None if "x" in done else me.x)
+        zs = slice(None) if z is None else pl.ds(0, NZ - 1) if z == "three" else pl.ds(z, 1)
+        ys = slice(None) if y is None else pl.ds(y, 1)
+        xs = slice(None) if x is None else cols(x, half)
+        return dst.at[zs, ys, c, :, xs]
+
+    def bulk(self, p, stage, c):
+        axis = gather_orders[p][stage]
+        return self.region(p, stage, c, z="three") if axis == "z" else self.coming(p, stage, c)[0]
+
+    def coming(self, p, stage, c):
+        me, axis = self.me, gather_orders[p][stage]
+        if axis == "z":
+            return [self.region(p, stage, c, z=lax.rem(me.z + NZ - k, NZ)) for k in range(1, NZ)]
+        return [self.region(p, stage, c, **{axis: 1 - (me.y if axis == "y" else me.x)})]
+
+    def send(self, p, stage):
+        me, axis = self.me, gather_orders[p][stage]
+        src, dst = self.pieces[p]
+        if stage == 0:
+            to = dst.at[me.z, me.y, me.c, :, cols(me.x, dst.shape[-1] // 2)]
+        else:
+            src = to = self.region(p, stage, me.c)
+        if axis == "z":
+            devs = [me.dev(z=lax.rem(me.z + k, NZ)) for k in range(1, NZ)]
+        else:
+            devs = [me.dev(**{axis: 1 - (me.y if axis == "y" else me.x)})]
+        for dev in devs:
+            remote(src, to, self.ss.at[p, stage], self.rs.at[p, stage], dev).start()
+        self.waits.append((self.bulk(p, stage, me.c), self.ss.at[p, stage]))
+
+    def arrived(self, ref, sem):
+        remote(ref, ref, sem, sem, self.me.dev(c=1 - self.me.c)).wait_recv()
+
+    def receive(self, p, stage):
+        self.arrived(self.bulk(p, stage, self.me.c), self.rs.at[p, stage])
+
+    def crossing(self, p, stage, c):
+        if stage == 0:
+            ref = self.region(p, 1, c)
+            return [ref], ref
+        return self.coming(p, stage, c), self.bulk(p, stage, c)
+
+    def cross(self, p, stage):
+        refs, whole = self.crossing(p, stage, self.me.c)
+        for ref in refs:
+            remote(ref, ref, self.ds.at[p, stage], self.dr.at[p, stage], self.me.dev(c=1 - self.me.c)).start()
+        self.waits.append((whole, self.ds.at[p, stage]))
 
     def step1(self, p):
         me = self.me
         src, dst = self.pieces[p]
+        self.send(p, 0)
         blk = dst.at[me.z, me.y, me.c, :, cols(me.x, dst.shape[-1] // 2)]
         loc = pltpu.make_async_copy(src, blk, self.lsem.at[p])
         loc.start()
         self.locs[p] = loc
-        for k in range(1, NZ):
-            dev = me.dev(z=lax.rem(me.z + k, NZ))
-            self.go(remote(src, blk, self.zs.at[p, k], self.zr.at[p, k], dev))
-
-    def part(self, p, stage, c):
-        me, dst = self.me, self.pieces[p][1]
-        half = dst.shape[-1] // 2
-        own, other = cols(me.x, half), cols(1 - me.x, half)
-        if stage == "z":
-            return dst.at[:, me.y, c, :, own]
-        if gather_routes[p] == "x":
-            if stage == "in1":
-                return dst.at[:, me.y, c, :, other]
-            if stage == "out2":
-                return dst.at[:, me.y, c]
-            return dst.at[:, 1 - me.y, c]
-        if stage == "in1":
-            return dst.at[:, 1 - me.y, c, :, own]
-        if stage == "out2":
-            return dst.at[:, :, c, :, own]
-        return dst.at[:, :, c, :, other]
-
-    def first(self, p):
-        return self.me.dev(x=1 - self.me.x) if gather_routes[p] == "x" else self.me.dev(y=1 - self.me.y)
-
-    def second(self, p):
-        return self.me.dev(y=1 - self.me.y) if gather_routes[p] == "x" else self.me.dev(x=1 - self.me.x)
-
-    def cross(self, p, ref, which):
-        self.go(remote(ref, ref, self.ds.at[p, which], self.dr.at[p, which], self.me.dev(c=1 - self.me.c)))
-
-    def arrived(self, ref, ssem, rsem):
-        remote(ref, ref, ssem, rsem, self.me.dev(c=1 - self.me.c)).wait_recv()
 
     def step2(self, p):
-        me, dst = self.me, self.pieces[p][1]
         self.locs[p].wait()
-        for k in range(1, NZ):
-            blk = dst.at[lax.rem(me.z + NZ - k, NZ), me.y, me.c, :, cols(me.x, dst.shape[-1] // 2)]
-            self.arrived(blk, self.zs.at[p, k], self.zr.at[p, k])
-        have = self.part(p, "z", me.c)
-        self.go(remote(have, have, self.s1.at[p], self.r1.at[p], self.first(p)))
-        self.cross(p, have, 0)
+        self.receive(p, 0)
+        self.send(p, 1)
+        self.cross(p, 0)
 
     def step3(self, p):
-        got = self.part(p, "in1", self.me.c)
-        self.arrived(got, self.s1.at[p], self.r1.at[p])
-        have = self.part(p, "out2", self.me.c)
-        self.go(remote(have, have, self.s2.at[p], self.r2.at[p], self.second(p)))
-        self.cross(p, got, 1)
+        self.receive(p, 1)
+        self.send(p, 2)
+        self.cross(p, 1)
 
     def step4(self, p):
-        got = self.part(p, "in2", self.me.c)
-        self.arrived(got, self.s2.at[p], self.r2.at[p])
-        self.cross(p, got, 2)
+        self.receive(p, 2)
+        self.cross(p, 2)
 
     def step5(self, p):
-        for which, stage in enumerate(("z", "in1", "in2")):
-            self.arrived(self.part(p, stage, 1 - self.me.c), self.ds.at[p, which], self.dr.at[p, which])
+        for stage in range(3):
+            self.arrived(self.crossing(p, stage, 1 - self.me.c)[1], self.dr.at[p, stage])
 
     def end(self):
-        for copy in self.waits:
-            copy.wait_send()
+        for ref, sem in self.waits:
+            remote(ref, ref, sem, sem, self.me.dev(c=1 - self.me.c)).wait_send()
 
 
 def norm_rows(z_ref, r_ref, n_rows, put):
@@ -245,9 +266,9 @@
     (lens, tokens, w_qkv, w_attn, w_inner, w_outer, w_proj, vectors) = refs[:8]
     outs = refs[8:27]
     scr = refs[27:]
-    (small_s, qk_s, va_s, inner_s, outer_s, small_g, qk, va, inner, outer) = scr[:10]
-    (xt, q, k, v, p, o, xh1, r1, g, gp, xh2, r2, out_own, proj, vec, x_all, h1b, vecp, bias_ff) = scr[10:29]
-    gsems, tsem, osem = scr[29:38], scr[38], scr[39]
+    (vec_s, proj_s, qk_s, va_s, inner_s, outer_s, vec_g, proj_g, qk, va, inner, outer) = scr[:12]
+    (xt, q, k, v, p, o, xh1, r1, g, gp, xh2, r2, out_own, proj, vec, x_all, h1b, vecp, bias_ff) = scr[12:31]
+    gsems, tsem, osem = scr[31:36], scr[36], scr[37]
     me = Place()
     mp = me.x
     n_all, width = x_all.shape
@@ -273,11 +294,12 @@
         cp.start()
         loads.append(cp)
 
+    greet_send(me.others())
     vecp[...] = jnp.zeros_like(vecp)
     nvec, nlane = vectors.shape
     vecp[0:nvec, 0:nlane] = vectors[...]
-    small_s[0:half_rows] = w_proj[pl.ds(pl.multiple_of(mp * half_rows, 8), half_rows), :]
-    small_s[half_rows : half_rows + nlane] = jnp.transpose(vecp[...])[0:nlane]
+    proj_s[...] = w_proj[pl.ds(pl.multiple_of(mp * half_rows, 8), half_rows), :]
+    vec_s[...] = jnp.transpose(vecp[...])[0:nlane]
     qk_s[...] = w_qkv[0:2].astype(BF)
     va_s[0] = w_qkv[2].astype(BF)
     va_s[1] = w_attn[...].astype(BF)
@@ -286,27 +308,29 @@
         inner_s[h] = w_inner[:, h * hf : (h + 1) * hf].astype(BF)
         outer_s[h] = w_outer[:, h * hf : (h + 1) * hf].astype(BF)
 
-    greet(me.others())
+    greet_wait(len(me.others()))
+    row_cut = 32
     pieces = [
-        (small_s, small_g),
+        (vec_s, vec_g),
         (qk_s.at[0], qk.at[0]),
         (qk_s.at[1], qk.at[1]),
-        (va_s.at[0], va.at[0]),
+        (va_s.at[0, pl.ds(0, row_cut)], va.at[0, :, :, :, pl.ds(0, row_cut)]),
+        (va_s.at[0, pl.ds(row_cut, rows - row_cut)], va.at[0, :, :, :, pl.ds(row_cut, rows - row_cut)]),
         (va_s.at[1], va.at[1]),
-        (inner_s.at[0], inner.at[0]),
-        (inner_s.at[1], inner.at[1]),
-        (outer_s.at[0], outer.at[0]),
-        (outer_s.at[1], outer.at[1]),
     ]
+    for shard, whole in ((inner_s, inner), (outer_s, outer)):
+        for h in range(2):
+            for j in range(2):
+                src = shard.at[h, :, pl.ds(j * (hf // 2), hf // 2)]
+                pieces.append((src, whole.at[h, :, :, :, :, pl.ds(j * hf, hf)]))
+    pieces.append((proj_s, proj_g))
     net = Gather(me, pieces, gsems)
-    groups = ((0, 1, 2), (3, 4), (5, 6), (7, 8))
-
-    def go(step, i):
-        for piece in groups[i]:
+
+    def go(step, *members):
+        for piece in members:
             (net.step1, net.step2, net.step3, net.step4, net.step5)[step - 1](piece)
 
-    go(1, 0)
-    go(1, 1)
+    go(1, 0, 1, 2, 12, 13)
     saves = []
 
     def save(i, ref):
@@ -323,28 +347,30 @@
     each(width // 256, x_turn)
     save(4, xt)
     go(2, 0)
-    go(1, 2)
-    go(3, 0)
-    go(2, 1)
-    go(1, 3)
+    go(1, 3, 4)
+    go(2, 1, 12, 13)
+    go(1, 5)
+    go(2, 2)
+    go(1, 6)
+    go(3, 0, 1)
+    go(2, 3)
+    go(3, 2)
+    go(1, 7)
+    go(2, 4)
     go(4, 0)
-    go(3, 1)
-    go(2, 2)
     go(5, 0)
     big = []
     for z in range(NZ):
         for y in range(NY):
             for c in range(NC):
                 for x in range(NX):
-                    blk = small_g[z, y, c, :, x * 128 : (x + 1) * 128]
-                    d = ((z * NY + y) * NC + c) * NX + x
-                    proj[d * half_rows : (d + 1) * half_rows] = blk[:half_rows]
-                    big.append(blk[half_rows : half_rows + nlane])
+                    big.append(vec_g[z, y, c, :, x * 128 : (x + 1) * 128])
     vec[...] = jnp.transpose(jnp.concatenate(big, axis=0))[0 : vec.shape[0]]
     for h in range(2):
         for x in range(NX):
-            bias_ff[h : h + 1, x * width : (x + 1) * width] = vec[5 + NX * x + h : 6 + NX * x + h, :]
-    save(16, proj)
+            for j in range(2):
+                row = vec[5 + NX * x + h : 6 + NX * x + h, j * (hf // 2) : (j + 1) * (hf // 2)]
+                bias_ff[h : h + 1, j * hf + x * (hf // 2) : j * hf + (x + 1) * (hf // 2)] = row
     save(17, vec)
 
     def project(w_ref, src_rows, dst, bias):
@@ -359,13 +385,26 @@
 
         each(width // n_tile, body)
 
+    go(3, 3)
+    go(4, 1)
+    go(3, 4)
+    go(2, 5)
+    go(1, 8)
+    go(4, 2)
+    go(5, 1)
     project(qk.at[0], n_own, q, 0)
+    go(5, 2)
+    go(2, 6)
+    go(1, 9)
     project(qk.at[1], n_all, k, None)
     save(0, qk)
-    go(4, 1)
-    go(2, 3)
-    go(5, 1)
+    go(4, 3, 4)
+    go(3, 5)
+    go(5, 3, 4)
     project(va.at[0], n_all, v, 1)
+    go(3, 6)
+    go(2, 7)
+    go(1, 10)
     save(5, q)
     save(6, k)
     save(7, v)
@@ -393,13 +432,20 @@
             o[at_q, l] = jnp.where(lane < HEAD_DIM, got[0], got[1]).astype(BF)
 
     slabs = p.shape[0]
+    jobs = [[(2, 8), (1, 11, 14), (3, 12)], [], [(2, 9)], [(4, 5, 6), (3, 13)], [(2, 10)], [(3, 7, 8), (5, 5, 6)]]
     for s in range(full):
         length = lens[mp * (full + 1) + s]
-        each(slabs, lambda i: attend(s * seq, seq, s * seq, i, length, pos))
-        go(3, 2 + s)
+        for i in range(slabs):
+            attend(s * seq, seq, s * seq, i, length, pos)
+            for job in jobs[3 * s + i]:
+                go(*job)
     length = lens[full]
     pos_c = jnp.where(pos < half_seq, pos + mp * half_seq, pos - half_seq + (1 - mp) * half_seq)
-    each(slabs, lambda i: attend(n_full, half_seq, n_full, i, length, pos_c))
+    for i in range(slabs):
+        attend(n_full, half_seq, n_full, i, length, pos_c)
+        if i == 0:
+            go(2, 11)
+    go(2, 14)
     save(8, p)
     save(9, o)
 
@@ -411,6 +457,7 @@
         xh1[rows_at(i, tile), :] = x_all[rows_at(i, tile), :].astype(F32) + a + vec[2:3, :]
 
     each(tiles, attn_out)
+    go(4, 7, 8)
     save(1, va)
 
     def put_h1(at, hat):
@@ -419,8 +466,8 @@
     norm_rows(xh1, r1, n_own, put_h1)
     save(10, xh1)
     save(11, r1)
-    go(4, 2)
-    go(5, 2)
+    go(5, 7)
+    go(3, 9, 10)
 
     def feed(h):
         n_tile = 256
@@ -439,9 +486,13 @@
         each(half_ff // n_tile, body)
 
     feed(0)
+    go(5, 8)
+    go(3, 11, 14)
+    go(4, 9)
+    go(5, 9)
     feed(1)
-    go(4, 3)
-    go(5, 3)
+    go(4, 10, 12, 11, 13)
+    go(5, 10, 12, 11, 13)
     save(2, inner)
     save(12, g)
     save(13, gp)
@@ -454,6 +505,12 @@
 
     each(tiles, ff_out)
     save(3, outer)
+    go(4, 14)
+    go(5, 14)
+    for d in range(NZ * NY * NC * NX):
+        block = proj_g[d // 8, d // 4 % 2, d // 2 % 2, :, d % 2 * 128 : (d % 2 + 1) * 128]
+        proj[d * half_rows : (d + 1) * half_rows] = block
+    save(16, proj)
 
     def put_y(at, hat):
         out_own[at, :] = (hat * vec[10:11, :] + vec[11:12, :]).astype(BF)
@@ -477,7 +534,7 @@
     rows, half_ff = w_qkv.shape[1], w_inner.shape[1]
     heads = width // HEAD_DIM
     zyc = (NZ, NY, NC)
-    small_rows = rows // 2 + vectors.shape[1]
+    hr, nlane = rows // 2, vectors.shape[1]
     weights = [
         ((2,) + zyc + (rows, width), BF),
         ((2,) + zyc + (rows, width), BF),
@@ -503,16 +560,18 @@
     ]
     order = kept[:12] + [kept[14], kept[12], kept[13]]
     scratch = [
-        ((small_rows, 128), F32),
+        ((nlane, 128), F32),
+        ((hr, 128), F32),
         ((2, rows, width // 2), BF),
         ((2, rows, width // 2), BF),
         ((2, rows, half_ff // 2), BF),
         ((2, rows, half_ff // 2), BF),
-        (zyc + (small_rows, 256), F32),
+        (zyc + (nlane, 256), F32),
+        (zyc + (hr, 256), F32),
     ]
     scratch += weights + order
     scratch += [((n_all, width), BF), ((n_own, width), BF), ((128, 128), F32), ((8, half_ff), F32)]
-    n = 9
+    n = 15
     vm = pl.BlockSpec(memory_space=pltpu.VMEM)
     hb = pl.BlockSpec(memory_space=ANY)
     sm = pl.BlockSpec(memory_space=pltpu.SMEM)
@@ -523,7 +582,7 @@
         out_specs=[hb] * 19,
         scratch_shapes=[pltpu.VMEM(s, d) for s, d in scratch]
         + [
-            dma(n), dma(n, NZ), dma(n, NZ), dma(n), dma(n), dma(n), dma(n), dma(n, 3), dma(n, 3),
+            dma(n), dma(n, 3), dma(n, 3), dma(n, 3), dma(n, 3),
             dma(3), dma(20),
         ],
         compiler_params=pltpu.CompilerParams(
@@ -536,7 +595,7 @@
 class Reduce:
     def __init__(self, me, pieces, sems):
         self.me, self.pieces = me, pieces
-        self.ds, self.dr, self.s1, self.r1, self.s2, self.r2, self.zs, self.zr = sems
+        self.ds, self.dr, self.ss, self.rs = sems
         self.waits = []
         self.squares = jnp.zeros((1, 1), F32)
 
@@ -547,84 +606,116 @@
     def arrived(self, ref, ssem, rsem):
         remote(ref, ref, ssem, rsem, self.me.dev(c=1 - self.me.c)).wait_recv()
 
+    def region(self, p, stage, **at):
+        order, src = self.pieces[p][0], self.pieces[p][2]
+        me, done = self.me, order[:stage]
+        half = src.shape[-1] // 2
+        z = at.get("z", me.z if "z" in done else None)
+        y = at.get("y", me.y if "y" in done else None)
+        x = at.get("x", me.x if "x" in done else None)
+        zs = slice(None) if z is None else pl.ds(0, NZ - 1) if z == "three" else pl.ds(z, 1)
+        ys = slice(None) if y is None else pl.ds(y, 1)
+        xs = slice(None) if x is None else cols(x, half)
+        return src.at[zs, ys, me.c, :, xs]
+
+    def send(self, p, stage):
+        order, got, me = self.pieces[p][0], self.pieces[p][4 + stage], self.me
+        ss, rs = self.ss, self.rs
+        if order[stage] == "z":
+            for k in range(1, NZ):
+                tz = lax.rem(me.z + k, NZ)
+                part = self.region(p, stage, z=tz)
+                remote(part, got.at[pl.ds(k, 1)], ss.at[p, stage], rs.at[p, stage], me.dev(z=tz)).start()
+            part = self.region(p, stage, z="three")
+            self.waits.append(remote(part, part, ss.at[p, stage], rs.at[p, stage], me.dev(c=1 - me.c)))
+        else:
+            far = 1 - (me.y if order[stage] == "y" else me.x)
+            part = self.region(p, stage, **{order[stage]: far})
+            dev = me.dev(**{order[stage]: far})
+            self.go(remote(part, got, ss.at[p, stage], rs.at[p, stage], dev))
+
+    def receive(self, p, stage):
+        order, got = self.pieces[p][0], self.pieces[p][4 + stage]
+        if order[stage] == "z":
+            got = got.at[pl.ds(1, NZ - 1)]
+        self.arrived(got, self.ss.at[p, stage], self.rs.at[p, stage])
+
+    def add(self, p, stage):
+        order, _, src, _, *gots = self.pieces[p]
+        got, me = gots[stage], self.me
+        done = order[: stage + 1]
+        half = src.shape[-1] // 2
+        xs = cols(me.x, half) if "x" in done else slice(None)
+        ys = [(me.y, 0)] if "y" in done else [(y, y) for y in range(NY)]
+        if order[stage] == "z":
+            for y, i in ys:
+                total = src[me.z, y, me.c, :, xs].astype(F32)
+                for k in range(1, NZ):
+                    total = total + got[k, i].astype(F32)
+                src[me.z, y, me.c, :, xs] = total.astype(src.dtype)
+            return
+
+        def one(z):
+            for y, i in ys:
+                src[z, y, me.c, :, xs] = src[z, y, me.c, :, xs] + got[0 if "z" in done else z, i]
+
+        if "z" in done:
+            one(me.z)
+        else:
+            each(NZ, one)
+
     def step1(self, p):
-        src, got1 = self.pieces[p][2], self.pieces[p][3]
+        src, got = self.pieces[p][2], self.pieces[p][3]
         oc = 1 - self.me.c
-        self.go(remote(src.at[:, :, oc], got1, self.ds.at[p], self.dr.at[p], self.me.dev(c=oc)))
+        self.go(remote(src.at[:, :, oc], got, self.ds.at[p], self.dr.at[p], self.me.dev(c=oc)))
 
     def step2(self, p):
-        route, _, src, got1, got2, _, _ = self.pieces[p]
+        src, got, c = self.pieces[p][2], self.pieces[p][3], self.me.c
+        self.arrived(got, self.ds.at[p], self.dr.at[p])
+
+        def one(z):
+            for y in range(NY):
+                src[z, y, c] = src[z, y, c] + got[z, y]
+
+        each(NZ, one)
+        self.send(p, 0)
+
+    def step3(self, p):
+        self.receive(p, 0)
+        self.add(p, 0)
+        self.send(p, 1)
+
+    def step4(self, p):
+        self.receive(p, 1)
+        self.add(p, 1)
+        self.send(p, 2)
+
+    def step5(self, p, counted=None):
+        order, dst, src, _, *gots = self.pieces[p]
         me = self.me
-        c, half = me.c, src.shape[-1] // 2
-        self.arrived(got1, self.ds.at[p], self.dr.at[p])
-
-        def add(z):
-            for y in range(NY):
-                src[z, y, c] = src[z, y, c] + got1[z, y]
-
-        each(NZ, add)
-        if route == "y":
-            part, dev = src.at[:, 1 - me.y, c], me.dev(y=1 - me.y)
-        else:
-            part, dev = src.at[:, :, c, :, cols(1 - me.x, half)], me.dev(x=1 - me.x)
-        self.go(remote(part, got2, self.s1.at[p], self.r1.at[p], dev))
-
-    def step3(self, p):
-        route, _, src, _, got2, got3, _ = self.pieces[p]
-        me = self.me
-        c, half = me.c, src.shape[-1] // 2
-        mine = cols(me.x, half)
-        self.arrived(got2, self.s1.at[p], self.r1.at[p])
-        if route == "y":
-
-            def add(z):
-                src[z, me.y, c] = src[z, me.y, c] + got2[z]
-
-            each(NZ, add)
-            part, dev = src.at[:, me.y, c, :, cols(1 - me.x, half)], me.dev(x=1 - me.x)
-        else:
-
-            def add(z):
-                for y in range(NY):
-                    src[z, y, c, :, mine] = src[z, y, c, :, mine] + got2[z, y]
-
-            each(NZ, add)
-            part, dev = src.at[:, 1 - me.y, c, :, mine], me.dev(y=1 - me.y)
-        self.go(remote(part, got3, self.s2.at[p], self.r2.at[p], dev))
-
-    def step4(self, p):
-        _, _, src, _, _, got3, got4 = self.pieces[p]
-        me = self.me
-        c, mine = me.c, cols(me.x, src.shape[-1] // 2)
-        self.arrived(got3, self.s2.at[p], self.r2.at[p])
-
-        def add(z):
-            src[z, me.y, c, :, mine] = src[z, me.y, c, :, mine] + got3[z]
-
-        each(NZ, add)
-        for k in range(1, NZ):
-            tz = lax.rem(me.z + k, NZ)
-            part = src.at[tz, me.y, c, :, mine]
-            self.go(remote(part, got4.at[k], self.zs.at[p, k], self.zr.at[p, k], me.dev(z=tz)))
-
-    def step5(self, p, counted=True):
-        _, dst, src, _, _, _, got4 = self.pieces[p]
-        me = self.me
-        for k in range(1, NZ):
-            self.arrived(got4.at[k], self.zs.at[p, k], self.zr.at[p, k])
+        self.receive(p, 2)
         total = src[me.z, me.y, me.c, :, cols(me.x, src.shape[-1] // 2)].astype(F32)
-        for k in range(1, NZ):
-            total = total + got4[k].astype(F32)
+        for k in range(1, NZ) if order[2] == "z" else (0,):
+            total = total + gots[2][k, 0].astype(F32)
         dst[...] = total
-        if counted:
-            self.squares = self.squares + jnp.sum(total * total, keepdims=True)
+        total = total[:counted]
+        self.squares = self.squares + jnp.sum(total * total, keepdims=True)
 
     def end(self):
         for copy in self.waits:
             copy.wait_send()
 
 
-routes = "yyyyyyyyy"
+def got_shapes(order, r, w):
+    out, done = [], ""
+    for axis in order:
+        done += axis
+        nz = NZ if axis == "z" or "z" not in done else 1
+        out.append((nz, 1 if "y" in done else NY, r, w // 2 if "x" in done else w))
+    return out
+
+
+orders = ("zyx", "zyx", "yxz", "yxz", "yxz", "yxz", "yzx", "yzx", "yzx", "yzx", "yxz", "yxz", "yxz", "yxz")
 
 
 def all_squares(me, net, total, sq4, sq8, sems):
@@ -708,11 +799,11 @@
         return got
 
     (inner, outer, attn, xt, q, k, v, o, xh1, gg, xh2, r2, proj, vec, cls_in, cot, df, dft) = take(18)
-    (cls_grad, acc1, acc2, ffacc, vg, small) = take(6)
+    (cls_grad, acc1, acc2, ffacc, vg, early, late) = take(7)
     grads = take(4)
-    bufs = take(9 * 4)
+    bufs = take(14 * 4)
     sq4, sq8 = take(2)
-    lsem, rsems, xs, xr, qsems = take(1)[0], take(8), *take(2), take(4)
+    lsem, rsems, xs, xr, qsems = take(1)[0], take(4), *take(2), take(4)
     do, da, dat, h1t, r1 = cot, df, dft, dft, r2
     me = Place()
     mp = me.x
@@ -760,16 +851,34 @@
 
     greet(me.others() + me.eights())
     pieces = []
-    dsts = [outer_r.at[0], outer_r.at[1], inner_r.at[0], inner_r.at[1], va_r.at[1], va_r.at[0], qk_r.at[0], qk_r.at[1], small_r]
-    for p in range(9):
-        src = grads[p] if p < 8 else small
-        pieces.append((routes[p], dsts[p], src) + tuple(bufs[4 * p : 4 * p + 4]))
+    hr = width // (NZ * NY * NC * NX)
+    n_early = early.shape[3]
+    hf = half_ff // 2
+    dsts, srcs = [], []
+    for i, ref in enumerate((outer_r, inner_r)):
+        for h in range(2):
+            for j in range(2):
+                dsts.append(ref.at[h, :, pl.ds(j * (hf // 2), hf // 2)])
+                srcs.append(grads[2 * i + h].at[:, :, :, :, pl.ds(j * hf, hf)])
+    dsts += [va_r.at[1], va_r.at[0], qk_r.at[0], qk_r.at[1]]
+    dsts += [small_r.at[pl.ds(0, n_early)], small_r.at[pl.ds(n_early, hr)]]
+    srcs += grads[4:] + [early, late]
+    for i in range(14):
+        pieces.append((orders[i], dsts[i], srcs[i]) + tuple(bufs[4 * i : 4 * i + 4]))
     net = Reduce(me, pieces, rsems)
+
+    def go(step, *members):
+        for piece in members:
+            if step == 5 and piece == 12:
+                net.step5(piece, hr)
+            else:
+                (net.step1, net.step2, net.step3, net.step4, net.step5)[step - 1](piece)
+
     send_out = remote(out_h, peer_out, xs.at[0], xr.at[0], other)
     net.go(send_out)
 
     vg[...] = jnp.zeros_like(vg)
-    small[...] = jnp.zeros_like(small)
+    early[...] = jnp.zeros_like(early)
     acc1[...] = jnp.zeros_like(acc1)
     acc2[...] = jnp.zeros_like(acc2)
     ffacc[...] = jnp.zeros_like(ffacc)
@@ -798,7 +907,21 @@
         row_grads.append(sg * query_s)
     dcq = dcq.astype(BF)
     cls_grad[...] = mm_nt(dcq, proj_low)
-    proj[...] = mm_tn(cls, dcq)
+    proj_grad = mm_tn(cls, dcq)
+    n_dev = NZ * NY * NC * NX
+    table_row = lax.broadcasted_iota(jnp.int32, (TAB_DEV * n_dev // NX, 1), 0)
+    table = jnp.zeros((TAB_DEV * n_dev // NX, 128), F32)
+    for s in range(full + 1):
+        for i in range(cands):
+            table = table + jnp.where(table_row == doc_ids[seq_ids[s], i], row_grads[s][i : i + 1], 0.0)
+    tr = TAB_DEV // NX
+    for d in range(n_dev):
+        z, y, c, x = d // 8, d // 4 % 2, d // 2 % 2, d % 2
+        l = slice(x * 128, (x + 1) * 128)
+        t0 = (d // 2) * TAB_DEV + x * tr
+        early[z, y, c, 0:hr, l] = proj_grad[d * hr : (d + 1) * hr]
+        early[z, y, c, hr : hr + tr, l] = table[t0 : t0 + tr]
+    go(1, 12)
 
     per = seq // 48
     row48 = lax.broadcasted_iota(jnp.int32, (48, 1), 0)
@@ -821,6 +944,7 @@
 
     load("r1", 13, r1_h, r1)
     turn(df, dft, n_own)
+    go(2, 12)
     n_tile = 256
     shape5 = (NZ, NY, NC, width // (NZ * NY * NC))
 
@@ -834,7 +958,8 @@
     need("g")
     for h in range(2):
         weight_grad(lambda: dft[:, 0:n_own], lambda l: gg[h, :, l], grads[h], half_ff)
-        net.step1(h)
+        go(1, 2 * h, 2 * h + 1)
+    go(2, 0, 1)
 
     need("outer", "gp")
     tile = 240
@@ -852,10 +977,9 @@
         each(half_ff // n_tile, body)
 
     hidden(0)
-    net.step2(0)
+    go(2, 2, 3)
+    go(3, 12)
     hidden(1)
-    net.step2(1)
-    net.step3(0)
     load("p0", 21, p_h.at[0], gg.at[0])
     load("p1", 22, p_h.at[1], gg.at[1])
     load("wq", 23, qk_h.at[0], outer.at[0, :, :, :, :, pl.ds(0, width)])
@@ -871,10 +995,8 @@
     each(width // 256, h1_turn)
     for h in range(2):
         weight_grad(lambda: h1t[:, 0:n_own], lambda l: gg[2 + h, :, l], grads[2 + h], half_ff)
-        net.step1(2 + h)
-    net.step2(2)
-    net.step3(1)
-    net.step4(0)
+        go(1, 4 + 2 * h, 5 + 2 * h)
+    go(2, 4, 5)
     need("inner")
 
     def hidden_back(i):
@@ -884,12 +1006,11 @@
 
     each(tiles, hidden_back)
     load("p2", 26, p_h.at[2], gg.at[2])
-    net.step2(3)
-    net.step3(2)
-    net.step4(1)
-    net.step5(0)
+    go(2, 6, 7)
+    go(3, 2)
 
     norm_back_rows(n_own, lambda i, at: xh2[at, :], xh1, r1, vec[3:4, :], put_df, acc1)
+    go(3, 3)
     need("attn", "o")
 
     def mixed_back(i):
@@ -898,7 +1019,7 @@
     each(width // n_tile, mixed_back)
     turn(da, dat, n_own)
     weight_grad(lambda: dat[:, 0:n_own], lambda l: o[:, l], grads[4], width)
-    net.step1(4)
+    go(1, 8)
 
     need("q", "k", "v", "p0", "p1", "p2")
     lane = lax.broadcasted_iota(jnp.int32, (1, 128), 1)
@@ -946,32 +1067,28 @@
 
     need("wq", "wk", "wv")
     for s in range(full):
-        each(slabs, lambda i: attend(s * seq, seq, s * seq, i))
+        for i in range(slabs):
+            attend(s * seq, seq, s * seq, i)
+            if s == 0:
+                (lambda: (go(2, 8), go(4, 12)), lambda: (go(3, 4), go(4, 2)), lambda: (go(3, 0, 1), go(4, 3)))[i]()
+            else:
+                (lambda: (go(3, 5), go(4, 4)), lambda: None, lambda: go(5, 2, 3))[i]()
         tokens_back(pl.ds(s * seq, seq), True)
         send_dx(s, o.at[pl.ds(s * seq, seq)], pl.ds(s * seq, seq))
-        if s == 0:
-            net.step2(4)
-            net.step3(3)
-            net.step4(2)
-            net.step5(1)
-        else:
-            net.step3(4)
-            net.step4(3)
-            net.step5(2)
-    each(slabs, lambda i: attend(n_full, half_seq, n_full, i))
+    for i in range(slabs):
+        attend(n_full, half_seq, n_full, i)
+        (lambda: go(3, 6), lambda: None, lambda: (go(3, 7), go(4, 5)))[i]()
     need("xt")
     weight_grad(lambda: xt[...], lambda l: v[:, l], grads[5], width)
-    net.step1(5)
+    go(1, 9)
+    go(5, 4)
     weight_grad(lambda: xt[:, 0:n_own], lambda l: q[:, l], grads[6], width)
-    net.step1(6)
-    net.step2(5)
-    net.step4(4)
-    net.step5(3)
+    go(1, 10)
+    go(2, 9)
+    go(4, 0, 1)
     weight_grad(lambda: xt[...], lambda l: k[:, l], grads[7], width)
-    net.step1(7)
-    net.step2(6)
-    net.step3(5)
-    net.step5(4)
+    go(1, 11)
+    go(2, 10)
     tokens_back(pl.ds(n_full, half_seq), True)
     tokens_back(pl.ds(n_own, half_seq), False)
     send_dx(full, o.at[pl.ds(n_full, half_seq)], pl.ds(n_full, half_seq))
@@ -985,47 +1102,39 @@
     for h in range(2):
         both = jnp.sum(ffacc[h], axis=0, keepdims=True)
         for x in range(NX):
-            vg[5 + NX * x + h : 6 + NX * x + h, :] = both[:, x * width : (x + 1) * width]
+            for j in range(2):
+                at = j * hf + x * (hf // 2)
+                vg[5 + NX * x + h : 6 + NX * x + h, j * (hf // 2) : (j + 1) * (hf // 2)] = both[:, at : at + hf // 2]
     vg[9:10, :] = jnp.sum(acc2[2], axis=0, keepdims=True)
     vg[10:11, :] = jnp.sum(acc2[0], axis=0, keepdims=True)
     vg[11:12, :] = jnp.sum(acc2[1], axis=0, keepdims=True)
     turned = jnp.transpose(vg[...])
-    n_dev = NZ * NY * NC * NX
-    table_row = lax.broadcasted_iota(jnp.int32, (TAB_DEV * n_dev // NX, 1), 0)
-    table = jnp.zeros((TAB_DEV * n_dev // NX, 128), F32)
-    for s in range(full + 1):
-        for i in range(cands):
-            table = table + jnp.where(table_row == doc_ids[seq_ids[s], i], row_grads[s][i : i + 1], 0.0)
-    hr = width // n_dev
-    for z in range(NZ):
-        for y in range(NY):
-            for c in range(NC):
-                dp = (z * NY + y) * NC + c
-                for x in range(NX):
-                    d = dp * NX + x
-                    l = slice(x * 128, (x + 1) * 128)
-                    small[z, y, c, 0:hr, l] = proj[d * hr : (d + 1) * hr]
-                    small[z, y, c, hr : 2 * hr, l] = turned[d * hr : (d + 1) * hr]
-                    t0 = dp * TAB_DEV + x * (TAB_DEV // NX)
-                    small[z, y, c, 2 * hr : 2 * hr + TAB_DEV // NX, l] = table[t0 : t0 + TAB_DEV // NX]
-    net.step1(8)
-    net.step2(7)
-    net.step3(6)
-    net.step4(5)
-    net.step2(8)
-    net.step3(7)
-    net.step4(6)
-    net.step3(8)
-    net.step4(7)
-    net.step5(5)
-    net.step4(8)
-    net.step5(6)
-    net.step5(7)
-    net.step5(8, False)
+    for d in range(n_dev):
+        z, y, c, x = d // 8, d // 4 % 2, d // 2 % 2, d % 2
+        late[z, y, c, :, x * 128 : (x + 1) * 128] = turned[d * hr : (d + 1) * hr]
+    go(1, 13)
+    go(2, 11)
+    go(3, 8)
+    go(2, 13)
+    go(5, 5)
+    go(4, 6, 7)
+    go(5, 12, 0, 1)
+    go(4, 8)
+    go(3, 9)
+    go(5, 6, 7)
+    go(3, 10)
+    go(4, 9)
+    go(5, 8)
+    go(4, 10)
+    go(3, 11)
+    go(5, 9)
+    go(3, 13)
+    go(4, 11)
+    go(5, 10)
+    go(4, 13)
+    go(5, 11, 13)
     net.go(remote(small_r, peer_small, xs.at[5], xr.at[5], other))
-    count = small_r[0 : 2 * hr, :]
-    total = net.squares + jnp.sum(count * count, keepdims=True)
-    norm_ref[...] = all_squares(me, net, total, sq4, sq8, qsems)
+    norm_ref[...] = all_squares(me, net, net.squares, sq4, sq8, qsems)
     parts = [pl.ds(0, seq), pl.ds(seq, seq), pl.ds(n_full, half_seq), pl.ds(n_own, half_seq)]
     for i, ref in enumerate([peer_out] + [peer_dx.at[at] for at in parts] + [peer_small]):
         net.arrived(ref, xs.at[i], xr.at[i])
@@ -1041,7 +1150,8 @@
     half_ff = inner.shape[-1]
     zyc = (NZ, NY, NC)
     hr = rows // NX
-    small_rows = 2 * hr + 8
+    n_early = hr + 8
+    small_rows = n_early + hr
     ins = [doc_ids, cotangent, doc_rows] + list(saved)
     out_shape = [
         ((small_rows, 128), F32),
@@ -1063,20 +1173,18 @@
         ((3, 16, width), BF), ((n_own, width), BF), ((n_own, width), BF),
         ((width, wide), BF),
         ((16, width), F32), ((3, 8, width), F32), ((3, 8, width), F32), ((2, 8, half_ff), F32),
-        ((128, width), F32), (zyc + (small_rows, 256), F32),
+        ((128, width), F32), (zyc + (n_early, 256), F32), (zyc + (hr, 256), F32),
     ]
     sizes = [half_ff] * 4 + [width] * 4
     scratch += [(zyc + (rows, w), BF) for w in sizes[:4]]
-    for i, (r, w, dt) in enumerate([(rows, w, BF) for w in sizes] + [(small_rows, 256, F32)]):
-        scratch.append(((NZ, NY, r, w), dt))
-        scratch.append((((NZ, r, w) if routes[i] == "y" else (NZ, NY, r, w // 2)), dt))
-        scratch.append(((NZ, r, w // 2), dt))
-        scratch.append(((NZ, r, w // 2), dt))
+    smalls = [(n_early, 256, F32), (hr, 256, F32)]
+    for i, (r, w, dt) in enumerate([(rows, width, BF)] * 12 + smalls):
+        scratch += [((NZ, NY, r, w), dt)] + [(shape, dt) for shape in got_shapes(orders[i], r, w)]
     scratch += [((NZ, 8, 128), F32), ((8, 8, 128), F32)]
     vm = pl.BlockSpec(memory_space=pltpu.VMEM)
     hb = pl.BlockSpec(memory_space=ANY)
     sm = pl.BlockSpec(memory_space=pltpu.SMEM)
-    n = 9
+    n = 14
     return pl.pallas_call(
         backward_kernel,
         out_shape=[jax.ShapeDtypeStruct(s, d) for s, d in out_shape],
@@ -1084,7 +1192,7 @@
         out_specs=[vm] * 5 + [hb, hb, hb, vm, vm],
         scratch_shapes=[pltpu.VMEM(s, d) for s, d in scratch]
         + [
-            dma(31), dma(n), dma(n), dma(n), dma(n), dma(n), dma(n), dma(n, NZ), dma(n, NZ),
+            dma(31), dma(n), dma(n), dma(n, 3), dma(n, 3),
             dma(6), dma(6), dma(NZ), dma(NZ), dma(8), dma(8),
         ],
         compiler_params=pltpu.CompilerParams(
@@ -1155,12 +1263,12 @@
         for h in range(2):
             adam(which, (slice(None), slice(h * hf, (h + 1) * hf)), ref[h], decay_rate, learn_rate)
     turn[...] = jnp.zeros_like(turn)
-    turn[0:nlane] = small_r[hr : hr + nlane]
+    turn[0:nlane] = small_r[hr + 8 : hr + 8 + nlane]
     adam(5, (slice(None), slice(None)), jnp.transpose(turn[...])[0:nvec, 0:nlane], 0.0, vector_rate)
     for block, first in ((small_r, mp), (peer_small, 1 - mp)):
         at = pl.ds(pl.multiple_of(first * hr, 8), hr)
         adam(4, (at, slice(None)), block[0:hr], decay_rate, learn_rate)
-    own_t, peer_t = small_r[hr + nlane : hr + nlane + tr], peer_small[hr + nlane : hr + nlane + tr]
+    own_t, peer_t = small_r[hr : hr + tr], peer_small[hr : hr + tr]
     table_grad[0:tr] = jnp.where(mp == 0, own_t, peer_t)
     table_grad[tr : 2 * tr] = jnp.where(mp == 0, peer_t, own_t)
     for cp in copies:

time: 248 us -> 213 us (0.86); the launches traced: 248 us -> 209 us
  Pallas kernels: 247 us -> 208 us
    pallas_call x1, Pallas kernels: 146 us -> 109 us  [backward_fast(): pl.pallas_call(backward_kernel, out_shape=[jax.ShapeDtypeStruct(s, d) for...]
where the time goes in v5:
time: 213 us; the launch traced here: 209 us
  Pallas kernels  208 us (98%)
    pallas_call x1, Pallas kernels, backward_fast(): pl.pallas_call(backward_kernel, out_shape=[jax.ShapeDtypeStruct(s, d) for...  109 us
    pallas_call x1, Pallas kernels, forward_fast(): pl.pallas_call(forward_kernel, out_shape=[jax.ShapeDtypeStruct(s, d) for...  91.6 us
    pallas_call x1, Pallas kernels, finish_fast(): pl.pallas_call(finish_kernel, out_shape=out_shape, in_specs=[vm] * 29, ou...  7.99 us

profile of v5, /device:TPU:0, one launch (start us, length us, event | category | flops | bytes accessed | tf_op | source)
XLA Modules:
  0.0 209.3 jit_solution(14225322584462655084)
XLA Ops:
  0.7 91.6 %forward.1 = (bf16[2,4,2,2,48,768]{5,4,3,2,1,0:T(8,128)(2,1)}, bf16[2,4,2,2,48,768]{5,4,3,2,1,0:T(8,128)(2,1)}, bf16[2,4,2,2,48,1536]{5,4,3,2,1,0:T(8,128)(2,1)}...) custom-call(s32[5]{0:T(128)} %refs_0_.2, ...), custom_call_target="tpu_custom_call" | custom-call | tf_op jit(solution)/shard_map/forward/pallas_call | solution.py:578
  92.3 108.8 %backward.1 = (f32[56,128]{1,0:T(8,128)}, f32[2,48,384]{2,1,0:T(8,128)}, f32[2,48,384]{2,1,0:T(8,128)}, f32[2,48,768]{2,1,0:T(8,128)}, f32[2,48,768]{2,1,0:T(8,1...) custom-call(s32[5,8]{1,0:T(8,128)} %refs_0_.3, ...), custom_call_target="tpu_custom_call" | custom-call | tf_op jit(solution)/shard_map/backward/pallas_call | solution.py:1188
  201.1 8.0 %finish.1 = (bf16[1440,768]{1,0:T(8,128)(2,1)}, f32[1440,768]{1,0:T(8,128)}, f32[1,1]{1,0:T(1,128)}, f32[3,48,384]{2,1,0:T(8,128)}, f32[3,48,384]{2,1,0:T(8,128)...) custom-call(f32[56,128]{1,0:T(8,128)} %get-tuple-element.92.refs_0_,, ...), custom_call_target="tpu_custom_call" | custom-call | tf_op jit(solution)/shard_map/finish/pallas_call | solution.py:1294
